TPU v7x, 256 devices: a whole 4x4x8 slice. The times are simulated.
256 devices in a mesh: ctx: 32 (over y, x, core), head: 8 (over z).
Axes of the slice: x: 4, y: 4, z: 8, core: 2. Of those that a mesh axis runs over, the one named last changes fastest.
Arguments:
- queries: bfloat16 [16384, 64, 128], P('ctx', 'head'), may hold values from -6 to 6
- key_rows: bfloat16 [16384, 64, 128], P('ctx', 'head'), may hold values from -2 to 2
- value_rows: bfloat16 [16384, 64, 128], P('ctx', 'head'), may hold values from -21 to 21
- upstream: bfloat16 [16384, 64, 128], P('ctx', 'head'), may hold values from -6 to 6
- norm_gain: float32 [64, 128], P('head'), may hold values from 0.1 to 1.9
- slope_index: int32 [64], P('head'), may hold values from 0 to 63
Outputs:
- grad_query: bfloat16 [16384, 64, 128], P('ctx', 'head')
- grad_key: bfloat16 [16384, 64, 128], P('ctx', 'head')
- grad_value: bfloat16 [16384, 64, 128], P('ctx', 'head')
All inputs are finite; a program needn't handle non-finite values.
Results may differ from a plain program's by a relative error of at most 0.0064.
Values sent between devices are 32-bit elements; how exact they have to be, the bound alone decides.
No kernel may reach another device: no remote copies, remote signals or barrier semaphores. Data moves between devices by JAX's collectives and lax.ppermute only.
A program may use at most 128 MiB of HBM per device.

v0:
```python
import jax
import jax.numpy as jnp
from jax import lax
from jax.sharding import PartitionSpec as P


def prefix(part, axis, combine, identity, reverse):
    count = lax.axis_size(axis)
    place = lax.axis_index(axis)
    ahead = count - 1 - place if reverse else place
    gathered = jax.tree.map(lambda a: lax.all_gather(a, axis), part)
    state = jax.tree.map(lambda a, e: jnp.zeros_like(a) + jnp.asarray(e, a.dtype), part, identity)

    def one(lap, state):
        source = count - 1 - lap if reverse else lap
        return combine(
            state, jax.tree.map(lambda a: lax.dynamic_index_in_dim(a, source, 0, False), gathered)
        )

    return lax.fori_loop(0, ahead, one, state)


def combine_states(before_part, after_part):
    decay_a, state_a = before_part
    decay_b, state_b = after_part
    return (decay_a * decay_b, decay_b[:, None, None] * state_a + state_b)


def on_device(queries, key_rows, value_rows, upstream, norm_gain, slope_index):
    length, head_count, head_size = queries.shape
    layer_factor = 1.0 - 78.0 / 79.0 + 1e-05
    decay_rate = 2.0 ** (-8.0 * (slope_index.astype(jnp.float32) + 1.0) / 64.0) * layer_factor
    position = jnp.arange(length).astype(jnp.float32)
    row_pos = position[:, None]
    col_pos = position[None, :]
    distance = jnp.maximum(row_pos - col_pos, 0.0)
    decay_mask = jnp.where(row_pos >= col_pos, jnp.exp(-decay_rate[:, None, None] * distance), 0.0)
    decay_in = jnp.exp(-decay_rate[:, None] * (position[None, :] + 1.0))[:, :, None]
    decay_first = jnp.exp(-decay_rate[:, None] * position[None, :])[:, :, None]
    decay_last = jnp.exp(-decay_rate[:, None] * (length - 1.0 - position[None, :]))[:, :, None]
    decay_back = jnp.exp(-decay_rate[:, None] * (length - position[None, :]))[:, :, None]
    block_decay = jnp.exp(-decay_rate * length)
    identity = (
        jnp.ones((head_count,), jnp.float32),
        jnp.zeros((head_count, head_size, head_size), jnp.float32),
    )
    q_heads = jnp.transpose(queries, (1, 0, 2))
    k_heads = jnp.transpose(key_rows, (1, 0, 2))
    v_heads = jnp.transpose(value_rows, (1, 0, 2))
    u_heads = jnp.transpose(upstream, (1, 0, 2))
    weighted_keys = (k_heads.astype(jnp.float32) * decay_last).astype(jnp.bfloat16)
    key_state = jnp.einsum(
        "hjd,hje->hde", weighted_keys, v_heads, preferred_element_type=jnp.float32
    )
    entering = prefix((block_decay, key_state), "ctx", combine_states, identity, False)[1]
    entering_b = entering.astype(jnp.bfloat16)
    scores = jnp.einsum("hid,hjd->hij", q_heads, k_heads, preferred_element_type=jnp.float32)
    attn_b = (scores * decay_mask).astype(jnp.bfloat16)
    local_part = jnp.einsum("hij,hjd->hid", attn_b, v_heads, preferred_element_type=jnp.float32)
    carried = jnp.einsum("hid,hde->hie", q_heads, entering_b, preferred_element_type=jnp.float32)
    output = local_part + decay_in * carried
    scaled_up = norm_gain[:, None, :] * u_heads.astype(jnp.float32)
    partial_sq = jnp.sum(output * output, axis=(0, 2))
    partial_dot = jnp.sum(output * scaled_up, axis=(0, 2))
    total_sq, total_dot = lax.psum((partial_sq, partial_dot), "head")
    features = lax.axis_size("head") * head_count * head_size
    inv_rms = lax.rsqrt(total_sq / features + 1e-06)
    grad_out = (
        inv_rms[None, :, None] * scaled_up
        - output * (inv_rms**3 * total_dot / features)[None, :, None]
    )
    grad_out = grad_out.astype(jnp.bfloat16)
    weighted_q = (q_heads.astype(jnp.float32) * decay_first).astype(jnp.bfloat16)
    query_state = jnp.einsum(
        "hid,hie->hde", weighted_q, grad_out, preferred_element_type=jnp.float32
    )
    leaving = prefix((block_decay, query_state), "ctx", combine_states, identity, True)[1]
    leaving_b = leaving.astype(jnp.bfloat16)
    back_scores = jnp.einsum("hie,hje->hij", grad_out, v_heads, preferred_element_type=jnp.float32)
    back_b = (back_scores * decay_mask).astype(jnp.bfloat16)
    grad_query = jnp.einsum("hij,hjd->hid", back_b, k_heads, preferred_element_type=jnp.float32)
    grad_query = grad_query + decay_in * jnp.einsum(
        "hie,hde->hid", grad_out, entering_b, preferred_element_type=jnp.float32
    )
    grad_key = jnp.einsum("hij,hid->hjd", back_b, q_heads, preferred_element_type=jnp.float32)
    grad_key = grad_key + decay_back * jnp.einsum(
        "hje,hde->hjd", v_heads, leaving_b, preferred_element_type=jnp.float32
    )
    grad_value = jnp.einsum("hij,hie->hje", attn_b, grad_out, preferred_element_type=jnp.float32)
    grad_value = grad_value + decay_back * jnp.einsum(
        "hjd,hde->hje", k_heads, leaving_b, preferred_element_type=jnp.float32
    )
    grad_query = jnp.transpose(grad_query.astype(jnp.bfloat16), (1, 0, 2))
    grad_key = jnp.transpose(grad_key.astype(jnp.bfloat16), (1, 0, 2))
    grad_value = jnp.transpose(grad_value.astype(jnp.bfloat16), (1, 0, 2))
    return (grad_query, grad_key, grad_value)


def solution(mesh):
    in_specs = (
        P("ctx", "head", None),
        P("ctx", "head", None),
        P("ctx", "head", None),
        P("ctx", "head", None),
        P("head", None),
        P("head"),
    )
    out_specs = (P("ctx", "head", None), P("ctx", "head", None), P("ctx", "head", None))
    return jax.shard_map(
        on_device, mesh=mesh, in_specs=in_specs, out_specs=out_specs, check_vma=False
    )
```

profile of v0, /device:TPU:1, one launch (start us, length us, event | category | flops | bytes accessed | tf_op | source)
XLA Modules:
  0.0 282.0 jit_solution(5214048449630994198)
XLA Ops:
  7.3 1.3 dynamic-slice
  10.2 1.7 multiply_convert_fusion.3
  12.0 1.4 fusion.11
  13.5 66.2 %all-reduce = f32[256]{0:T(256)S(1)} all-reduce(f32[256]{0:T(256)S(1)} %get-tuple-element.173), channel_id=2, replica_groups=mesh['ctx'=32,'head'=8] {'ctx'}, use_global_device_ids=true, to_apply=%add | all-reduce | flops 256 | bytes 2048
  79.8 2.4 copy.73
  82.8 1.5 multiply_convert_fusion.2
  84.3 3.9 %multiply_convert_fusion.1 = bf16[8,512,512]{2,1,0:T(8,128)(2,1)S(1)} fusion(f32[512,512]{1,0:T(8,128)S(1)} %subtract_maximum_fusion, f32[8]{0:T(128)S(1)} %get-tuple-element.174, pred[512,512]{1,0:T(8,128)(4,1)S(1)} %broadcast_compare_fusion, bf16[8,512,128]{2,0,1:T(8,128)(2,1)} %bitcast.74, bf16[8,512,128]{2,0,1:T(8,128)(2,1)S(1)} %bitcast.71), kind=kOutput, calls=%fused_computation.5 | convolution fusion | flops 545259520 | bytes 7602208 | tf_op jit(solution)/shard_map/hid,hjd->hij/dot_general | solution.py:57
  88.2 1.9 copy-done.1
  90.1 2.8 %fusion.21 = f32[8,512,128]{1,2,0:T(8,128)} fusion(bf16[8,512,512]{2,1,0:T(8,128)(2,1)S(1)} %multiply_convert_fusion.1, bf16[8,512,128]{2,0,1:T(8,128)(2,1)S(1)} %bitcast.68), kind=kOutput, calls=%fused_computation.39 | convolution fusion | flops 536870912 | bytes 7340032 | tf_op jit(solution)/shard_map/hij,hjd->hid/dot_general | solution.py:59
  92.9 2.7 all-gather.6.cloned.1.call-done
  95.7 1.2 while.26
  95.7 1.2 bitcast_add_fusion.5
  96.9 4.1 %multiply_reduce_fusion = (f32[512]{0:T(512)S(1)}, f32[512]{0:T(512)S(1)}, f32[8,512,128]{1,2,0:T(8,128)}) fusion(bf16[512,8,128]{0,2,1:T(8,128)(2,1)} %copy.73, f32[8,128]{1,0:T(8,128)S(1)} %copy-done.10, f32[8,512,128]{1,2,0:T(8,128)} %fusion.21, bf16[8,512,128]{2,0,1:T(8,128)(2,1)S(1)} %bitcast.72, f32[8,128,128]{2,1,0:T(8,128)S(1)} %get-tuple-element.131, ...), kind=kOutput, calls=%fused_computation.24 | convolution fusion | flops 138542080 | bytes 6840320 | tf_op jit(solution)/shard_map/hid,hde->hie/dot_general | solution.py:60
  101.0 13.9 %all-reduce.1 = (f32[512]{0:T(512)S(1)}, f32[512]{0:T(512)S(1)}) all-reduce(f32[512]{0:T(512)S(1)} %get-tuple-element.143, f32[512]{0:T(512)S(1)} %get-tuple-element.142), channel_id=1, replica_groups=mesh['ctx'=32,'head'=8] {'head'}, use_global_device_ids=true, to_apply=%region_5.6 | all-reduce | flops 1024 | bytes 8192 | tf_op jit(solution)/shard_map/psum | solution.py:65
  115.0 2.4 fusion.7
  117.4 1.3 fusion.9
  118.8 3.9 %multiply_convert_fusion = bf16[8,512,512]{2,1,0:T(8,128)(2,1)S(1)} fusion(f32[512,512]{1,0:T(8,128)} %copy-done.9, f32[8]{0:T(128)S(1)} %get-tuple-element.174, pred[512,512]{1,0:T(8,128)(4,1)S(1)} %broadcast_compare_fusion, bf16[8,512,128]{1,2,0:T(8,128)(2,1)S(1)} %fusion.7, bf16[8,512,128]{2,0,1:T(8,128)(2,1)S(1)} %bitcast.70), kind=kOutput, calls=%fused_computation.4 | convolution fusion | flops 545259520 | bytes 7602208 | tf_op jit(solution)/shard_map/hie,hje->hij/dot_general | solution.py:79
  122.7 1.2 fusion.14
  125.1 1.6 copy.90
  126.7 2.8 fusion.35
  129.5 2.8 %fusion.17 = f32[8,512,128]{2,1,0:T(8,128)} fusion(bf16[8,512,512]{2,1,0:T(8,128)(2,1)S(1)} %multiply_convert_fusion, bf16[8,512,128]{2,0,1:T(8,128)(2,1)S(1)} %bitcast.73), kind=kOutput, calls=%fused_computation.35 | convolution fusion | flops 536870912 | bytes 7340032 | tf_op jit(solution)/shard_map/hij,hid->hjd/dot_general | solution.py:85
  132.3 99.5 %all-gather.8.cloned.1.call-done = f32[256,128,128]{2,1,0:T(8,128)} async-done(((f32[8,128,128]{2,1,0:T(8,128)}), f32[256,128,128]{2,1,0:T(8,128)}) %all-gather.8.cloned.1.call-update) | async-done | bytes 16777232 | tf_op jit(solution)/shard_map/all_gather | solution.py:11
  231.9 37.2 %while.27 = (s32[]{:T(128)}, f32[8,128,128]{2,1,0:T(8,128)S(1)}, s32[]{:T(128)}, f32[32,8]{1,0:T(8,128)S(1)}, f32[32,8,128,128]{3,2,1,0:T(8,128)}, /*index=5*/s32[]{:T(128)}, s32[]{:T(128)}, s32[]{:T(128)}, s32[]{:T(128)}) while((s32[]{:T(128)}, f32[8,128,128]{2,1,0:T(8,128)S(1)}, s32[]{:T(128)}, f32[32,8]{1,0:T(8,128)S(1)}, ...), condition=%wide.region_7.8_spmd, body=%wide.region_6.7_spmd.sunk | while | flops 262150 | bytes 1573107 | solution.py:20
  231.9 1.3 bitcast_add_fusion.6
  234.4 1.2 bitcast_add_fusion.6
  239.4 1.2 bitcast_add_fusion.6
  240.6 1.2 bitcast_add_fusion.6
  245.6 1.2 bitcast_add_fusion.6
  246.8 1.2 bitcast_add_fusion.6
  269.0 2.0 fusion.1
  271.1 1.6 copy.92
  273.5 1.6 copy.91
  (97 shorter events, 32.6 us)
Async XLA Ops:
  7.2 4.8 %copy-start = (bf16[512,8,128]{2,1,0:T(8,128)(2,1)S(1)}, bf16[512,8,128]{2,1,0:T(8,128)(2,1)}, u32[]{:S(2)}) copy-start(bf16[512,8,128]{2,1,0:T(8,128)(2,1)} %param.12) | copy-start | bytes 3145732
  7.2 88.5 %all-gather.6.cloned.1.call-start = ((), (), s32[]{:S(2)}) async-start(), calls=%async_computation | async-start | bytes 17301504 | tf_op jit(solution)/shard_map/all_gather | solution.py:11
  13.4 69.3 %copy-start.3 = (bf16[512,8,128]{2,1,0:T(8,128)(2,1)S(1)}, bf16[512,8,128]{2,1,0:T(8,128)(2,1)}, u32[]{:S(2)}) copy-start(bf16[512,8,128]{2,1,0:T(8,128)(2,1)} %param.10) | copy-start | bytes 3145732
  13.5 218.3 %all-gather.8.cloned.1.call-start = ((), (), s32[]{:S(2)}) async-start(), calls=%async_computation.1 | async-start | bytes 17301504 | tf_op jit(solution)/shard_map/all_gather | solution.py:11
  82.8 5.4 %copy-start.9 = (f32[512,512]{1,0:T(8,128)}, f32[512,512]{1,0:T(8,128)S(1)}, u32[]{:S(2)}) copy-start(f32[512,512]{1,0:T(8,128)S(1)} %subtract_maximum_fusion) | copy-start | bytes 3145732
  88.2 1.9 copy-start.1
  95.7 1.3 copy-start.10
  115.0 2.4 copy-start.8
  118.8 3.9 %copy-start.5 = (bf16[512,8,128]{2,1,0:T(8,128)(2,1)S(1)}, bf16[512,8,128]{2,1,0:T(8,128)(2,1)}, u32[]{:S(2)}) copy-start(bf16[512,8,128]{2,1,0:T(8,128)(2,1)} %param.11) | copy-start | bytes 3145732
  124.0 2.7 copy-start.2
  126.7 2.8 copy-start.4
  231.8 37.2 %copy-start.6 = (bf16[512,8,128]{2,1,0:T(8,128)(2,1)S(1)}, bf16[512,8,128]{2,1,0:T(8,128)(2,1)}, u32[]{:S(2)}) copy-start(bf16[512,8,128]{2,1,0:T(8,128)(2,1)} %param.11) | copy-start | bytes 3145732
  271.1 1.7 copy-start.7
Sparse Core Ops, SparseCore 0:
  13.6 82.0 all-gather.5
  118.8 112.9 all-gather.7
where the time goes:
time: 284 us; the launch traced here: 282 us
  waiting for transfers between devices  102 us (36%)
  blocking collectives  80.1 us (28%)
  other arithmetic  43.9 us (15%)
  matrix products  28.2 us (10%)
  between operations  15 us (5%)
  local copies, waits for them, and re-layouts  11.4 us (4%)
    all_gather x2, waiting for transfers between devices, prefix(): gathered = jax.tree.map(lambda a: lax.all_gather(a, axis), part)  102 us
    unnamed x1, blocking collectives  66.2 us
    add x31, other arithmetic, combine_states(): return (decay_a * decay_b, decay_b[:, None, None] * state_a + state_b)  37 us
    psum x1, blocking collectives, on_device(): total_sq, total_dot = lax.psum((partial_sq, partial_dot), 'head')  13.9 us
    unnamed x28, local copies, waits for them, and re-layouts  10.7 us
  transfers between devices with their start and end apart: 2, of which 2 were waited for; matrix products, arithmetic and copies ran while one was open for 9% of the time, Pallas kernels for 0%

commit v1 on v0

v1 whole, which is shorter than its diff:
```python
import functools
import math

import jax
import jax.numpy as jnp
from jax import lax
from jax.experimental import pallas as pl
from jax.experimental.pallas import tpu as pltpu
from jax.sharding import PartitionSpec as P

F32 = jnp.float32
BF16 = jnp.bfloat16
LAYER_FACTOR = 1.0 - 78.0 / 79.0 + 1e-05
HEADS = 8
HALF = 4
LENGTH = 512
SIZE = 128
CHIPS = 16
VMEM_LIMIT = 40 * 1024 * 1024


def rate_of(slope_ref, head):
    slope = jnp.full((1, 1), slope_ref[head].astype(F32), F32)
    return jnp.exp((slope + 1.0) * (-8.0 / 64.0 * math.log(2.0))) * LAYER_FACTOR


def rows_of(shape, start=0):
    return lax.broadcasted_iota(jnp.int32, shape, 0).astype(F32) + jnp.float32(start)


def dot(a, b, dims):
    return lax.dot_general(a, b, (dims, ((), ())), preferred_element_type=F32)


NN = ((1,), (0,))
NT = ((1,), (1,))
TN = ((0,), (0,))


def masks(rate):
    shape = (256, 256)
    gap = (
        lax.broadcasted_iota(jnp.int32, shape, 0) - lax.broadcasted_iota(jnp.int32, shape, 1)
    ).astype(F32)
    base = jnp.exp(-rate * gap)
    return jnp.where(gap >= 0.0, base, 0.0), base * jnp.exp(-256.0 * rate)


def masks_t(rate):
    shape = (256, 256)
    gap = (
        lax.broadcasted_iota(jnp.int32, shape, 1) - lax.broadcasted_iota(jnp.int32, shape, 0)
    ).astype(F32)
    base = jnp.exp(-rate * gap)
    return jnp.where(gap >= 0.0, base, 0.0), base * jnp.exp(-256.0 * rate)


def key_kernel(chunk, slope_ref, core_ref, k_ref, v_ref, keep_ref, send_ref, kh_ref, vh_ref, kf, vf, acc):
    step = pl.program_id(0)
    kf[...] = k_ref[...].astype(F32).reshape(chunk * HEADS, SIZE)
    vf[...] = v_ref[...].astype(F32).reshape(chunk * HEADS, SIZE)
    core = core_ref[0]
    for h in range(HEADS):
        k = kf[pl.ds(h, chunk, stride=HEADS), :]
        v = vf[pl.ds(h, chunk, stride=HEADS), :].astype(BF16)
        pos = lax.broadcasted_iota(jnp.int32, (chunk, SIZE), 0) + step * chunk
        weight = jnp.exp(-rate_of(slope_ref, h) * (LENGTH - 1.0 - pos.astype(F32)))
        kh_ref[h] = k.astype(BF16)
        vh_ref[h] = v
        part = dot((k * weight).astype(BF16), v, TN)

        @pl.when(step == 0)
        def _():
            acc[h] = part

        @pl.when(step > 0)
        def _():
            acc[h] += part

    @pl.when(step == pl.num_programs(0) - 1)
    def _():
        @pl.when(core == 0)
        def _():
            keep_ref[...] = acc[:HALF]
            send_ref[...] = acc[HALF:]

        @pl.when(core == 1)
        def _():
            keep_ref[...] = acc[HALF:]
            send_ref[...] = acc[:HALF]


def smem():
    return pl.BlockSpec(memory_space=pltpu.SMEM)


def params():
    return pltpu.CompilerParams(vmem_limit_bytes=VMEM_LIMIT)


def cost(flops, bytes_accessed):
    return pl.CostEstimate(flops=flops, bytes_accessed=bytes_accessed, transcendentals=0)


def head_block(rows=LENGTH, width=SIZE):
    return pl.BlockSpec((1, rows, width), lambda h: (h, 0, 0))


def whole(shape):
    return pl.BlockSpec(shape, lambda *_: (0,) * len(shape))


def sds(shape, dtype):
    return jax.ShapeDtypeStruct(shape, dtype)


def key_states(slope, core, k, v, chunk=128):
    half = (HALF, SIZE, SIZE)
    return pl.pallas_call(
        functools.partial(key_kernel, chunk),
        grid=(LENGTH // chunk,),
        in_specs=[
            smem(),
            smem(),
            pl.BlockSpec((chunk, HEADS, SIZE), lambda i: (i, 0, 0)),
            pl.BlockSpec((chunk, HEADS, SIZE), lambda i: (i, 0, 0)),
        ],
        out_specs=[
            whole(half),
            whole(half),
            pl.BlockSpec((HEADS, chunk, SIZE), lambda i: (0, i, 0)),
            pl.BlockSpec((HEADS, chunk, SIZE), lambda i: (0, i, 0)),
        ],
        out_shape=[
            sds(half, F32),
            sds(half, F32),
            sds((HEADS, LENGTH, SIZE), BF16),
            sds((HEADS, LENGTH, SIZE), BF16),
        ],
        scratch_shapes=[
            pltpu.VMEM((chunk * HEADS, SIZE), F32),
            pltpu.VMEM((chunk * HEADS, SIZE), F32),
            pltpu.VMEM((HEADS, SIZE, SIZE), F32),
        ],
        compiler_params=params(),
        name="key_states",
    )(slope, core, k, v)


def turn_kernel(chunk, q_ref, u_ref, qh_ref, uh_ref, qf, uf):
    qf[...] = q_ref[...].astype(F32).reshape(chunk * HEADS, SIZE)
    uf[...] = u_ref[...].astype(F32).reshape(chunk * HEADS, SIZE)
    for h in range(HEADS):
        qh_ref[h] = qf[pl.ds(h, chunk, stride=HEADS), :].astype(BF16)
        uh_ref[h] = uf[pl.ds(h, chunk, stride=HEADS), :].astype(BF16)


def turn(q, u, chunk=128):
    block = pl.BlockSpec((chunk, HEADS, SIZE), lambda i: (i, 0, 0))
    out = pl.BlockSpec((HEADS, chunk, SIZE), lambda i: (0, i, 0))
    return pl.pallas_call(
        functools.partial(turn_kernel, chunk),
        grid=(LENGTH // chunk,),
        in_specs=[block, block],
        out_specs=[out, out],
        out_shape=[sds((HEADS, LENGTH, SIZE), BF16)] * 2,
        scratch_shapes=[pltpu.VMEM((chunk * HEADS, SIZE), F32)] * 2,
        compiler_params=params(),
        cost_estimate=cost(0, 4 * 2**20),
        name="turn",
    )(q, u)


def local_kernel(slope_ref, q_ref, k_ref, v_ref, loc_ref):
    rate = rate_of(slope_ref, pl.program_id(0))
    diag, off = masks(rate)
    q0, q1 = q_ref[0, :256], q_ref[0, 256:]
    k0, k1 = k_ref[0, :256], k_ref[0, 256:]
    v0, v1 = v_ref[0, :256], v_ref[0, 256:]
    a00 = (dot(q0, k0, NT) * diag).astype(BF16)
    a10 = (dot(q1, k0, NT) * off).astype(BF16)
    a11 = (dot(q1, k1, NT) * diag).astype(BF16)
    loc_ref[0, :256] = dot(a00, v0, NN)
    loc_ref[0, 256:] = dot(a10, v0, NN) + dot(a11, v1, NN)


def local_part(slope, q, k, v):
    return pl.pallas_call(
        local_kernel,
        grid=(HEADS,),
        in_specs=[smem(), head_block(), head_block(), head_block()],
        out_specs=head_block(),
        out_shape=sds((HEADS, LENGTH, SIZE), F32),
        compiler_params=params(),
        cost_estimate=cost(2 * 10**9, 5 * 2**20),
        name="local_part",
    )(slope, q, k, v)


def prefix_kernel(reverse, slope_ref, place_ref, z_ref, out_ref):
    rate = rate_of(slope_ref, place_ref[0])
    decay = jnp.exp(-2.0 * LENGTH * rate)
    state = jnp.zeros((32, SIZE), F32)
    order = list(range(CHIPS))
    if reverse:
        order = order[::-1]
    for p in order:
        out_ref[p] = state
        state = decay * state + z_ref[p]


def prefix(slope, place, z, reverse):
    shape = (CHIPS, 32, SIZE)
    return pl.pallas_call(
        functools.partial(prefix_kernel, reverse),
        in_specs=[smem(), smem(), pl.BlockSpec(memory_space=pltpu.VMEM)],
        out_specs=pl.BlockSpec(memory_space=pltpu.VMEM),
        out_shape=sds(shape, F32),
        compiler_params=params(),
        name="prefix",
    )(slope, place, z)


def state_of(core_ref, head, own_ref, other_ref):
    mine = (head // HALF) == core_ref[0]
    return jnp.where(mine, own_ref[0], other_ref[0]).astype(BF16)


def half_block():
    return pl.BlockSpec((1, SIZE, SIZE), lambda h: (lax.rem(h, HALF), 0, 0))


def output_kernel(slope_ref, core_ref, q_ref, u_ref, gain_ref, own_ref, other_ref, loc_ref, o_ref, sums_ref, sq, dt):
    h = pl.program_id(0)
    rate = rate_of(slope_ref, h)
    state = state_of(core_ref, h, own_ref, other_ref)
    decay_in = jnp.exp(-rate * (rows_of((LENGTH, SIZE)) + 1.0))
    out = loc_ref[0] + decay_in * dot(q_ref[0], state, NN)
    o_ref[0] = out
    scaled = gain_ref[0] * u_ref[0].astype(F32)

    @pl.when(h == 0)
    def _():
        sq[...] = out * out
        dt[...] = out * scaled

    @pl.when(h > 0)
    def _():
        sq[...] += out * out
        dt[...] += out * scaled

    @pl.when(h == HEADS - 1)
    def _():
        for b in range(4):
            sums_ref[pl.ds(b, 1), :] = jnp.sum(sq[b * 128 : (b + 1) * 128, :].T, axis=0, keepdims=True)
            sums_ref[pl.ds(4 + b, 1), :] = jnp.sum(dt[b * 128 : (b + 1) * 128, :].T, axis=0, keepdims=True)


def outputs(slope, core, q, u, gain, own, other, loc):
    return pl.pallas_call(
        output_kernel,
        grid=(HEADS,),
        in_specs=[
            smem(),
            smem(),
            head_block(),
            head_block(),
            pl.BlockSpec((1, 1, SIZE), lambda h: (h, 0, 0)),
            half_block(),
            half_block(),
            head_block(),
        ],
        out_specs=[head_block(), whole((8, SIZE))],
        out_shape=[sds((HEADS, LENGTH, SIZE), F32), sds((8, SIZE), F32)],
        scratch_shapes=[pltpu.VMEM((LENGTH, SIZE), F32)] * 2,
        compiler_params=params(),
        name="outputs",
    )(slope, core, q, u, gain, own, other, loc)


def grad_kernel(features, slope_ref, core_ref, sums_ref, q_ref, u_ref, gain_ref, o_ref, g_ref, keep_ref, send_ref, inv, coef):
    h = pl.program_id(0)

    @pl.when(h == 0)
    def _():
        sq = sums_ref[0:4, :]
        dt = sums_ref[4:8, :]
        root = lax.rsqrt(sq * (1.0 / features) + 1e-06)
        factor = root * root * root * dt * (1.0 / features)
        for b in range(4):
            inv[b * 128 : (b + 1) * 128, :] = jnp.broadcast_to(root[b : b + 1, :], (128, 128)).T
            coef[b * 128 : (b + 1) * 128, :] = jnp.broadcast_to(factor[b : b + 1, :], (128, 128)).T

    rate = rate_of(slope_ref, h)
    scaled = gain_ref[0] * u_ref[0].astype(F32)
    g = (inv[...] * scaled - o_ref[0] * coef[...]).astype(BF16)
    g_ref[0] = g
    first = jnp.exp(-rate * rows_of((LENGTH, SIZE)))
    weighted = (q_ref[0].astype(F32) * first).astype(BF16)
    state = dot(weighted, g, TN)
    slot = lax.rem(h, HALF)

    @pl.when(h // HALF == core_ref[0])
    def _():
        keep_ref[slot] = state

    @pl.when(h // HALF != core_ref[0])
    def _():
        send_ref[slot] = state


def grads(slope, core, sums, q, u, gain, o, features):
    half = (HALF, SIZE, SIZE)
    return pl.pallas_call(
        functools.partial(grad_kernel, features),
        grid=(HEADS,),
        in_specs=[
            smem(),
            smem(),
            whole((8, SIZE)),
            head_block(),
            head_block(),
            pl.BlockSpec((1, 1, SIZE), lambda h: (h, 0, 0)),
            head_block(),
        ],
        out_specs=[head_block(), whole(half), whole(half)],
        out_shape=[sds((HEADS, LENGTH, SIZE), BF16), sds(half, F32), sds(half, F32)],
        scratch_shapes=[pltpu.VMEM((LENGTH, SIZE), F32)] * 2,
        compiler_params=params(),
        name="grads",
    )(slope, core, sums, q, u, gain, o)


def grad_query_kernel(slope_ref, core_ref, g_ref, k_ref, v_ref, own_ref, other_ref, out_ref, wide):
    h = pl.program_id(0)
    rate = rate_of(slope_ref, h)
    diag, off = masks(rate)
    g0, g1 = g_ref[0, :256], g_ref[0, 256:]
    k0, k1 = k_ref[0, :256], k_ref[0, 256:]
    v0, v1 = v_ref[0, :256], v_ref[0, 256:]
    state = state_of(core_ref, h, own_ref, other_ref)
    b00 = (dot(g0, v0, NT) * diag).astype(BF16)
    b10 = (dot(g1, v0, NT) * off).astype(BF16)
    b11 = (dot(g1, v1, NT) * diag).astype(BF16)
    decay_in = jnp.exp(-rate * (rows_of((LENGTH, SIZE)) + 1.0))
    carried = decay_in * dot(g_ref[0], state, NT)
    wide[pl.ds(h, 256, stride=HEADS), :] = dot(b00, k0, NN) + carried[:256]
    wide[pl.ds(h + 256 * HEADS, 256, stride=HEADS), :] = (
        dot(b10, k0, NN) + dot(b11, k1, NN) + carried[256:]
    )

    @pl.when(h == HEADS - 1)
    def _():
        out_ref[...] = wide[...].reshape(LENGTH, HEADS, SIZE).astype(BF16)


def grad_query(slope, core, g, k, v, own, other):
    return pl.pallas_call(
        grad_query_kernel,
        grid=(HEADS,),
        in_specs=[smem(), smem(), head_block(), head_block(), head_block(), half_block(), half_block()],
        out_specs=whole((LENGTH, HEADS, SIZE)),
        out_shape=sds((LENGTH, HEADS, SIZE), BF16),
        scratch_shapes=[pltpu.VMEM((LENGTH * HEADS, SIZE), F32)],
        compiler_params=params(),
        cost_estimate=cost(3 * 10**9, 5 * 2**20),
        name="grad_query",
    )(slope, core, g, k, v, own, other)


def back_kernel(slope_ref, a_ref, b_ref, c_ref, out_ref):
    rate = rate_of(slope_ref, pl.program_id(0))
    diag, off = masks_t(rate)
    a0, a1 = a_ref[0, :256], a_ref[0, 256:]
    b0, b1 = b_ref[0, :256], b_ref[0, 256:]
    c0, c1 = c_ref[0, :256], c_ref[0, 256:]
    t00 = (dot(a0, b0, NT) * diag).astype(BF16)
    t01 = (dot(a0, b1, NT) * off).astype(BF16)
    t11 = (dot(a1, b1, NT) * diag).astype(BF16)
    out_ref[0, :256] = dot(t00, c0, NN) + dot(t01, c1, NN)
    out_ref[0, 256:] = dot(t11, c1, NN)


def back(slope, a, b, c, name):
    return pl.pallas_call(
        back_kernel,
        grid=(HEADS,),
        in_specs=[smem(), head_block(), head_block(), head_block()],
        out_specs=head_block(),
        out_shape=sds((HEADS, LENGTH, SIZE), F32),
        compiler_params=params(),
        cost_estimate=cost(2 * 10**9, 5 * 2**20),
        name=name,
    )(slope, a, b, c)


def finish_kernel(chunk, slope_ref, core_ref, k_ref, v_ref, kl_ref, vl_ref, own_ref, other_ref, gk_ref, gv_ref, wk, wv):
    step = pl.program_id(0)
    core = core_ref[0]
    for h in range(HEADS):
        rate = rate_of(slope_ref, h)
        pos = (lax.broadcasted_iota(jnp.int32, (chunk, SIZE), 0) + step * chunk).astype(F32)
        decay = jnp.exp(-rate * (LENGTH - pos))
        mine = core == h // HALF
        state = jnp.where(mine, own_ref[h % HALF], other_ref[h % HALF]).astype(BF16)
        wk[pl.ds(h, chunk, stride=HEADS), :] = kl_ref[h] + decay * dot(v_ref[h], state, NT)
        wv[pl.ds(h, chunk, stride=HEADS), :] = vl_ref[h] + decay * dot(k_ref[h], state, NN)
    gk_ref[...] = wk[...].reshape(chunk, HEADS, SIZE).astype(BF16)
    gv_ref[...] = wv[...].reshape(chunk, HEADS, SIZE).astype(BF16)


def finish(slope, core, k, v, kl, vl, own, other, chunk=128):
    half = (HALF, SIZE, SIZE)
    rows = pl.BlockSpec((HEADS, chunk, SIZE), lambda i: (0, i, 0))
    out = pl.BlockSpec((chunk, HEADS, SIZE), lambda i: (i, 0, 0))
    return pl.pallas_call(
        functools.partial(finish_kernel, chunk),
        grid=(LENGTH // chunk,),
        in_specs=[smem(), smem(), rows, rows, rows, rows, whole(half), whole(half)],
        out_specs=[out, out],
        out_shape=[sds((LENGTH, HEADS, SIZE), BF16)] * 2,
        scratch_shapes=[pltpu.VMEM((chunk * HEADS, SIZE), F32)] * 2,
        compiler_params=params(),
        name="finish",
    )(slope, core, k, v, kl, vl, own, other)


def exchange(a):
    return lax.ppermute(a, "ctx", [(i, i ^ 1) for i in range(2 * CHIPS)])


def all_to_all(a):
    groups = [[2 * p + c for p in range(CHIPS)] for c in range(2)]
    return lax.all_to_all(a, "ctx", 0, 0, axis_index_groups=groups, tiled=True)


def scan_states(slope, place, core, decay, keep, send, reverse):
    recv = exchange(send)
    first = core == 0
    low = jnp.where(first, keep, recv)
    high = jnp.where(first, recv, keep)
    if reverse:
        total = low + decay * high
    else:
        total = decay * low + high
    moved = all_to_all(total.reshape(CHIPS, 32, SIZE))
    state = all_to_all(prefix(slope, place, moved, reverse)).reshape(HALF, SIZE, SIZE)
    if reverse:
        beyond = high + decay * state
        mine = jnp.where(first, beyond, state)
        give = jnp.where(first, state, beyond)
    else:
        beyond = decay * state + low
        mine = jnp.where(first, state, beyond)
        give = jnp.where(first, beyond, state)
    return mine, exchange(give)


def on_device(queries, key_rows, value_rows, upstream, norm_gain, slope_index):
    place = lax.axis_index("ctx")
    core = lax.rem(place, 2)
    chip = place // 2
    core_ref = core.reshape(1).astype(jnp.int32)
    own_head = (core * HALF + chip // (CHIPS // HALF)).reshape(1).astype(jnp.int32)
    rate = 2.0 ** (-8.0 * (slope_index.astype(F32) + 1.0) / 64.0) * LAYER_FACTOR
    block_decay = jnp.exp(-rate * LENGTH)
    decay = jnp.where(core == 0, block_decay[:HALF], block_decay[HALF:])[:, None, None]
    gain = norm_gain.reshape(HEADS, 1, SIZE)

    keep, send, kh, vh = key_states(slope_index, core_ref, key_rows, value_rows)
    qh, uh = turn(queries, upstream)
    loc = local_part(slope_index, qh, kh, vh)
    e_own, e_other = scan_states(slope_index, own_head, core, decay, keep, send, False)
    out, sums = outputs(slope_index, core_ref, qh, uh, gain, e_own, e_other, loc)
    sums = lax.psum(sums, "head")
    features = float(lax.axis_size("head") * HEADS * SIZE)
    g, keep, send = grads(slope_index, core_ref, sums, qh, uh, gain, out, features)
    gv_local = back(slope_index, kh, qh, g, "gv_local")
    gk_local = back(slope_index, vh, g, qh, "gk_local")
    gq = grad_query(slope_index, core_ref, g, kh, vh, e_own, e_other)
    l_own, l_other = scan_states(slope_index, own_head, core, decay, keep, send, True)
    gk, gv = finish(slope_index, core_ref, kh, vh, gk_local, gv_local, l_own, l_other)
    return gq, gk, gv


def solution(mesh):
    rows = P("ctx", "head", None)
    return jax.shard_map(
        on_device,
        mesh=mesh,
        in_specs=(rows, rows, rows, rows, P("head", None), P("head")),
        out_specs=(rows, rows, rows),
        check_vma=False,
    )
```

time: 284 us -> 130 us (0.46)
  waiting for transfers between devices: 102 us -> 10.3 us
  blocking collectives: 80.1 us -> 37.3 us
  other arithmetic: 43.9 us -> 2.23 us
  Pallas kernels: 0 us -> 38.6 us
  matrix products: 28.2 us -> 0 us
  starting transfers between devices: 0.08 us -> 20.8 us
  between operations: 15 us -> 0.94 us
  local copies, waits for them, and re-layouts: 11.4 us -> 18.6 us
    all_gather x2 -> x0, waiting for transfers between devices: 102 us -> none  [prefix(): gathered = jax.tree.map(lambda a: lax.all_gather(a, axis), part)]
    unnamed x1 -> x0, blocking collectives: 66.2 us -> none
    pallas_call x0 -> x11, Pallas kernels: none -> 38.6 us  [the longest x2 8.23 us: back(): pl.pallas_call(back_kernel, grid=(HEADS,), in_specs=[smem(), head_block()...]
    add x31 -> x2, other arithmetic: 37 us -> 0.88 us  [the longest x1 0.79 us: scan_states(): total = decay * low + high]
    dot_general x12 -> x0, matrix products: 28.2 us -> none  [the longest x1 4.1 us: on_device(): jnp.einsum('hid,hde->hie', q_heads, entering_b, preferred_element_type=jn...]
    all_to_all x0 -> x2, blocking collectives: none -> 21.1 us  [all_to_all(): return lax.all_to_all(a, 'ctx', 0, 0, axis_index_groups=groups, tiled=True)]
    ppermute x0 -> x4, starting transfers between devices: none -> 11.6 us  [exchange(): return lax.ppermute(a, 'ctx', [(i, i ^ 1) for i in range(2 * CHIPS)])]
    all_to_all x0 -> x2, starting transfers between devices: none -> 9.21 us  [all_to_all(): return lax.all_to_all(a, 'ctx', 0, 0, axis_index_groups=groups, tiled=True)]
  transfers between devices with their start and end apart: 2 -> 6, of which waited for: 2 -> 3; matrix products, arithmetic and copies ran while one was open for 9% -> 0% of each run, Pallas kernels for 0% -> 15%
where the time goes in v1:
time: 130 us; the launch traced here: 129 us
  Pallas kernels  38.6 us (30%)
  blocking collectives  37.3 us (29%)
  starting transfers between devices  20.8 us (16%)
  local copies, waits for them, and re-layouts  18.6 us (14%)
  waiting for transfers between devices  10.3 us (8%)
  other arithmetic  2.23 us (2%)
    all_to_all x2, blocking collectives, all_to_all(): return lax.all_to_all(a, 'ctx', 0, 0, axis_index_groups=groups, tiled=True)  21.1 us
    unnamed x52, local copies, waits for them, and re-layouts  18.6 us
    psum x1, blocking collectives, on_device(): sums = lax.psum(sums, 'head')  16.2 us
    ppermute x4, starting transfers between devices, exchange(): return lax.ppermute(a, 'ctx', [(i, i ^ 1) for i in range(2 * CHIPS)])  11.6 us
    all_to_all x2, starting transfers between devices, all_to_all(): return lax.all_to_all(a, 'ctx', 0, 0, axis_index_groups=groups, tiled=True)  9.21 us
    pallas_call x2, Pallas kernels, back(): pl.pallas_call(back_kernel, grid=(HEADS,), in_specs=[smem(), head_block()...  8.23 us
    all_to_all x2, waiting for transfers between devices, all_to_all(): return lax.all_to_all(a, 'ctx', 0, 0, axis_index_groups=groups, tiled=True)  8.08 us
    pallas_call x1, Pallas kernels, key_states(): pl.pallas_call(functools.partial(key_kernel, chunk), grid=(LENGTH // chun...  7.97 us
  transfers between devices with their start and end apart: 6, of which 3 were waited for; matrix products, arithmetic and copies ran while one was open for 0% of the time, Pallas kernels for 15%

profile of v1, /device:TPU:1, one launch (start us, length us, event | category | flops | bytes accessed | tf_op | source)
XLA Modules:
  0.0 128.9 jit_solution(12372351693771597663)
XLA Ops:
  0.7 1.2 copy-done.6
  1.9 1.2 copy-done.7
  3.8 8.0 %key_states.1 = (f32[4,128,128]{2,1,0:T(8,128)S(1)}, f32[4,128,128]{2,1,0:T(8,128)S(1)}, bf16[8,512,128]{2,1,0:T(8,128)(2,1)S(1)}, bf16[8,512,128]{2,1,0:T(8,128)(2,1)S(1)}) custom-call(s32[8]{0:T(128)S(1)} %copy-done.19, s32[1]{0:T(128)} %bitcast.core_ref, bf16[512,8,128]{2,1,0:T(8,128)(2,1)S(1)} %copy-done.6, bf16[512,8,128]{2,1,0:T(8,128)(2,1)S(1)} %copy-done.7), custom_call_target="tpu_custom_call" | custom-call | tf_op jit(solution)/shard_map/key_states/pallas_call | solution.py:119
  13.7 3.2 %collective-permute-start = (f32[4,128,128]{2,1,0:T(8,128)S(1)}, f32[4,128,128]{2,1,0:T(8,128)S(1)}, u32[]{:S(2)}, u32[]{:S(2)}) collective-permute-start(f32[4,128,128]{2,1,0:T(8,128)S(1)} %get-tuple-element.19), channel_id=1, source_target_pairs={{0,8},{8,0},{16,24},{24,16},{32,40},{40,32},{48,56},{56,48},{64,72... | collective-permute-start | bytes 786440 | tf_op jit(solution)/shard_map/ppermute | solution.py:429
  18.9 5.0 %all-to-all-start = ((f32[16,32,128]{2,1,0:T(8,128)}), f32[16,32,128]{2,1,0:T(8,128)S(1)}, u32[]{:S(2)}, u32[]{:S(2)}) async-start(f32[16,32,128]{2,1,0:T(8,128)} %bitcast.3), calls=%async_computation | async-start | bytes 524288 | tf_op jit(solution)/shard_map/all_to_all | solution.py:434
  23.9 8.1 %all-to-all-done.z_ref = f32[16,32,128]{2,1,0:T(8,128)S(1)} async-done(((f32[16,32,128]{2,1,0:T(8,128)}), f32[16,32,128]{2,1,0:T(8,128)S(1)}, u32[]{:S(2)}, u32[]{:S(2)}) %all-to-all-start) | async-done | bytes 262176 | tf_op jit(solution)/shard_map/all_to_all | solution.py:434
  32.6 10.4 %all_to_all.20 = f32[16,32,128]{2,1,0:T(8,128)S(1)} all-to-all(f32[16,32,128]{2,1,0:T(8,128)S(1)} %prefix.2), channel_id=1, replica_groups={{0,16,32,48,64,80,96,112,128,144,160,176,192,208,224,240},{8,24,40,56,7..., dimensions={0} | all-to-all | bytes 524288 | tf_op jit(solution)/shard_map/all_to_all | solution.py:434
  43.1 3.0 %collective-permute-start.1 = (f32[4,128,128]{2,1,0:T(8,128)S(1)}, f32[4,128,128]{2,1,0:T(8,128)S(1)}, u32[]{:S(2)}, u32[]{:S(2)}) collective-permute-start(f32[4,128,128]{2,1,0:T(8,128)S(1)} %get-tuple-element.31), channel_id=1, source_target_pairs={{0,8},{8,0},{16,24},{24,16},{32,40},{40,32},{48,56},{56,48},{64,72... | collective-permute-start | bytes 786440 | tf_op jit(solution)/shard_map/ppermute | solution.py:429
  46.1 1.2 copy-done.5
  48.5 4.1 %local_part.1.loc_ref = f32[8,512,128]{2,1,0:T(8,128)S(1)} custom-call(s32[8]{0:T(128)S(1)} %copy-done.20, bf16[8,512,128]{2,1,0:T(8,128)(2,1)S(1)} %get-tuple-element.16.q_ref.c_ref.b_ref, bf16[8,512,128]{2,1,0:T(8,128)(2,1)S(1)} %copy-done.10, bf16[8,512,128]{2,1,0:T(8,128)(2,1)S(1)} %copy-done.14), custom_call_target="tpu_custom_call" | custom-call | flops 2000000000 | bytes 5242880 | tf_op jit(solution)/shard_map/local_part/pallas_call | solution.py:188
  52.6 2.8 %outputs.1 = (f32[8,512,128]{2,1,0:T(8,128)S(1)}, f32[8,128]{1,0:T(8,128)S(1)}) custom-call(s32[8]{0:T(128)S(1)} %copy-done.20, s32[1]{0:T(128)} %bitcast.core_ref, bf16[8,512,128]{2,1,0:T(8,128)(2,1)S(1)} %get-tuple-element.16.q_ref.c_ref.b_ref, bf16[8,512,128]{2,1,0:T(8,128)(2,1)S(1)} %get-tuple-element.17.u_ref, f32[8,1,128]{2,1,0:T(1,128)S(1)} %bitcast.27, ...), custom_call_target="tpu_custom_call" | custom-call | tf_op jit(solution)/shard_map/outputs/pallas_call | solution.py:260
  55.5 1.4 %copy-done = f32[8,512,128]{2,1,0:T(8,128)} copy-done((f32[8,512,128]{2,1,0:T(8,128)}, f32[8,512,128]{2,1,0:T(8,128)S(1)}, u32[]{:S(2)}) %copy-start) | copy-done | bytes 2097176
  56.9 16.2 %psum.7.sums_ref = f32[8,128]{1,0:T(8,128)S(1)} all-reduce(f32[8,128]{1,0:T(8,128)S(1)} %get-tuple-element.22), channel_id=1, replica_groups=mesh['ctx'=32,'head'=8] {'head'}, use_global_device_ids=true, to_apply=%region_0.1 | all-reduce | flops 1024 | bytes 8192 | tf_op jit(solution)/shard_map/psum | solution.py:475
  73.1 1.6 %copy-done.1 = f32[8,512,128]{2,1,0:T(8,128)S(1)} copy-done((f32[8,512,128]{2,1,0:T(8,128)S(1)}, f32[8,512,128]{2,1,0:T(8,128)}, u32[]{:S(2)}) %copy-start.1) | copy-done | bytes 2097176
  74.7 3.2 %grads.1 = (bf16[8,512,128]{2,1,0:T(8,128)(2,1)S(1)}, f32[4,128,128]{2,1,0:T(8,128)S(1)}, f32[4,128,128]{2,1,0:T(8,128)S(1)}) custom-call(s32[8]{0:T(128)S(1)} %copy-done.20, s32[1]{0:T(128)} %bitcast.core_ref, f32[8,128]{1,0:T(8,128)S(1)} %psum.7.sums_ref, bf16[8,512,128]{2,1,0:T(8,128)(2,1)S(1)} %get-tuple-element.16.q_ref.c_ref.b_ref, ...), custom_call_target="tpu_custom_call" | custom-call | tf_op jit(solution)/shard_map/grads/pallas_call | solution.py:314
  78.8 3.8 %collective-permute-start.2 = (f32[4,128,128]{2,1,0:T(8,128)S(1)}, f32[4,128,128]{2,1,0:T(8,128)S(1)}, u32[]{:S(2)}, u32[]{:S(2)}) collective-permute-start(f32[4,128,128]{2,1,0:T(8,128)S(1)} %get-tuple-element.25), channel_id=1, source_target_pairs={{0,8},{8,0},{16,24},{24,16},{32,40},{40,32},{48,56},{56,48},{64,72... | collective-permute-start | bytes 786440 | tf_op jit(solution)/shard_map/ppermute | solution.py:429
  82.6 1.2 collective-permute-done.2
  83.9 10.7 %all_to_all.21.z_ref = f32[16,32,128]{2,1,0:T(8,128)S(1)} all-to-all(f32[16,32,128]{2,1,0:T(8,128)S(1)} %bitcast.29), channel_id=1, replica_groups={{0,16,32,48,64,80,96,112,128,144,160,176,192,208,224,240},{8,24,40,56,7..., dimensions={0} | all-to-all | bytes 524288 | tf_op jit(solution)/shard_map/all_to_all | solution.py:434
  94.6 1.3 %prefix.3 = f32[16,32,128]{2,1,0:T(8,128)} custom-call(s32[8]{0:T(128)S(1)} %copy-done.20, s32[1]{0:T(128)} %bitcast.2.place_ref, f32[16,32,128]{2,1,0:T(8,128)S(1)} %all_to_all.21.z_ref), custom_call_target="tpu_custom_call" | custom-call | tf_op jit(solution)/shard_map/prefix/pallas_call | solution.py:214
  95.9 4.2 %all-to-all-start.3 = ((f32[16,32,128]{2,1,0:T(8,128)}), f32[16,32,128]{2,1,0:T(8,128)}, u32[]{:S(2)}, u32[]{:S(2)}) async-start(f32[16,32,128]{2,1,0:T(8,128)} %prefix.3), calls=%async_computation.3 | async-start | bytes 524288 | tf_op jit(solution)/shard_map/all_to_all | solution.py:434
  100.1 1.2 copy-done.11
  101.4 1.2 copy-done.23
  102.6 4.1 %gv_local.1.vl_ref = f32[8,512,128]{2,1,0:T(8,128)S(1)} custom-call(s32[8]{0:T(128)S(1)} %copy-done.20, bf16[8,512,128]{2,1,0:T(8,128)(2,1)S(1)} %copy-done.11, bf16[8,512,128]{2,1,0:T(8,128)(2,1)S(1)} %get-tuple-element.16.q_ref.c_ref.b_ref, bf16[8,512,128]{2,1,0:T(8,128)(2,1)S(1)} %copy-done.23), custom_call_target="tpu_custom_call" | custom-call | flops 2000000000 | bytes 5242880 | tf_op jit(solution)/shard_map/gv_local/pallas_call | solution.py:385
  106.7 4.1 %gk_local.1.kl_ref = f32[8,512,128]{2,1,0:T(8,128)S(1)} custom-call(s32[8]{0:T(128)S(1)} %copy-done.20, bf16[8,512,128]{2,1,0:T(8,128)(2,1)S(1)} %copy-done.15, bf16[8,512,128]{2,1,0:T(8,128)(2,1)S(1)} %copy-done.23, bf16[8,512,128]{2,1,0:T(8,128)(2,1)S(1)} %get-tuple-element.16.q_ref.c_ref.b_ref), custom_call_target="tpu_custom_call" | custom-call | flops 2000000000 | bytes 5242880 | tf_op jit(solution)/shard_map/gk_local/pallas_call | solution.py:385
  110.9 1.4 %copy-done.2 = f32[8,512,128]{2,1,0:T(8,128)} copy-done((f32[8,512,128]{2,1,0:T(8,128)}, f32[8,512,128]{2,1,0:T(8,128)S(1)}, u32[]{:S(2)}) %copy-start.2) | copy-done | bytes 2097176
  112.2 1.1 bitcast_select_fusion
  113.4 1.6 %collective-permute-start.3 = (f32[4,128,128]{2,1,0:T(8,128)S(1)}, f32[4,128,128]{2,1,0:T(8,128)S(1)}, u32[]{:S(2)}, u32[]{:S(2)}) collective-permute-start(f32[4,128,128]{2,1,0:T(8,128)S(1)} %get-tuple-element.29), channel_id=1, source_target_pairs={{0,8},{8,0},{16,24},{24,16},{32,40},{40,32},{48,56},{56,48},{64,72... | collective-permute-start | bytes 786440 | tf_op jit(solution)/shard_map/ppermute | solution.py:429
  115.0 1.2 copy-done.12
  116.2 1.2 copy-done.16
  118.4 1.2 copy-done.24
  119.6 5.2 %grad_query.1 = bf16[512,8,128]{2,1,0:T(8,128)(2,1)} custom-call(s32[8]{0:T(128)S(1)} %copy-done.20, s32[1]{0:T(128)} %bitcast.core_ref, bf16[8,512,128]{2,1,0:T(8,128)(2,1)S(1)} %copy-done.24, bf16[8,512,128]{2,1,0:T(8,128)(2,1)S(1)} %copy-done.12, bf16[8,512,128]{2,1,0:T(8,128)(2,1)S(1)} %copy-done.16, f32[4,128,128]{2,1,0:T(8,128)S(1)} %get-tuple-element.32.own_ref, ...), custom_call_target="tpu_custom_call" | custom-call | flops 3000000000 | bytes 5242880 | tf_op jit(solution)/shard_map/grad_query/pallas_call | solution.py:358
  124.8 4.0 %finish.1 = (bf16[512,8,128]{2,1,0:T(8,128)(2,1)}, bf16[512,8,128]{2,1,0:T(8,128)(2,1)}) custom-call(s32[8]{0:T(128)S(1)} %copy-done.20, s32[1]{0:T(128)} %bitcast.core_ref, bf16[8,512,128]{2,1,0:T(8,128)(2,1)S(1)} %copy-done.12, bf16[8,512,128]{2,1,0:T(8,128)(2,1)S(1)} %copy-done.16, f32[8,512,128]{2,1,0:T(8,128)S(1)} %copy-done.3, ...), custom_call_target="tpu_custom_call" | custom-call | tf_op jit(solution)/shard_map/finish/pallas_call | solution.py:416
  (52 shorter events, 8.4 us)
Async XLA Ops:
  0.6 31.4 %copy-start.20 = (s32[8]{0:T(128)S(1)}, s32[8]{0:T(128)}, u32[]{:S(2)}) copy-start(s32[8]{0:T(128)} %slope_ref.19) | copy-start | bytes 100
  0.6 1.2 copy-start.6
  1.9 1.2 copy-start.7
  3.1 0.7 copy-start.19
  11.7 1.0 copy-start.9
  12.7 1.0 copy-start.13
  13.7 32.4 %copy-start.4 = (bf16[512,8,128]{2,1,0:T(8,128)(2,1)S(1)}, bf16[512,8,128]{2,1,0:T(8,128)(2,1)}, u32[]{:S(2)}) copy-start(bf16[512,8,128]{2,1,0:T(8,128)(2,1)} %q_ref.1) | copy-start | bytes 3145732
  13.7 4.4 %collective-permute-start = (f32[4,128,128]{2,1,0:T(8,128)S(1)}, f32[4,128,128]{2,1,0:T(8,128)S(1)}, u32[]{:S(2)}, u32[]{:S(2)}) collective-permute-start(f32[4,128,128]{2,1,0:T(8,128)S(1)} %get-tuple-element.19), channel_id=1, source_target_pairs={{0,8},{8,0},{16,24},{24,16},{32,40},{40,32},{48,56},{56,48},{64,72... | collective-permute-start | bytes 786440 | tf_op jit(solution)/shard_map/ppermute | solution.py:429
  18.9 13.1 %all-to-all-start = ((f32[16,32,128]{2,1,0:T(8,128)}), f32[16,32,128]{2,1,0:T(8,128)S(1)}, u32[]{:S(2)}, u32[]{:S(2)}) async-start(f32[16,32,128]{2,1,0:T(8,128)} %bitcast.3), calls=%async_computation | async-start | bytes 524288 | tf_op jit(solution)/shard_map/all_to_all | solution.py:434
  32.0 16.4 %copy-start.14 = (bf16[8,512,128]{2,1,0:T(8,128)(2,1)S(1)}, bf16[8,512,128]{2,1,0:T(8,128)(2,1)}, u32[]{:S(2)}) copy-start(bf16[8,512,128]{2,1,0:T(8,128)(2,1)} %copy-done.13) | copy-start | bytes 3145732
  32.6 15.8 %copy-start.10 = (bf16[8,512,128]{2,1,0:T(8,128)(2,1)S(1)}, bf16[8,512,128]{2,1,0:T(8,128)(2,1)}, u32[]{:S(2)}) copy-start(bf16[8,512,128]{2,1,0:T(8,128)(2,1)} %copy-done.9) | copy-start | bytes 3145732
  43.1 9.5 %collective-permute-start.1 = (f32[4,128,128]{2,1,0:T(8,128)S(1)}, f32[4,128,128]{2,1,0:T(8,128)S(1)}, u32[]{:S(2)}, u32[]{:S(2)}) collective-permute-start(f32[4,128,128]{2,1,0:T(8,128)S(1)} %get-tuple-element.31), channel_id=1, source_target_pairs={{0,8},{8,0},{16,24},{24,16},{32,40},{40,32},{48,56},{56,48},{64,72... | collective-permute-start | bytes 786440 | tf_op jit(solution)/shard_map/ppermute | solution.py:429
  46.1 1.2 copy-start.5
  48.4 4.2 %copy-start.21 = (f32[8,128]{1,0:T(8,128)S(1)}, f32[8,128]{1,0:T(8,128)}, u32[]{:S(2)}) copy-start(f32[8,128]{1,0:T(8,128)} %param.10) | copy-start | bytes 12292
  52.6 2.9 %copy-start.17 = (f32[4,128,128]{2,1,0:T(8,128)}, f32[4,128,128]{2,1,0:T(8,128)S(1)}, u32[]{:S(2)}) copy-start(f32[4,128,128]{2,1,0:T(8,128)S(1)} %collective-permute-done.1.other_ref) | copy-start | bytes 786436
  55.5 1.4 %copy-start = (f32[8,512,128]{2,1,0:T(8,128)}, f32[8,512,128]{2,1,0:T(8,128)S(1)}, u32[]{:S(2)}) copy-start(f32[8,512,128]{2,1,0:T(8,128)S(1)} %get-tuple-element.23.o_ref) | copy-start | bytes 6291460
  73.1 1.6 %copy-start.1 = (f32[8,512,128]{2,1,0:T(8,128)S(1)}, f32[8,512,128]{2,1,0:T(8,128)}, u32[]{:S(2)}) copy-start(f32[8,512,128]{2,1,0:T(8,128)} %copy-done) | copy-start | bytes 6291460
  77.9 1.0 copy-start.22
  78.8 5.0 %copy-start.8 = (f32[4,128,128]{2,1,0:T(8,128)}, f32[4,128,128]{2,1,0:T(8,128)S(1)}, u32[]{:S(2)}) copy-start(f32[4,128,128]{2,1,0:T(8,128)S(1)} %get-tuple-element.26) | copy-start | bytes 786436
  78.8 4.9 %collective-permute-start.2 = (f32[4,128,128]{2,1,0:T(8,128)S(1)}, f32[4,128,128]{2,1,0:T(8,128)S(1)}, u32[]{:S(2)}, u32[]{:S(2)}) collective-permute-start(f32[4,128,128]{2,1,0:T(8,128)S(1)} %get-tuple-element.25), channel_id=1, source_target_pairs={{0,8},{8,0},{16,24},{24,16},{32,40},{40,32},{48,56},{56,48},{64,72... | collective-permute-start | bytes 786440 | tf_op jit(solution)/shard_map/ppermute | solution.py:429
  83.8 16.3 %copy-start.25 = (f32[4,128,128]{2,1,0:T(8,128)}, f32[4,128,128]{2,1,0:T(8,128)S(1)}, u32[]{:S(2)}) copy-start(f32[4,128,128]{2,1,0:T(8,128)S(1)} %collective-permute-done.2) | copy-start | bytes 786436
  95.9 16.3 %all-to-all-start.3 = ((f32[16,32,128]{2,1,0:T(8,128)}), f32[16,32,128]{2,1,0:T(8,128)}, u32[]{:S(2)}, u32[]{:S(2)}) async-start(f32[16,32,128]{2,1,0:T(8,128)} %prefix.3), calls=%async_computation.3 | async-start | bytes 524288 | tf_op jit(solution)/shard_map/all_to_all | solution.py:434
  100.1 1.2 copy-start.11
  101.4 1.2 copy-start.23
  102.6 4.1 %copy-start.15 = (bf16[8,512,128]{2,1,0:T(8,128)(2,1)S(1)}, bf16[8,512,128]{2,1,0:T(8,128)(2,1)}, u32[]{:S(2)}) copy-start(bf16[8,512,128]{2,1,0:T(8,128)(2,1)} %copy-done.13) | copy-start | bytes 3145732
  110.8 1.4 %copy-start.2 = (f32[8,512,128]{2,1,0:T(8,128)}, f32[8,512,128]{2,1,0:T(8,128)S(1)}, u32[]{:S(2)}) copy-start(f32[8,512,128]{2,1,0:T(8,128)S(1)} %gk_local.1.kl_ref) | copy-start | bytes 6291460
  113.4 11.5 %copy-start.3 = (f32[8,512,128]{2,1,0:T(8,128)S(1)}, f32[8,512,128]{2,1,0:T(8,128)}, u32[]{:S(2)}) copy-start(f32[8,512,128]{2,1,0:T(8,128)} %copy-done.2) | copy-start | bytes 6291460
  113.4 11.5 %collective-permute-start.3 = (f32[4,128,128]{2,1,0:T(8,128)S(1)}, f32[4,128,128]{2,1,0:T(8,128)S(1)}, u32[]{:S(2)}, u32[]{:S(2)}) collective-permute-start(f32[4,128,128]{2,1,0:T(8,128)S(1)} %get-tuple-element.29), channel_id=1, source_target_pairs={{0,8},{8,0},{16,24},{24,16},{32,40},{40,32},{48,56},{56,48},{64,72... | collective-permute-start | bytes 786440 | tf_op jit(solution)/shard_map/ppermute | solution.py:429
  115.0 1.2 copy-start.12
  116.2 1.2 copy-start.16
  117.4 0.9 copy-start.18
  118.4 1.2 copy-start.24

commit v2 on v0

v2 whole, which is shorter than its diff:
```python
import functools
import math

import jax
import jax.numpy as jnp
from jax import lax
from jax.experimental import pallas as pl
from jax.experimental.pallas import tpu as pltpu
from jax.sharding import PartitionSpec as P

F32 = jnp.float32
BF16 = jnp.bfloat16
LAYER_FACTOR = 1.0 - 78.0 / 79.0 + 1e-05
HEADS = 8
LENGTH = 512
SIZE = 128
BLOCKS = 32
SLICE = HEADS * SIZE // BLOCKS
CHUNK = 128
PARTS = LENGTH // CHUNK
VMEM_LIMIT = 24 * 1024 * 1024

NN = ((1,), (0,))
NT = ((1,), (1,))
TN = ((0,), (0,))


def rate_of(slope_ref, head):
    slope = jnp.full((1, 1), slope_ref[head].astype(F32), F32)
    return jnp.exp((slope + 1.0) * (-8.0 / 64.0 * math.log(2.0))) * LAYER_FACTOR


def rows_of(shape, start=0):
    return (lax.broadcasted_iota(jnp.int32, shape, 0) + start).astype(F32)


def dot(a, b, dims):
    return lax.dot_general(a, b, (dims, ((), ())), preferred_element_type=F32)


def masks(rate, transposed=False):
    shape = (256, 256)
    gap = lax.broadcasted_iota(jnp.int32, shape, 0) - lax.broadcasted_iota(jnp.int32, shape, 1)
    if transposed:
        gap = -gap
    base = jnp.exp(-rate * gap.astype(F32))
    return jnp.where(gap >= 0, base, 0.0), base * jnp.exp(-256.0 * rate)


def hbm(x):
    return pltpu.with_memory_space_constraint(x, pltpu.HBM)


def near(x):
    return pltpu.with_memory_space_constraint(x, pltpu.VMEM)


def call(body, name, ins, outs, scratch=(), flops=0, moved=0):
    kinds = {"smem": pltpu.SMEM, "vmem": pltpu.VMEM, "hbm": pl.ANY, "any": pl.ANY}
    args, in_specs = [], []
    for kind, x in ins:
        in_specs.append(pl.BlockSpec(memory_space=kinds[kind]))
        args.append({"vmem": near, "hbm": hbm}.get(kind, lambda a: a)(x))
    out_shape, out_specs = [], []
    for kind, shape, dtype in outs:
        out_specs.append(pl.BlockSpec(memory_space=kinds[kind]))
        out_shape.append((pltpu.VMEM if kind == "vmem" else pltpu.HBM)(shape, dtype))
    return pl.pallas_call(
        body,
        in_specs=in_specs,
        out_specs=out_specs,
        out_shape=out_shape,
        scratch_shapes=list(scratch),
        compiler_params=pltpu.CompilerParams(vmem_limit_bytes=VMEM_LIMIT),
        cost_estimate=pl.CostEstimate(flops=flops, bytes_accessed=moved, transcendentals=0),
        name=name,
    )(*args)


STATE = (HEADS, SIZE, SIZE)
ROWS = (HEADS, LENGTH, SIZE)
WHOLE = (LENGTH, HEADS, SIZE)


def by_head(wide, part):
    return [wide[pl.ds(h + part * CHUNK * HEADS, CHUNK, stride=HEADS), :] for h in range(HEADS)]


def spread(wide, block, part):
    wide[pl.ds(part * CHUNK * HEADS, CHUNK * HEADS), :] = block.astype(F32).reshape(CHUNK * HEADS, SIZE)


SPLIT = ((0, 2), (2, 6))


def fetch(pairs, sems):
    groups = []
    for n, (start, count) in enumerate(SPLIT):
        groups.append([])
        for i, (src, dst) in enumerate(pairs):
            part = pl.ds(start, count)
            c = pltpu.make_async_copy(src.at[part], dst.at[part], sems.at[n * len(pairs) + i])
            c.start()
            groups[-1].append(c)
    return groups


def await_head(groups, h):
    for n, (start, _) in enumerate(SPLIT):
        if h == start:
            wait_all(groups[n])


def put(src, dst, part, sem):
    c = pltpu.make_async_copy(src.at[part], dst.at[part], sem)
    c.start()
    return c


def fetch_rows(src, dst, sems, base=0):
    return [put(src, dst, pl.ds(p * CHUNK, CHUNK), sems.at[base + p]) for p in range(PARTS)]


def wait_all(copies):
    for c in copies:
        c.wait()


def dma(count):
    return pltpu.SemaphoreType.DMA((count,))


def key_kernel(slope_hbm, k_hbm, v_hbm, s_ref, kh_hbm, vh_hbm, slope_ref, kin, vin, kw, vw, kh, vh, sems, out_sems):
    first = pltpu.make_async_copy(slope_hbm, slope_ref, sems.at[2 * PARTS])
    first.start()
    k_copies = fetch_rows(k_hbm, kin, sems)
    v_copies = fetch_rows(v_hbm, vin, sems, PARTS)
    first.wait()
    rates = [rate_of(slope_ref, h) for h in range(HEADS)]
    writes = []
    for p in range(PARTS):
        rows = pl.ds(p * CHUNK, CHUNK)
        k_copies[p].wait()
        v_copies[p].wait()
        spread(kw, kin[rows], p)
        spread(vw, vin[rows], p)
        ks, vs = by_head(kw, p), by_head(vw, p)
        left = LENGTH - 1.0 - rows_of((CHUNK, SIZE), p * CHUNK)
        for h in range(HEADS):
            v = vs[h].astype(BF16)
            kh[h, rows, :] = ks[h].astype(BF16)
            vh[h, rows, :] = v
            part = dot((ks[h] * jnp.exp(-rates[h] * left)).astype(BF16), v, TN)
            s_ref[h] = part if p == 0 else s_ref[h] + part
        for i, (a, b) in enumerate(((kh, kh_hbm), (vh, vh_hbm))):
            writes.append(pltpu.make_async_copy(a.at[:, rows], b.at[:, rows], out_sems.at[2 * p + i]))
            writes[-1].start()
    wait_all(writes)


def key_states(slope, k, v):
    wide = pltpu.VMEM((LENGTH * HEADS, SIZE), F32)
    return call(
        key_kernel,
        "key_states",
        [("hbm", slope), ("hbm", k), ("hbm", v)],
        [("vmem", STATE, F32), ("hbm", ROWS, BF16), ("hbm", ROWS, BF16)],
        [
            pltpu.SMEM((HEADS,), jnp.int32),
            pltpu.VMEM(WHOLE, BF16),
            pltpu.VMEM(WHOLE, BF16),
            wide,
            wide,
            pltpu.VMEM(ROWS, BF16),
            pltpu.VMEM(ROWS, BF16),
            dma(2 * PARTS + 1),
            dma(2 * PARTS),
        ],
    )


def local_kernel(slope_ref, q_hbm, k_hbm, v_hbm, u_hbm, loc_hbm, qh_hbm, uh_hbm, wq_hbm, qin, uin, qw, uw, q, k, v, u, loc, wq, sems, in_sems, out_sems):
    q_copies = fetch_rows(q_hbm, qin, in_sems)
    copies = fetch(((k_hbm, k), (v_hbm, v)), sems)
    u_copies = fetch_rows(u_hbm, uin, in_sems, PARTS)
    wait_all(q_copies)
    writes = []
    for p in range(PARTS):
        rows = pl.ds(p * CHUNK, CHUNK)
        spread(qw, qin[rows], p)
        for h, block in enumerate(by_head(qw, p)):
            q[h, rows, :] = block.astype(BF16)
    writes.append(pltpu.make_async_copy(q, qh_hbm, out_sems.at[0]))
    writes[-1].start()
    done = rows_of((LENGTH, SIZE))
    for h in range(HEADS):
        await_head(copies, h)
        rate = rate_of(slope_ref, h)
        diag, off = masks(rate)
        q0, q1 = q[h, :256], q[h, 256:]
        k0, k1 = k[h, :256], k[h, 256:]
        v0, v1 = v[h, :256], v[h, 256:]
        a00 = (dot(q0, k0, NT) * diag).astype(BF16)
        a10 = (dot(q1, k0, NT) * off).astype(BF16)
        a11 = (dot(q1, k1, NT) * diag).astype(BF16)
        loc[h, :256] = dot(a00, v0, NN)
        loc[h, 256:] = dot(a10, v0, NN) + dot(a11, v1, NN)
        wq[h] = (q[h].astype(F32) * jnp.exp(-rate * done)).T.astype(BF16)
    writes.append(pltpu.make_async_copy(loc, loc_hbm, out_sems.at[1]))
    writes.append(pltpu.make_async_copy(wq, wq_hbm, out_sems.at[2]))
    writes[-1].start()
    writes[-2].start()
    wait_all(u_copies)
    for p in range(PARTS):
        rows = pl.ds(p * CHUNK, CHUNK)
        spread(uw, uin[rows], p)
        for h, block in enumerate(by_head(uw, p)):
            u[h, rows, :] = block.astype(BF16)
    writes.append(pltpu.make_async_copy(u, uh_hbm, out_sems.at[3]))
    writes[-1].start()
    wait_all(writes)


def local_part(slope, q, k, v, u):
    rows, wide = pltpu.VMEM(ROWS, BF16), pltpu.VMEM((LENGTH * HEADS, SIZE), F32)
    whole = pltpu.VMEM(WHOLE, BF16)
    turned = (HEADS, SIZE, LENGTH)
    return call(
        local_kernel,
        "local_part",
        [("smem", slope), ("hbm", q), ("hbm", k), ("hbm", v), ("hbm", u)],
        [("hbm", ROWS, F32), ("hbm", ROWS, BF16), ("hbm", ROWS, BF16), ("hbm", turned, BF16)],
        [
            whole,
            whole,
            wide,
            wide,
            rows,
            rows,
            rows,
            rows,
            pltpu.VMEM(ROWS, F32),
            pltpu.VMEM(turned, BF16),
            dma(4),
            dma(2 * PARTS),
            dma(4),
        ],
        flops=2 * 10**9,
        moved=8 * 2**20,
    )


def prefix_kernel(reverse, slope_ref, z_ref, out_ref):
    head = lax.axis_index("ctx") // (BLOCKS // HEADS)
    decay = jnp.exp(-float(LENGTH) * rate_of(slope_ref, head))
    state = jnp.zeros((SLICE, SIZE), F32)
    for p in range(BLOCKS - 1, -1, -1) if reverse else range(BLOCKS):
        out_ref[p] = state
        state = decay * state + z_ref[p]


def prefix(slope, z, reverse):
    (out,) = call(
        functools.partial(prefix_kernel, reverse),
        "prefix",
        [("smem", slope), ("vmem", z)],
        [("vmem", (BLOCKS, SLICE, SIZE), F32)],
    )
    return out


def output_kernel(slope_ref, q_ref, u_ref, gain_ref, e_ref, loc_ref, o_ref, sums_ref, sq, dt, sums):
    done = rows_of((LENGTH, SIZE), 1)
    for h in range(HEADS):
        decay_in = jnp.exp(-rate_of(slope_ref, h) * done)
        out = loc_ref[h] + decay_in * dot(q_ref[h], e_ref[h].astype(BF16), NN)
        o_ref[h] = out
        scaled = gain_ref[h : h + 1, :] * u_ref[h].astype(F32)
        sq[...] = out * out if h == 0 else sq[...] + out * out
        dt[...] = out * scaled if h == 0 else dt[...] + out * scaled
    for b in range(4):
        rows = slice(b * 128, (b + 1) * 128)
        sums[b : b + 1, :] = jnp.sum(sq[rows, :].T, axis=0, keepdims=True)
        sums[4 + b : 5 + b, :] = jnp.sum(dt[rows, :].T, axis=0, keepdims=True)
    for i in range(sums_ref.shape[0]):
        sums_ref[i] = sums[...]


def outputs(slope, q, u, gain, e, loc, peers):
    return call(
        output_kernel,
        "outputs",
        [("smem", slope), ("vmem", q), ("vmem", u), ("vmem", gain), ("vmem", e), ("vmem", loc)],
        [("vmem", ROWS, F32), ("vmem", (peers, 8, SIZE), F32)],
        [pltpu.VMEM((LENGTH, SIZE), F32), pltpu.VMEM((LENGTH, SIZE), F32), pltpu.VMEM((8, SIZE), F32)],
    )


def grad_kernel(sums_ref, wq_ref, u_ref, gain_ref, o_ref, g_hbm, s_ref, g, sems):
    peers = sums_ref.shape[0]
    features = float(peers * HEADS * SIZE)
    sums = sums_ref[0]
    for i in range(1, peers):
        sums = sums + sums_ref[i]
    root = lax.rsqrt(sums[0:4, :] * (1.0 / features) + 1e-06)
    factor = root * root * root * sums[4:8, :] * (1.0 / features)
    writes = []
    for b in range(4):
        rows = pl.ds(b * 128, 128)
        inv = jnp.broadcast_to(root[b : b + 1, :], (128, 128)).T
        coef = jnp.broadcast_to(factor[b : b + 1, :], (128, 128)).T
        for h in range(HEADS):
            scaled = gain_ref[h : h + 1, :] * u_ref[h, rows, :].astype(F32)
            g[h, rows, :] = (inv * scaled - o_ref[h, rows, :] * coef).astype(BF16)
        writes.append(pltpu.make_async_copy(g.at[:, rows], g_hbm.at[:, rows], sems.at[b]))
        writes[-1].start()
    for h in range(HEADS):
        s_ref[h] = dot(wq_ref[h], g[h], NN)
    wait_all(writes)


def grads(sums, wq, u, gain, o):
    return call(
        grad_kernel,
        "grads",
        [("vmem", sums), ("vmem", wq), ("vmem", u), ("vmem", gain), ("vmem", o)],
        [("hbm", ROWS, BF16), ("vmem", STATE, F32)],
        [pltpu.VMEM(ROWS, BF16), dma(4)],
    )


def query_kernel(slope_ref, g_hbm, k_hbm, v_hbm, e_hbm, out_hbm, g, k, v, e, wide, block, sems, e_sems, out_sems):
    e_copy = pltpu.make_async_copy(e_hbm, e, e_sems.at[0])
    e_copy.start()
    copies = fetch(((g_hbm, g), (k_hbm, k), (v_hbm, v)), sems)
    e_copy.wait()
    done = rows_of((LENGTH, SIZE), 1)
    for h in range(HEADS):
        await_head(copies, h)
        rate = rate_of(slope_ref, h)
        diag, off = masks(rate)
        g0, g1 = g[h, :256], g[h, 256:]
        k0, k1 = k[h, :256], k[h, 256:]
        v0, v1 = v[h, :256], v[h, 256:]
        b00 = (dot(g0, v0, NT) * diag).astype(BF16)
        b10 = (dot(g1, v0, NT) * off).astype(BF16)
        b11 = (dot(g1, v1, NT) * diag).astype(BF16)
        carried = jnp.exp(-rate * done) * dot(g[h], e[h].astype(BF16), NT)
        wide[pl.ds(h, 256, stride=HEADS), :] = dot(b00, k0, NN) + carried[:256]
        wide[pl.ds(h + 256 * HEADS, 256, stride=HEADS), :] = (
            dot(b10, k0, NN) + dot(b11, k1, NN) + carried[256:]
        )
    writes = []
    for p in range(PARTS):
        rows = pl.ds(p * CHUNK, CHUNK)
        block[rows] = wide[pl.ds(p * CHUNK * HEADS, CHUNK * HEADS), :].reshape(CHUNK, HEADS, SIZE).astype(BF16)
        writes.append(pltpu.make_async_copy(block.at[rows], out_hbm.at[rows], out_sems.at[p]))
        writes[-1].start()
    wait_all(writes)


def grad_query(slope, g, k, v, e):
    rows = pltpu.VMEM(ROWS, BF16)
    (out,) = call(
        query_kernel,
        "grad_query",
        [("smem", slope), ("hbm", g), ("hbm", k), ("hbm", v), ("any", e)],
        [("hbm", WHOLE, BF16)],
        [
            rows,
            rows,
            rows,
            pltpu.VMEM(STATE, F32),
            pltpu.VMEM((LENGTH * HEADS, SIZE), F32),
            pltpu.VMEM(WHOLE, BF16),
            dma(6),
            dma(1),
            dma(PARTS),
        ],
        flops=3 * 10**9,
        moved=5 * 2**20,
    )
    return out


def back_kernel(slope_ref, k_hbm, v_hbm, q_hbm, g_hbm, kl_hbm, vl_hbm, k, v, q, g, kl, vl, sems, out_sems):
    copies = fetch(((k_hbm, k), (q_hbm, q), (g_hbm, g), (v_hbm, v)), sems)
    writes = []
    for h in range(HEADS):
        await_head(copies, h)
        diag, off = masks(rate_of(slope_ref, h), True)
        k0, k1 = k[h, :256], k[h, 256:]
        v0, v1 = v[h, :256], v[h, 256:]
        q0, q1 = q[h, :256], q[h, 256:]
        g0, g1 = g[h, :256], g[h, 256:]
        for a0, a1, b0, b1, c0, c1, to in (
            (k0, k1, q0, q1, g0, g1, vl),
            (v0, v1, g0, g1, q0, q1, kl),
        ):
            t00 = (dot(a0, b0, NT) * diag).astype(BF16)
            t01 = (dot(a0, b1, NT) * off).astype(BF16)
            t11 = (dot(a1, b1, NT) * diag).astype(BF16)
            to[h, :256] = (dot(t00, c0, NN) + dot(t01, c1, NN)).astype(BF16)
            to[h, 256:] = dot(t11, c1, NN).astype(BF16)
        if h % 4 == 3:
            part = pl.ds(h - 3, 4)
            writes.append(put(vl, vl_hbm, part, out_sems.at[h // 4]))
            writes.append(put(kl, kl_hbm, part, out_sems.at[2 + h // 4]))
    wait_all(writes)


def back(slope, k, v, q, g):
    rows = pltpu.VMEM(ROWS, BF16)
    return call(
        back_kernel,
        "back",
        [("smem", slope), ("hbm", k), ("hbm", v), ("hbm", q), ("hbm", g)],
        [("hbm", ROWS, BF16), ("hbm", ROWS, BF16)],
        [rows, rows, rows, rows, rows, rows, dma(8), dma(4)],
        flops=4 * 10**9,
        moved=8 * 2**20,
    )


def finish_kernel(slope_ref, k_hbm, v_hbm, kl_hbm, vl_hbm, l_ref, gk_hbm, gv_hbm, k, v, kl, vl, wk, wv, gk, gv, sems, out_sems):
    copies = []
    for p in range(2):
        rows = pl.ds(p * 256, 256)
        group = []
        for i, (a, b) in enumerate(((k_hbm, k), (v_hbm, v), (kl_hbm, kl), (vl_hbm, vl))):
            group.append(pltpu.make_async_copy(a.at[:, rows], b.at[:, rows], sems.at[4 * p + i]))
            group[-1].start()
        copies.append(group)
    rates = [rate_of(slope_ref, h) for h in range(HEADS)]
    writes = []
    for p in range(2):
        rows = pl.ds(p * 256, 256)
        wait_all(copies[p])
        left = LENGTH - rows_of((256, SIZE), p * 256)
        flat = pl.ds(p * 256 * HEADS, 256 * HEADS)
        for h in range(HEADS):
            strided = pl.ds(h + p * 256 * HEADS, 256, stride=HEADS)
            decay = jnp.exp(-rates[h] * left)
            state = l_ref[h].astype(BF16)
            wk[strided, :] = kl[h, rows, :].astype(F32) + decay * dot(v[h, rows, :], state, NT)
            wv[strided, :] = vl[h, rows, :].astype(F32) + decay * dot(k[h, rows, :], state, NN)
        gk[rows] = wk[flat, :].reshape(256, HEADS, SIZE).astype(BF16)
        gv[rows] = wv[flat, :].reshape(256, HEADS, SIZE).astype(BF16)
        for i, (a, b) in enumerate(((gk, gk_hbm), (gv, gv_hbm))):
            writes.append(pltpu.make_async_copy(a.at[rows], b.at[rows], out_sems.at[2 * p + i]))
            writes[-1].start()
    wait_all(writes)


def finish(slope, k, v, kl, vl, l):
    wide = pltpu.VMEM((LENGTH * HEADS, SIZE), F32)
    rows, block = pltpu.VMEM(ROWS, BF16), pltpu.VMEM(WHOLE, BF16)
    return call(
        finish_kernel,
        "finish",
        [("smem", slope), ("hbm", k), ("hbm", v), ("hbm", kl), ("hbm", vl), ("vmem", l)],
        [("hbm", WHOLE, BF16), ("hbm", WHOLE, BF16)],
        [rows, rows, rows, rows, wide, wide, block, block, dma(8), dma(4)],
    )


def all_to_all(a):
    return lax.all_to_all(a.reshape(BLOCKS, SLICE, SIZE), "ctx", 0, 0, tiled=True)


def on_device(queries, key_rows, value_rows, upstream, norm_gain, slope_index):
    slope = slope_index

    states, kh, vh = key_states(slope, key_rows, value_rows)
    moved = all_to_all(states)
    loc, qh, uh, wq = local_part(slope, queries, kh, vh, upstream)
    moved, loc, qh, uh, wq = lax.optimization_barrier((moved, loc, qh, uh, wq))
    entering = all_to_all(prefix(slope, moved, False)).reshape(STATE)

    peers = lax.axis_size("head")
    out, sums = outputs(slope, qh, uh, norm_gain, entering, loc, peers)
    sums = lax.all_to_all(sums, "head", 0, 0, tiled=True)
    g, states = grads(sums, wq, uh, norm_gain, out)

    moved = all_to_all(states)
    gk_local, gv_local = back(slope, kh, vh, qh, g)
    moved, gk_local, gv_local = lax.optimization_barrier((moved, gk_local, gv_local))
    leaving = all_to_all(prefix(slope, moved, True)).reshape(STATE)
    gq = grad_query(slope, g, kh, vh, entering)
    leaving, gq = lax.optimization_barrier((leaving, gq))
    gk, gv = finish(slope, kh, vh, gk_local, gv_local, leaving)
    return gq, gk, gv


def solution(mesh):
    rows = P("ctx", "head", None)
    return jax.shard_map(
        on_device,
        mesh=mesh,
        in_specs=(rows, rows, rows, rows, P("head", None), P("head")),
        out_specs=(rows, rows, rows),
        check_vma=False,
    )
```

time: 284 us -> 101 us (0.36)
  waiting for transfers between devices: 102 us -> 15.6 us
  blocking collectives: 80.1 us -> 30.1 us
  other arithmetic: 43.9 us -> 0 us
  Pallas kernels: 0 us -> 34 us
  matrix products: 28.2 us -> 0 us
  starting transfers between devices: 0.08 us -> 18 us
  between operations: 15 us -> 0.92 us
  local copies, waits for them, and re-layouts: 11.4 us -> 1.61 us
    all_gather x2 -> x0, waiting for transfers between devices: 102 us -> none  [prefix(): gathered = jax.tree.map(lambda a: lax.all_gather(a, axis), part)]
    unnamed x1 -> x0, blocking collectives: 66.2 us -> none
    add x31 -> x0, other arithmetic: 37 us -> none  [combine_states(): return (decay_a * decay_b, decay_b[:, None, None] * state_a + state_b)]
    pallas_call x0 -> x9, Pallas kernels: none -> 34 us  [call(): pl.pallas_call(body, in_specs=in_specs, out_specs=out_specs, out_shape=ou...]
    all_to_all x0 -> x2, blocking collectives: none -> 30.1 us  [the longest x1 15.2 us: all_to_all(): lax.all_to_all(a.reshape(BLOCKS, SLICE, SIZE), 'ctx', 0, 0, tiled=True)]
    dot_general x12 -> x0, matrix products: 28.2 us -> none  [the longest x1 4.1 us: on_device(): jnp.einsum('hid,hde->hie', q_heads, entering_b, preferred_element_type=jn...]
    all_to_all x0 -> x3, starting transfers between devices: none -> 18 us  [all_to_all(): lax.all_to_all(a.reshape(BLOCKS, SLICE, SIZE), 'ctx', 0, 0, tiled=True)]
    all_to_all x0 -> x3, waiting for transfers between devices: none -> 15.6 us  [all_to_all(): lax.all_to_all(a.reshape(BLOCKS, SLICE, SIZE), 'ctx', 0, 0, tiled=True)]
  transfers between devices with their start and end apart: 2 -> 3, of which waited for: 2 -> 3; matrix products, arithmetic and copies ran while one was open for 9% -> 0% of each run, Pallas kernels for 0% -> 19%
where the time goes in v2:
time: 101 us; the launch traced here: 100 us
  Pallas kernels  34 us (34%)
  blocking collectives  30.1 us (30%)
  starting transfers between devices  18 us (18%)
  waiting for transfers between devices  15.6 us (15%)
  local copies, waits for them, and re-layouts  1.61 us (2%)
    pallas_call x9, Pallas kernels, call(): pl.pallas_call(body, in_specs=in_specs, out_specs=out_specs, out_shape=ou...  34 us
    all_to_all x3, starting transfers between devices, all_to_all(): lax.all_to_all(a.reshape(BLOCKS, SLICE, SIZE), 'ctx', 0, 0, tiled=True)  18 us
    all_to_all x3, waiting for transfers between devices, all_to_all(): lax.all_to_all(a.reshape(BLOCKS, SLICE, SIZE), 'ctx', 0, 0, tiled=True)  15.6 us
    all_to_all x1, blocking collectives, all_to_all(): lax.all_to_all(a.reshape(BLOCKS, SLICE, SIZE), 'ctx', 0, 0, tiled=True)  15.2 us
    all_to_all x1, blocking collectives, on_device(): sums = lax.all_to_all(sums, 'head', 0, 0, tiled=True)  14.9 us
  transfers between devices with their start and end apart: 3, of which 3 were waited for; matrix products, arithmetic and copies ran while one was open for 0% of the time, Pallas kernels for 19%

profile of v2, /device:TPU:1, one launch (start us, length us, event | category | flops | bytes accessed | tf_op | source)
XLA Modules:
  0.0 100.3 jit_solution(11131017707170897366)
XLA Ops:
  0.6 0.0 copy-start.5
  0.6 4.2 %key_states.1 = (f32[8,128,128]{2,1,0:T(8,128)}, bf16[8,512,128]{2,1,0:T(8,128)(2,1)}, bf16[8,512,128]{2,1,0:T(8,128)(2,1)}) custom-call(s32[8]{0:T(128)} %slope_ref.13, bf16[512,8,128]{2,1,0:T(8,128)(2,1)} %k_hbm.1, bf16[512,8,128]{2,1,0:T(8,128)(2,1)} %v_hbm.1), custom_call_target="tpu_custom_call" | custom-call | tf_op jit(solution)/shard_map/key_states/pallas_call | solution.py:68
  4.8 8.6 %all-to-all-start = ((f32[32,32,128]{2,1,0:T(8,128)}), f32[32,32,128]{2,1,0:T(8,128)S(1)}, u32[]{:S(2)}, u32[]{:S(2)}) async-start(f32[32,32,128]{2,1,0:T(8,128)} %bitcast), calls=%async_computation | async-start | bytes 1048576 | tf_op jit(solution)/shard_map/all_to_all | solution.py:468
  13.4 0.0 copy-done.5
  13.4 6.9 %local_part.1 = (f32[8,512,128]{2,1,0:T(8,128)}, bf16[8,512,128]{2,1,0:T(8,128)(2,1)}, bf16[8,512,128]{2,1,0:T(8,128)(2,1)}, bf16[8,128,512]{2,1,0:T(8,128)(2,1)}) custom-call(s32[8]{0:T(128)S(1)} %copy-done.5, bf16[512,8,128]{2,1,0:T(8,128)(2,1)} %q_hbm.1, bf16[8,512,128]{2,1,0:T(8,128)(2,1)} %get-tuple-element.29.k_hbm, ...), custom_call_target="tpu_custom_call" | custom-call | flops 2000000000 | bytes 8388608 | tf_op jit(solution)/shard_map/local_part/pallas_call | solution.py:68
  20.4 0.0 copy-start
  20.4 0.0 copy-start.3
  20.4 0.0 copy-start.4
  20.4 4.6 %all-to-all-done.z_ref = f32[32,32,128]{2,1,0:T(8,128)S(1)} async-done(((f32[32,32,128]{2,1,0:T(8,128)}), f32[32,32,128]{2,1,0:T(8,128)S(1)}, u32[]{:S(2)}, u32[]{:S(2)}) %all-to-all-start) | async-done | bytes 524320 | tf_op jit(solution)/shard_map/all_to_all | solution.py:468
  25.0 0.6 prefix.2
  25.6 15.2 %all_to_all.25 = f32[32,32,128]{2,1,0:T(8,128)S(1)} all-to-all(f32[32,32,128]{2,1,0:T(8,128)S(1)} %prefix.2), channel_id=1, replica_groups=mesh['ctx'=32,'head'=8] {'ctx'}, dimensions={0} | all-to-all | bytes 1048576 | tf_op jit(solution)/shard_map/all_to_all | solution.py:468
  40.9 0.0 copy-done
  40.9 0.0 copy-done.3
  40.9 0.0 copy-done.4
  40.9 0.0 copy-start.1
  40.9 1.6 %copy-done.1 = f32[8,512,128]{2,1,0:T(8,128)S(1)} copy-done((f32[8,512,128]{2,1,0:T(8,128)S(1)}, f32[8,512,128]{2,1,0:T(8,128)}, u32[]{:S(2)}) %copy-start.1) | copy-done | bytes 2097176
  42.5 0.0 copy-start.2
  42.5 1.6 %outputs.1 = (f32[8,512,128]{2,1,0:T(8,128)S(1)}, f32[8,8,128]{2,1,0:T(8,128)S(1)}) custom-call(s32[8]{0:T(128)S(1)} %copy-done.5, bf16[8,512,128]{2,1,0:T(8,128)(2,1)S(1)} %copy-done.3, bf16[8,512,128]{2,1,0:T(8,128)(2,1)S(1)} %copy-done, f32[8,128]{1,0:T(8,128)S(1)} %copy-done.4, f32[8,128,128]{2,1,0:T(8,128)S(1)} %bitcast.5, f32[8,512,128]{2,1,0:T(8,128)S(1)} %copy-done.1), custom_call_target="tpu_custom_call" | custom-call | tf_op jit(solution)/shard_map/outputs/pallas_call | solution.py:68
  44.1 14.9 %all_to_all.26.sums_ref = f32[8,8,128]{2,1,0:T(8,128)S(1)} all-to-all(f32[8,8,128]{2,1,0:T(8,128)S(1)} %get-tuple-element.39), channel_id=1, replica_groups=mesh['ctx'=32,'head'=8] {'head'}, dimensions={0} | all-to-all | bytes 65536 | tf_op jit(solution)/shard_map/all_to_all | solution.py:482
  58.9 0.0 copy-done.2
  59.0 2.0 %grads.1 = (bf16[8,512,128]{2,1,0:T(8,128)(2,1)}, f32[8,128,128]{2,1,0:T(8,128)}) custom-call(f32[8,8,128]{2,1,0:T(8,128)S(1)} %all_to_all.26.sums_ref, bf16[8,128,512]{2,1,0:T(8,128)(2,1)S(1)} %copy-done.2, bf16[8,512,128]{2,1,0:T(8,128)(2,1)S(1)} %copy-done, f32[8,128]{1,0:T(8,128)S(1)} %copy-done.4, f32[8,512,128]{2,1,0:T(8,128)S(1)} %get-tuple-element.41.o_ref), custom_call_target="tpu_custom_call" | custom-call | tf_op jit(solution)/shard_map/grads/pallas_call | solution.py:68
  61.0 5.4 %all-to-all-start.3 = ((f32[32,32,128]{2,1,0:T(8,128)}), f32[32,32,128]{2,1,0:T(8,128)S(1)}, u32[]{:S(2)}, u32[]{:S(2)}) async-start(f32[32,32,128]{2,1,0:T(8,128)} %bitcast.2), calls=%async_computation.3 | async-start | bytes 1048576 | tf_op jit(solution)/shard_map/all_to_all | solution.py:468
  66.4 7.1 %back.1 = (bf16[8,512,128]{2,1,0:T(8,128)(2,1)}, bf16[8,512,128]{2,1,0:T(8,128)(2,1)}) custom-call(s32[8]{0:T(128)S(1)} %copy-done.5, bf16[8,512,128]{2,1,0:T(8,128)(2,1)} %get-tuple-element.29.k_hbm, bf16[8,512,128]{2,1,0:T(8,128)(2,1)} %get-tuple-element.30.v_hbm, bf16[8,512,128]{2,1,0:T(8,128)(2,1)} %get-tuple-element.35.q_ref.q_hbm, ...), custom_call_target="tpu_custom_call" | custom-call | flops 4000000000 | bytes 8388608 | tf_op jit(solution)/shard_map/back/pallas_call | solution.py:68
  73.5 4.6 %all-to-all-done.3.z_ref = f32[32,32,128]{2,1,0:T(8,128)S(1)} async-done(((f32[32,32,128]{2,1,0:T(8,128)}), f32[32,32,128]{2,1,0:T(8,128)S(1)}, u32[]{:S(2)}, u32[]{:S(2)}) %all-to-all-start.3) | async-done | bytes 524320 | tf_op jit(solution)/shard_map/all_to_all | solution.py:468
  78.1 1.4 %prefix.3 = f32[32,32,128]{2,1,0:T(8,128)} custom-call(s32[8]{0:T(128)S(1)} %copy-done.5, f32[32,32,128]{2,1,0:T(8,128)S(1)} %all-to-all-done.3.z_ref), custom_call_target="tpu_custom_call" | custom-call | tf_op jit(solution)/shard_map/prefix/pallas_call | solution.py:68
  79.5 4.0 %all-to-all-start.4 = ((f32[32,32,128]{2,1,0:T(8,128)}), f32[32,32,128]{2,1,0:T(8,128)S(1)}, u32[]{:S(2)}, u32[]{:S(2)}) async-start(f32[32,32,128]{2,1,0:T(8,128)} %prefix.3), calls=%async_computation.4 | async-start | bytes 1048576 | tf_op jit(solution)/shard_map/all_to_all | solution.py:468
  83.5 5.1 %grad_query.1 = bf16[512,8,128]{2,1,0:T(8,128)(2,1)} custom-call(s32[8]{0:T(128)S(1)} %copy-done.5, bf16[8,512,128]{2,1,0:T(8,128)(2,1)} %get-tuple-element.43.g_hbm, bf16[8,512,128]{2,1,0:T(8,128)(2,1)} %get-tuple-element.29.k_hbm, bf16[8,512,128]{2,1,0:T(8,128)(2,1)} %get-tuple-element.30.v_hbm, f32[8,128,128]{2,1,0:T(8,128)S(1)} %bitcast.6), custom_call_target="tpu_custom_call" | custom-call | flops 3000000000 | bytes 5242880 | tf_op jit(solution)/shard_map/grad_query/pallas_call | solution.py:68
  88.7 6.5 %all-to-all-done.4 = f32[32,32,128]{2,1,0:T(8,128)S(1)} async-done(((f32[32,32,128]{2,1,0:T(8,128)}), f32[32,32,128]{2,1,0:T(8,128)S(1)}, u32[]{:S(2)}, u32[]{:S(2)}) %all-to-all-start.4) | async-done | bytes 524320 | tf_op jit(solution)/shard_map/all_to_all | solution.py:468
  95.2 4.9 %finish.1 = (bf16[512,8,128]{2,1,0:T(8,128)(2,1)}, bf16[512,8,128]{2,1,0:T(8,128)(2,1)}) custom-call(s32[8]{0:T(128)S(1)} %copy-done.5, bf16[8,512,128]{2,1,0:T(8,128)(2,1)} %get-tuple-element.29.k_hbm, bf16[8,512,128]{2,1,0:T(8,128)(2,1)} %get-tuple-element.30.v_hbm, bf16[8,512,128]{2,1,0:T(8,128)(2,1)} %get-tuple-element.48.kl_hbm, ...), custom_call_target="tpu_custom_call" | custom-call | tf_op jit(solution)/shard_map/finish/pallas_call | solution.py:68
Async XLA Ops:
  0.6 12.8 %copy-start.5 = (s32[8]{0:T(128)S(1)}, s32[8]{0:T(128)}, u32[]{:S(2)}) copy-start(s32[8]{0:T(128)} %slope_ref.13) | copy-start | bytes 100
  4.8 20.2 %all-to-all-start = ((f32[32,32,128]{2,1,0:T(8,128)}), f32[32,32,128]{2,1,0:T(8,128)S(1)}, u32[]{:S(2)}, u32[]{:S(2)}) async-start(f32[32,32,128]{2,1,0:T(8,128)} %bitcast), calls=%async_computation | async-start | bytes 1048576 | tf_op jit(solution)/shard_map/all_to_all | solution.py:468
  20.4 20.5 %copy-start = (bf16[8,512,128]{2,1,0:T(8,128)(2,1)S(1)}, bf16[8,512,128]{2,1,0:T(8,128)(2,1)}, u32[]{:S(2)}) copy-start(bf16[8,512,128]{2,1,0:T(8,128)(2,1)} %get-tuple-element.36.u_ref) | copy-start | bytes 3145732
  20.4 20.4 %copy-start.3 = (bf16[8,512,128]{2,1,0:T(8,128)(2,1)S(1)}, bf16[8,512,128]{2,1,0:T(8,128)(2,1)}, u32[]{:S(2)}) copy-start(bf16[8,512,128]{2,1,0:T(8,128)(2,1)} %get-tuple-element.35.q_ref.q_hbm) | copy-start | bytes 3145732
  20.4 20.4 %copy-start.4 = (f32[8,128]{1,0:T(8,128)S(1)}, f32[8,128]{1,0:T(8,128)}, u32[]{:S(2)}) copy-start(f32[8,128]{1,0:T(8,128)} %gain_ref.3) | copy-start | bytes 12292
  40.9 1.6 %copy-start.1 = (f32[8,512,128]{2,1,0:T(8,128)S(1)}, f32[8,512,128]{2,1,0:T(8,128)}, u32[]{:S(2)}) copy-start(f32[8,512,128]{2,1,0:T(8,128)} %get-tuple-element.38.loc_ref) | copy-start | bytes 6291460
  42.5 16.5 %copy-start.2 = (bf16[8,128,512]{2,1,0:T(8,128)(2,1)S(1)}, bf16[8,128,512]{2,1,0:T(8,128)(2,1)}, u32[]{:S(2)}) copy-start(bf16[8,128,512]{2,1,0:T(8,128)(2,1)} %get-tuple-element.40.wq_ref) | copy-start | bytes 3145732
  61.0 17.1 %all-to-all-start.3 = ((f32[32,32,128]{2,1,0:T(8,128)}), f32[32,32,128]{2,1,0:T(8,128)S(1)}, u32[]{:S(2)}, u32[]{:S(2)}) async-start(f32[32,32,128]{2,1,0:T(8,128)} %bitcast.2), calls=%async_computation.3 | async-start | bytes 1048576 | tf_op jit(solution)/shard_map/all_to_all | solution.py:468
  79.5 15.7 %all-to-all-start.4 = ((f32[32,32,128]{2,1,0:T(8,128)}), f32[32,32,128]{2,1,0:T(8,128)S(1)}, u32[]{:S(2)}, u32[]{:S(2)}) async-start(f32[32,32,128]{2,1,0:T(8,128)} %prefix.3), calls=%async_computation.4 | async-start | bytes 1048576 | tf_op jit(solution)/shard_map/all_to_all | solution.py:468

commit v3 on v2

--- a/solution.py
+++ b/solution.py
@@ -18,7 +18,7 @@
 SLICE = HEADS * SIZE // BLOCKS
 CHUNK = 128
 PARTS = LENGTH // CHUNK
-VMEM_LIMIT = 24 * 1024 * 1024
+VMEM_LIMIT = 32 * 1024 * 1024
 
 NN = ((1,), (0,))
 NT = ((1,), (1,))
@@ -130,7 +130,7 @@
     return pltpu.SemaphoreType.DMA((count,))
 
 
-def key_kernel(slope_hbm, k_hbm, v_hbm, s_ref, kh_hbm, vh_hbm, slope_ref, kin, vin, kw, vw, kh, vh, sems, out_sems):
+def key_kernel(slope_hbm, k_hbm, v_hbm, s_hbm, slope_ref, kin, vin, kw, vw, s, sems, out_sems):
     first = pltpu.make_async_copy(slope_hbm, slope_ref, sems.at[2 * PARTS])
     first.start()
     k_copies = fetch_rows(k_hbm, kin, sems)
@@ -147,54 +147,49 @@
         ks, vs = by_head(kw, p), by_head(vw, p)
         left = LENGTH - 1.0 - rows_of((CHUNK, SIZE), p * CHUNK)
         for h in range(HEADS):
-            v = vs[h].astype(BF16)
-            kh[h, rows, :] = ks[h].astype(BF16)
-            vh[h, rows, :] = v
-            part = dot((ks[h] * jnp.exp(-rates[h] * left)).astype(BF16), v, TN)
-            s_ref[h] = part if p == 0 else s_ref[h] + part
-        for i, (a, b) in enumerate(((kh, kh_hbm), (vh, vh_hbm))):
-            writes.append(pltpu.make_async_copy(a.at[:, rows], b.at[:, rows], out_sems.at[2 * p + i]))
-            writes[-1].start()
+            weighted = (ks[h] * jnp.exp(-rates[h] * left)).astype(BF16)
+            part = dot(weighted, vs[h].astype(BF16), TN)
+            s[h] = part if p == 0 else s[h] + part
+            if p == PARTS - 1 and h % 4 == 3:
+                writes.append(put(s, s_hbm, pl.ds(h - 3, 4), out_sems.at[h // 4]))
     wait_all(writes)
 
 
 def key_states(slope, k, v):
-    wide = pltpu.VMEM((LENGTH * HEADS, SIZE), F32)
-    return call(
+    whole, wide = pltpu.VMEM(WHOLE, BF16), pltpu.VMEM((LENGTH * HEADS, SIZE), F32)
+    (out,) = call(
         key_kernel,
         "key_states",
         [("hbm", slope), ("hbm", k), ("hbm", v)],
-        [("vmem", STATE, F32), ("hbm", ROWS, BF16), ("hbm", ROWS, BF16)],
-        [
-            pltpu.SMEM((HEADS,), jnp.int32),
-            pltpu.VMEM(WHOLE, BF16),
-            pltpu.VMEM(WHOLE, BF16),
-            wide,
-            wide,
-            pltpu.VMEM(ROWS, BF16),
-            pltpu.VMEM(ROWS, BF16),
-            dma(2 * PARTS + 1),
-            dma(2 * PARTS),
-        ],
-    )
-
-
-def local_kernel(slope_ref, q_hbm, k_hbm, v_hbm, u_hbm, loc_hbm, qh_hbm, uh_hbm, wq_hbm, qin, uin, qw, uw, q, k, v, u, loc, wq, sems, in_sems, out_sems):
-    q_copies = fetch_rows(q_hbm, qin, in_sems)
-    copies = fetch(((k_hbm, k), (v_hbm, v)), sems)
-    u_copies = fetch_rows(u_hbm, uin, in_sems, PARTS)
-    wait_all(q_copies)
-    writes = []
-    for p in range(PARTS):
-        rows = pl.ds(p * CHUNK, CHUNK)
-        spread(qw, qin[rows], p)
-        for h, block in enumerate(by_head(qw, p)):
-            q[h, rows, :] = block.astype(BF16)
-    writes.append(pltpu.make_async_copy(q, qh_hbm, out_sems.at[0]))
-    writes[-1].start()
+        [("hbm", STATE, F32)],
+        [pltpu.SMEM((HEADS,), jnp.int32), whole, whole, wide, wide, pltpu.VMEM(STATE, F32), dma(2 * PARTS + 1), dma(2)],
+    )
+    return out
+
+
+def local_kernel(slope_ref, q_hbm, k_hbm, v_hbm, u_hbm, loc, qh_hbm, kh_hbm, vh_hbm, uh_hbm, wq_hbm, qin, kin, vin, uin, wide, q, k, v, u, wq, in_sems, out_sems):
+    sources = ((q_hbm, qin, q, qh_hbm), (k_hbm, kin, k, kh_hbm), (v_hbm, vin, v, vh_hbm), (u_hbm, uin, u, uh_hbm))
+    copies = [pltpu.make_async_copy(s[0], s[1], in_sems.at[i]) for i, s in enumerate(sources)]
+    for c in copies:
+        c.start()
+    writes = []
+
+    def turn(i):
+        _, near_by, turned, to = sources[i]
+        copies[i].wait()
+        for p in range(PARTS):
+            rows = pl.ds(p * CHUNK, CHUNK)
+            spread(wide.at[i], near_by[rows], p)
+            for h, block in enumerate(by_head(wide.at[i], p)):
+                turned[h, rows, :] = block.astype(BF16)
+        writes.append(pltpu.make_async_copy(turned, to, out_sems.at[i]))
+        writes[-1].start()
+
+    turn(0)
+    turn(1)
+    turn(2)
     done = rows_of((LENGTH, SIZE))
     for h in range(HEADS):
-        await_head(copies, h)
         rate = rate_of(slope_ref, h)
         diag, off = masks(rate)
         q0, q1 = q[h, :256], q[h, 256:]
@@ -206,78 +201,82 @@
         loc[h, :256] = dot(a00, v0, NN)
         loc[h, 256:] = dot(a10, v0, NN) + dot(a11, v1, NN)
         wq[h] = (q[h].astype(F32) * jnp.exp(-rate * done)).T.astype(BF16)
-    writes.append(pltpu.make_async_copy(loc, loc_hbm, out_sems.at[1]))
-    writes.append(pltpu.make_async_copy(wq, wq_hbm, out_sems.at[2]))
+    writes.append(pltpu.make_async_copy(wq, wq_hbm, out_sems.at[4]))
     writes[-1].start()
-    writes[-2].start()
-    wait_all(u_copies)
-    for p in range(PARTS):
-        rows = pl.ds(p * CHUNK, CHUNK)
-        spread(uw, uin[rows], p)
-        for h, block in enumerate(by_head(uw, p)):
-            u[h, rows, :] = block.astype(BF16)
-    writes.append(pltpu.make_async_copy(u, uh_hbm, out_sems.at[3]))
-    writes[-1].start()
+    turn(3)
     wait_all(writes)
 
 
 def local_part(slope, q, k, v, u):
-    rows, wide = pltpu.VMEM(ROWS, BF16), pltpu.VMEM((LENGTH * HEADS, SIZE), F32)
-    whole = pltpu.VMEM(WHOLE, BF16)
+    rows, whole = pltpu.VMEM(ROWS, BF16), pltpu.VMEM(WHOLE, BF16)
     turned = (HEADS, SIZE, LENGTH)
     return call(
         local_kernel,
         "local_part",
         [("smem", slope), ("hbm", q), ("hbm", k), ("hbm", v), ("hbm", u)],
-        [("hbm", ROWS, F32), ("hbm", ROWS, BF16), ("hbm", ROWS, BF16), ("hbm", turned, BF16)],
-        [
-            whole,
-            whole,
-            wide,
-            wide,
-            rows,
-            rows,
-            rows,
-            rows,
-            pltpu.VMEM(ROWS, F32),
-            pltpu.VMEM(turned, BF16),
-            dma(4),
-            dma(2 * PARTS),
-            dma(4),
-        ],
+        [("vmem", ROWS, F32)] + [("hbm", ROWS, BF16)] * 4 + [("hbm", turned, BF16)],
+        [whole] * 4
+        + [pltpu.VMEM((4, LENGTH * HEADS, SIZE), F32)]
+        + [rows] * 4
+        + [pltpu.VMEM(turned, BF16), dma(4), dma(5)],
         flops=2 * 10**9,
         moved=8 * 2**20,
     )
 
 
-def prefix_kernel(reverse, slope_ref, z_ref, out_ref):
+def prefix_kernel(reverse, slope_ref, z_ref, out_hbm, out, sems):
     head = lax.axis_index("ctx") // (BLOCKS // HEADS)
     decay = jnp.exp(-float(LENGTH) * rate_of(slope_ref, head))
     state = jnp.zeros((SLICE, SIZE), F32)
-    for p in range(BLOCKS - 1, -1, -1) if reverse else range(BLOCKS):
+    writes = []
+    for n in range(BLOCKS):
+        p = BLOCKS - 1 - n if reverse else n
+        out[p] = state
+        state = decay * state + z_ref[p]
+        if n % 8 == 7:
+            writes.append(put(out, out_hbm, pl.ds(p if reverse else p - 7, 8), sems.at[n // 8]))
+    wait_all(writes)
+
+
+def prefix_near_kernel(slope_ref, z_ref, out_ref):
+    head = lax.axis_index("ctx") // (BLOCKS // HEADS)
+    decay = jnp.exp(-float(LENGTH) * rate_of(slope_ref, head))
+    state = jnp.zeros((SLICE, SIZE), F32)
+    for p in range(BLOCKS):
         out_ref[p] = state
         state = decay * state + z_ref[p]
 
 
 def prefix(slope, z, reverse):
+    shape = (BLOCKS, SLICE, SIZE)
+    if not reverse:
+        return call(prefix_near_kernel, "prefix", [("smem", slope), ("vmem", z)], [("vmem", shape, F32)])[0]
     (out,) = call(
         functools.partial(prefix_kernel, reverse),
         "prefix",
         [("smem", slope), ("vmem", z)],
-        [("vmem", (BLOCKS, SLICE, SIZE), F32)],
+        [("hbm", shape, F32)],
+        [pltpu.VMEM(shape, F32), dma(4)],
     )
     return out
 
 
-def output_kernel(slope_ref, q_ref, u_ref, gain_ref, e_ref, loc_ref, o_ref, sums_ref, sq, dt, sums):
+def output_kernel(slope_ref, q_ref, u_ref, gain_ref, e_ref, loc, o_ref, sums_ref, sq, dt, sums):
     done = rows_of((LENGTH, SIZE), 1)
     for h in range(HEADS):
         decay_in = jnp.exp(-rate_of(slope_ref, h) * done)
-        out = loc_ref[h] + decay_in * dot(q_ref[h], e_ref[h].astype(BF16), NN)
-        o_ref[h] = out
-        scaled = gain_ref[h : h + 1, :] * u_ref[h].astype(F32)
-        sq[...] = out * out if h == 0 else sq[...] + out * out
-        dt[...] = out * scaled if h == 0 else dt[...] + out * scaled
+        o_ref[h] = decay_in * dot(q_ref[h], e_ref[h].astype(BF16), NN)
+    for r in range(0, LENGTH, 32):
+        rows = pl.ds(r, 32)
+        square = product = None
+        for h in range(HEADS):
+            out = o_ref[h, rows, :] + loc[h, rows, :]
+            o_ref[h, rows, :] = out
+            scaled = gain_ref[h : h + 1, :] * u_ref[h, rows, :].astype(F32)
+            square = out * out if h == 0 else square + out * out
+            product = out * scaled if h == 0 else product + out * scaled
+        sq[rows, :] = square
+        dt[rows, :] = product
     for b in range(4):
         rows = slice(b * 128, (b + 1) * 128)
         sums[b : b + 1, :] = jnp.sum(sq[rows, :].T, axis=0, keepdims=True)
@@ -292,11 +291,15 @@
         "outputs",
         [("smem", slope), ("vmem", q), ("vmem", u), ("vmem", gain), ("vmem", e), ("vmem", loc)],
         [("vmem", ROWS, F32), ("vmem", (peers, 8, SIZE), F32)],
-        [pltpu.VMEM((LENGTH, SIZE), F32), pltpu.VMEM((LENGTH, SIZE), F32), pltpu.VMEM((8, SIZE), F32)],
-    )
-
-
-def grad_kernel(sums_ref, wq_ref, u_ref, gain_ref, o_ref, g_hbm, s_ref, g, sems):
+        [
+            pltpu.VMEM((LENGTH, SIZE), F32),
+            pltpu.VMEM((LENGTH, SIZE), F32),
+            pltpu.VMEM((8, SIZE), F32),
+        ],
+    )
+
+
+def grad_kernel(sums_ref, wq_ref, u_ref, gain_ref, o_ref, g_hbm, s_hbm, g, s, sems):
     peers = sums_ref.shape[0]
     features = float(peers * HEADS * SIZE)
     sums = sums_ref[0]
@@ -315,7 +318,9 @@
         writes.append(pltpu.make_async_copy(g.at[:, rows], g_hbm.at[:, rows], sems.at[b]))
         writes[-1].start()
     for h in range(HEADS):
-        s_ref[h] = dot(wq_ref[h], g[h], NN)
+        s[h] = dot(wq_ref[h], g[h], NN)
+        if h % 4 == 3:
+            writes.append(put(s, s_hbm, pl.ds(h - 3, 4), sems.at[4 + h // 4]))
     wait_all(writes)
 
 
@@ -324,8 +329,8 @@
         grad_kernel,
         "grads",
         [("vmem", sums), ("vmem", wq), ("vmem", u), ("vmem", gain), ("vmem", o)],
-        [("hbm", ROWS, BF16), ("vmem", STATE, F32)],
-        [pltpu.VMEM(ROWS, BF16), dma(4)],
+        [("hbm", ROWS, BF16), ("hbm", STATE, F32)],
+        [pltpu.VMEM(ROWS, BF16), pltpu.VMEM(STATE, F32), dma(6)],
     )
 
 
@@ -383,9 +388,8 @@
     return out
 
 
-def back_kernel(slope_ref, k_hbm, v_hbm, q_hbm, g_hbm, kl_hbm, vl_hbm, k, v, q, g, kl, vl, sems, out_sems):
+def back_kernel(slope_ref, k_hbm, v_hbm, q_hbm, g_hbm, kl, vl, k, v, q, g, sems):
     copies = fetch(((k_hbm, k), (q_hbm, q), (g_hbm, g), (v_hbm, v)), sems)
-    writes = []
     for h in range(HEADS):
         await_head(copies, h)
         diag, off = masks(rate_of(slope_ref, h), True)
@@ -402,11 +406,6 @@
             t11 = (dot(a1, b1, NT) * diag).astype(BF16)
             to[h, :256] = (dot(t00, c0, NN) + dot(t01, c1, NN)).astype(BF16)
             to[h, 256:] = dot(t11, c1, NN).astype(BF16)
-        if h % 4 == 3:
-            part = pl.ds(h - 3, 4)
-            writes.append(put(vl, vl_hbm, part, out_sems.at[h // 4]))
-            writes.append(put(kl, kl_hbm, part, out_sems.at[2 + h // 4]))
-    wait_all(writes)
 
 
 def back(slope, k, v, q, g):
@@ -415,40 +414,32 @@
         back_kernel,
         "back",
         [("smem", slope), ("hbm", k), ("hbm", v), ("hbm", q), ("hbm", g)],
-        [("hbm", ROWS, BF16), ("hbm", ROWS, BF16)],
-        [rows, rows, rows, rows, rows, rows, dma(8), dma(4)],
+        [("vmem", ROWS, BF16), ("vmem", ROWS, BF16)],
+        [rows, rows, rows, rows, dma(8)],
         flops=4 * 10**9,
         moved=8 * 2**20,
     )
 
 
-def finish_kernel(slope_ref, k_hbm, v_hbm, kl_hbm, vl_hbm, l_ref, gk_hbm, gv_hbm, k, v, kl, vl, wk, wv, gk, gv, sems, out_sems):
-    copies = []
-    for p in range(2):
-        rows = pl.ds(p * 256, 256)
-        group = []
-        for i, (a, b) in enumerate(((k_hbm, k), (v_hbm, v), (kl_hbm, kl), (vl_hbm, vl))):
-            group.append(pltpu.make_async_copy(a.at[:, rows], b.at[:, rows], sems.at[4 * p + i]))
-            group[-1].start()
-        copies.append(group)
+def finish_kernel(slope_ref, k_hbm, v_hbm, kl_ref, vl_ref, l_ref, gk_hbm, gv_hbm, k, v, wk, wv, gk, gv, sems, out_sems):
+    copies = [pltpu.make_async_copy(v_hbm, v, sems.at[0]), pltpu.make_async_copy(k_hbm, k, sems.at[1])]
+    for c in copies:
+        c.start()
     rates = [rate_of(slope_ref, h) for h in range(HEADS)]
-    writes = []
-    for p in range(2):
-        rows = pl.ds(p * 256, 256)
-        wait_all(copies[p])
-        left = LENGTH - rows_of((256, SIZE), p * 256)
-        flat = pl.ds(p * 256 * HEADS, 256 * HEADS)
+    left = LENGTH - rows_of((LENGTH, SIZE))
+    writes = []
+    for n, (x, add, wide, out, to, dims) in enumerate(
+        ((v, kl_ref, wk, gk, gk_hbm, NT), (k, vl_ref, wv, gv, gv_hbm, NN))
+    ):
+        copies[n].wait()
         for h in range(HEADS):
-            strided = pl.ds(h + p * 256 * HEADS, 256, stride=HEADS)
-            decay = jnp.exp(-rates[h] * left)
-            state = l_ref[h].astype(BF16)
-            wk[strided, :] = kl[h, rows, :].astype(F32) + decay * dot(v[h, rows, :], state, NT)
-            wv[strided, :] = vl[h, rows, :].astype(F32) + decay * dot(k[h, rows, :], state, NN)
-        gk[rows] = wk[flat, :].reshape(256, HEADS, SIZE).astype(BF16)
-        gv[rows] = wv[flat, :].reshape(256, HEADS, SIZE).astype(BF16)
-        for i, (a, b) in enumerate(((gk, gk_hbm), (gv, gv_hbm))):
-            writes.append(pltpu.make_async_copy(a.at[rows], b.at[rows], out_sems.at[2 * p + i]))
-            writes[-1].start()
+            moved = jnp.exp(-rates[h] * left) * dot(x[h], l_ref[h].astype(BF16), dims)
+            wide[pl.ds(h, LENGTH, stride=HEADS), :] = add[h].astype(F32) + moved
+        for p in range(2):
+            rows = pl.ds(p * 256, 256)
+            flat = pl.ds(p * 256 * HEADS, 256 * HEADS)
+            out[rows] = wide[flat, :].reshape(256, HEADS, SIZE).astype(BF16)
+            writes.append(put(out, to, rows, out_sems.at[2 * n + p]))
     wait_all(writes)
 
 
@@ -458,9 +449,9 @@
     return call(
         finish_kernel,
         "finish",
-        [("smem", slope), ("hbm", k), ("hbm", v), ("hbm", kl), ("hbm", vl), ("vmem", l)],
+        [("smem", slope), ("hbm", k), ("hbm", v), ("vmem", kl), ("vmem", vl), ("vmem", l)],
         [("hbm", WHOLE, BF16), ("hbm", WHOLE, BF16)],
-        [rows, rows, rows, rows, wide, wide, block, block, dma(8), dma(4)],
+        [rows, rows, wide, wide, block, block, dma(2), dma(4)],
     )
 
 
@@ -471,10 +462,10 @@
 def on_device(queries, key_rows, value_rows, upstream, norm_gain, slope_index):
     slope = slope_index
 
-    states, kh, vh = key_states(slope, key_rows, value_rows)
+    states = key_states(slope, key_rows, value_rows)
     moved = all_to_all(states)
-    loc, qh, uh, wq = local_part(slope, queries, kh, vh, upstream)
-    moved, loc, qh, uh, wq = lax.optimization_barrier((moved, loc, qh, uh, wq))
+    loc, qh, kh, vh, uh, wq = local_part(slope, queries, key_rows, value_rows, upstream)
+    moved, loc, qh, kh, vh, uh, wq = lax.optimization_barrier((moved, loc, qh, kh, vh, uh, wq))
     entering = all_to_all(prefix(slope, moved, False)).reshape(STATE)
 
     peers = lax.axis_size("head")

time: 101 us -> 98.3 us (0.973)
  Pallas kernels: 34 us -> 32.1 us
  local copies, waits for them, and re-layouts: 1.61 us -> 0.03 us
    pallas_call x9, Pallas kernels: 34 us -> 32.1 us  [call(): pl.pallas_call(body, in_specs=in_specs, out_specs=out_specs, out_shape=ou...]
    unnamed x12 -> x14, local copies, waits for them, and re-layouts: 1.61 us -> 0.03 us
where the time goes in v3:
time: 98.3 us; the launch traced here: 97.7 us
  Pallas kernels  32.1 us (33%)
  blocking collectives  30.1 us (31%)
  starting transfers between devices  18.1 us (18%)
  waiting for transfers between devices  16.5 us (17%)
    pallas_call x9, Pallas kernels, call(): pl.pallas_call(body, in_specs=in_specs, out_specs=out_specs, out_shape=ou...  32.1 us
    all_to_all x3, starting transfers between devices, all_to_all(): lax.all_to_all(a.reshape(BLOCKS, SLICE, SIZE), 'ctx', 0, 0, tiled=True)  18.1 us
    all_to_all x3, waiting for transfers between devices, all_to_all(): lax.all_to_all(a.reshape(BLOCKS, SLICE, SIZE), 'ctx', 0, 0, tiled=True)  16.5 us
    all_to_all x1, blocking collectives, all_to_all(): lax.all_to_all(a.reshape(BLOCKS, SLICE, SIZE), 'ctx', 0, 0, tiled=True)  15.2 us
    all_to_all x1, blocking collectives, on_device(): sums = lax.all_to_all(sums, 'head', 0, 0, tiled=True)  14.9 us
  transfers between devices with their start and end apart: 3, of which 3 were waited for; matrix products, arithmetic and copies ran while one was open for 0% of the time, Pallas kernels for 19%

profile of v3, /device:TPU:1, one launch (start us, length us, event | category | flops | bytes accessed | tf_op | source)
XLA Modules:
  0.0 97.7 jit_solution(4169198692494823640)
XLA Ops:
  0.6 0.0 copy-start.6
  0.6 3.5 %key_states.1 = f32[8,128,128]{2,1,0:T(8,128)} custom-call(s32[8]{0:T(128)} %slope_ref.13, bf16[512,8,128]{2,1,0:T(8,128)(2,1)} %k_hbm.3, bf16[512,8,128]{2,1,0:T(8,128)(2,1)} %v_hbm.3), custom_call_target="tpu_custom_call" | custom-call | tf_op jit(solution)/shard_map/key_states/pallas_call | solution.py:68
  4.1 8.7 %all-to-all-start = ((f32[32,32,128]{2,1,0:T(8,128)}), f32[32,32,128]{2,1,0:T(8,128)}, u32[]{:S(2)}, u32[]{:S(2)}) async-start(f32[32,32,128]{2,1,0:T(8,128)} %bitcast.7), calls=%async_computation | async-start | bytes 1048576 | tf_op jit(solution)/shard_map/all_to_all | solution.py:459
  12.8 0.0 copy-done.6
  12.8 7.0 %local_part.1 = (f32[8,512,128]{2,1,0:T(8,128)S(1)}, bf16[8,512,128]{2,1,0:T(8,128)(2,1)}, bf16[8,512,128]{2,1,0:T(8,128)(2,1)}, bf16[8,512,128]{2,1,0:T(8,128)(...) custom-call(s32[8]{0:T(128)S(1)} %copy-done.6, bf16[512,8,128]{2,1,0:T(8,128)(2,1)} %q_hbm.1, ...), custom_call_target="tpu_custom_call" | custom-call | flops 2000000000 | bytes 8388608 | tf_op jit(solution)/shard_map/local_part/pallas_call | solution.py:68
  19.8 0.0 copy-start
  19.8 0.0 copy-start.5
  19.8 4.6 %all-to-all-done.z_ref = f32[32,32,128]{2,1,0:T(8,128)} async-done(((f32[32,32,128]{2,1,0:T(8,128)}), f32[32,32,128]{2,1,0:T(8,128)}, u32[]{:S(2)}, u32[]{:S(2)}) %all-to-all-start) | async-done | bytes 524320 | tf_op jit(solution)/shard_map/all_to_all | solution.py:459
  24.4 0.0 copy-start.4
  24.4 1.2 %prefix.2 = f32[32,32,128]{2,1,0:T(8,128)S(1)} custom-call(s32[8]{0:T(128)S(1)} %copy-done.6, f32[32,32,128]{2,1,0:T(8,128)} %all-to-all-done.z_ref), custom_call_target="tpu_custom_call" | custom-call | tf_op jit(solution)/shard_map/prefix/pallas_call | solution.py:68
  25.6 15.2 %all_to_all.25 = f32[32,32,128]{2,1,0:T(8,128)S(1)} all-to-all(f32[32,32,128]{2,1,0:T(8,128)S(1)} %prefix.2), channel_id=1, replica_groups=mesh['ctx'=32,'head'=8] {'ctx'}, dimensions={0} | all-to-all | bytes 1048576 | tf_op jit(solution)/shard_map/all_to_all | solution.py:459
  40.9 0.0 copy-start.1
  40.9 0.0 copy-done
  40.9 0.0 copy-done.5
  40.9 0.0 copy-done.4
  40.9 0.0 copy-start.3
  40.9 1.7 %outputs.1 = (f32[8,512,128]{2,1,0:T(8,128)S(1)}, f32[8,8,128]{2,1,0:T(8,128)S(1)}) custom-call(s32[8]{0:T(128)S(1)} %copy-done.6, bf16[8,512,128]{2,1,0:T(8,128)(2,1)S(1)} %copy-done.4, bf16[8,512,128]{2,1,0:T(8,128)(2,1)S(1)} %copy-done, f32[8,128]{1,0:T(8,128)S(1)} %copy-done.5, f32[8,128,128]{2,1,0:T(8,128)S(1)} %bitcast.5, ...), custom_call_target="tpu_custom_call" | custom-call | tf_op jit(solution)/shard_map/outputs/pallas_call | solution.py:68
  42.5 0.0 copy-done.1
  42.5 14.9 %all_to_all.26.sums_ref = f32[8,8,128]{2,1,0:T(8,128)S(1)} all-to-all(f32[8,8,128]{2,1,0:T(8,128)S(1)} %get-tuple-element.39), channel_id=1, replica_groups=mesh['ctx'=32,'head'=8] {'head'}, dimensions={0} | all-to-all | bytes 65536 | tf_op jit(solution)/shard_map/all_to_all | solution.py:473
  57.4 0.0 copy-done.3
  57.4 1.6 %grads.1 = (bf16[8,512,128]{2,1,0:T(8,128)(2,1)}, f32[8,128,128]{2,1,0:T(8,128)}) custom-call(f32[8,8,128]{2,1,0:T(8,128)S(1)} %all_to_all.26.sums_ref, bf16[8,128,512]{2,1,0:T(8,128)(2,1)S(1)} %copy-done.3, bf16[8,512,128]{2,1,0:T(8,128)(2,1)S(1)} %copy-done, f32[8,128]{1,0:T(8,128)S(1)} %copy-done.5, f32[8,512,128]{2,1,0:T(8,128)S(1)} %get-tuple-element.41.o_ref), custom_call_target="tpu_custom_call" | custom-call | tf_op jit(solution)/shard_map/grads/pallas_call | solution.py:68
  59.1 5.4 %all-to-all-start.3 = ((f32[32,32,128]{2,1,0:T(8,128)}), f32[32,32,128]{2,1,0:T(8,128)S(1)}, u32[]{:S(2)}, u32[]{:S(2)}) async-start(f32[32,32,128]{2,1,0:T(8,128)} %bitcast.8), calls=%async_computation.3 | async-start | bytes 1048576 | tf_op jit(solution)/shard_map/all_to_all | solution.py:459
  64.5 6.3 %back.1 = (bf16[8,512,128]{2,1,0:T(8,128)(2,1)S(1)}, bf16[8,512,128]{2,1,0:T(8,128)(2,1)S(1)}) custom-call(s32[8]{0:T(128)S(1)} %copy-done.6, bf16[8,512,128]{2,1,0:T(8,128)(2,1)} %get-tuple-element.43.k_hbm, bf16[8,512,128]{2,1,0:T(8,128)(2,1)} %get-tuple-element.44.v_hbm, bf16[8,512,128]{2,1,0:T(8,128)(2,1)} %get-tuple-element.35.q_ref.q_hbm, ...), custom_call_target="tpu_custom_call" | custom-call | flops 4000000000 | bytes 8388608 | tf_op jit(solution)/shard_map/back/pallas_call | solution.py:68
  70.8 0.0 copy-start.2
  70.8 5.4 %all-to-all-done.3.z_ref = f32[32,32,128]{2,1,0:T(8,128)S(1)} async-done(((f32[32,32,128]{2,1,0:T(8,128)}), f32[32,32,128]{2,1,0:T(8,128)S(1)}, u32[]{:S(2)}, u32[]{:S(2)}) %all-to-all-start.3) | async-done | bytes 524320 | tf_op jit(solution)/shard_map/all_to_all | solution.py:459
  76.2 1.4 %prefix.3 = f32[32,32,128]{2,1,0:T(8,128)} custom-call(s32[8]{0:T(128)S(1)} %copy-done.6, f32[32,32,128]{2,1,0:T(8,128)S(1)} %all-to-all-done.3.z_ref), custom_call_target="tpu_custom_call" | custom-call | tf_op jit(solution)/shard_map/prefix/pallas_call | solution.py:68
  77.6 4.0 %all-to-all-start.4 = ((f32[32,32,128]{2,1,0:T(8,128)}), f32[32,32,128]{2,1,0:T(8,128)S(1)}, u32[]{:S(2)}, u32[]{:S(2)}) async-start(f32[32,32,128]{2,1,0:T(8,128)} %prefix.3), calls=%async_computation.4 | async-start | bytes 1048576 | tf_op jit(solution)/shard_map/all_to_all | solution.py:459
  81.6 0.0 copy-done.2
  81.6 5.2 %grad_query.1 = bf16[512,8,128]{2,1,0:T(8,128)(2,1)} custom-call(s32[8]{0:T(128)S(1)} %copy-done.6, bf16[8,512,128]{2,1,0:T(8,128)(2,1)} %get-tuple-element.45.g_hbm, bf16[8,512,128]{2,1,0:T(8,128)(2,1)} %get-tuple-element.43.k_hbm, bf16[8,512,128]{2,1,0:T(8,128)(2,1)} %get-tuple-element.44.v_hbm, f32[8,128,128]{2,1,0:T(8,128)S(1)} %bitcast.6), custom_call_target="tpu_custom_call" | custom-call | flops 3000000000 | bytes 5242880 | tf_op jit(solution)/shard_map/grad_query/pallas_call | solution.py:68
  86.8 6.5 %all-to-all-done.4 = f32[32,32,128]{2,1,0:T(8,128)S(1)} async-done(((f32[32,32,128]{2,1,0:T(8,128)}), f32[32,32,128]{2,1,0:T(8,128)S(1)}, u32[]{:S(2)}, u32[]{:S(2)}) %all-to-all-start.4) | async-done | bytes 524320 | tf_op jit(solution)/shard_map/all_to_all | solution.py:459
  93.3 4.3 %finish.1 = (bf16[512,8,128]{2,1,0:T(8,128)(2,1)}, bf16[512,8,128]{2,1,0:T(8,128)(2,1)}) custom-call(s32[8]{0:T(128)S(1)} %copy-done.6, bf16[8,512,128]{2,1,0:T(8,128)(2,1)} %get-tuple-element.43.k_hbm, bf16[8,512,128]{2,1,0:T(8,128)(2,1)} %get-tuple-element.44.v_hbm, bf16[8,512,128]{2,1,0:T(8,128)(2,1)S(1)} %get-tuple-element.50.kl_ref, ...), custom_call_target="tpu_custom_call" | custom-call | tf_op jit(solution)/shard_map/finish/pallas_call | solution.py:68
Async XLA Ops:
  0.6 12.2 %copy-start.6 = (s32[8]{0:T(128)S(1)}, s32[8]{0:T(128)}, u32[]{:S(2)}) copy-start(s32[8]{0:T(128)} %slope_ref.13) | copy-start | bytes 100
  4.1 20.3 %all-to-all-start = ((f32[32,32,128]{2,1,0:T(8,128)}), f32[32,32,128]{2,1,0:T(8,128)}, u32[]{:S(2)}, u32[]{:S(2)}) async-start(f32[32,32,128]{2,1,0:T(8,128)} %bitcast.7), calls=%async_computation | async-start | bytes 1048576 | tf_op jit(solution)/shard_map/all_to_all | solution.py:459
  19.8 21.1 %copy-start = (bf16[8,512,128]{2,1,0:T(8,128)(2,1)S(1)}, bf16[8,512,128]{2,1,0:T(8,128)(2,1)}, u32[]{:S(2)}) copy-start(bf16[8,512,128]{2,1,0:T(8,128)(2,1)} %get-tuple-element.36.u_ref) | copy-start | bytes 3145732
  19.8 21.1 %copy-start.5 = (f32[8,128]{1,0:T(8,128)S(1)}, f32[8,128]{1,0:T(8,128)}, u32[]{:S(2)}) copy-start(f32[8,128]{1,0:T(8,128)} %gain_ref.3) | copy-start | bytes 12292
  24.4 16.5 %copy-start.4 = (bf16[8,512,128]{2,1,0:T(8,128)(2,1)S(1)}, bf16[8,512,128]{2,1,0:T(8,128)(2,1)}, u32[]{:S(2)}) copy-start(bf16[8,512,128]{2,1,0:T(8,128)(2,1)} %get-tuple-element.35.q_ref.q_hbm) | copy-start | bytes 3145732
  40.9 1.7 %copy-start.1 = (f32[32,32,128]{2,1,0:T(8,128)}, f32[32,32,128]{2,1,0:T(8,128)S(1)}, u32[]{:S(2)}) copy-start(f32[32,32,128]{2,1,0:T(8,128)S(1)} %all_to_all.25) | copy-start | bytes 1572868
  40.9 16.5 %copy-start.3 = (bf16[8,128,512]{2,1,0:T(8,128)(2,1)S(1)}, bf16[8,128,512]{2,1,0:T(8,128)(2,1)}, u32[]{:S(2)}) copy-start(bf16[8,128,512]{2,1,0:T(8,128)(2,1)} %get-tuple-element.40.wq_ref) | copy-start | bytes 3145732
  59.1 17.1 %all-to-all-start.3 = ((f32[32,32,128]{2,1,0:T(8,128)}), f32[32,32,128]{2,1,0:T(8,128)S(1)}, u32[]{:S(2)}, u32[]{:S(2)}) async-start(f32[32,32,128]{2,1,0:T(8,128)} %bitcast.8), calls=%async_computation.3 | async-start | bytes 1048576 | tf_op jit(solution)/shard_map/all_to_all | solution.py:459
  70.8 10.8 %copy-start.2 = (f32[32,32,128]{2,1,0:T(8,128)S(1)}, f32[32,32,128]{2,1,0:T(8,128)}, u32[]{:S(2)}) copy-start(f32[32,32,128]{2,1,0:T(8,128)} %copy-done.1) | copy-start | bytes 1572868
  77.6 15.7 %all-to-all-start.4 = ((f32[32,32,128]{2,1,0:T(8,128)}), f32[32,32,128]{2,1,0:T(8,128)S(1)}, u32[]{:S(2)}, u32[]{:S(2)}) async-start(f32[32,32,128]{2,1,0:T(8,128)} %prefix.3), calls=%async_computation.4 | async-start | bytes 1048576 | tf_op jit(solution)/shard_map/all_to_all | solution.py:459

commit v4 on v3

v4 whole, which is shorter than its diff:
```python
import functools
import math

import jax
import jax.numpy as jnp
from jax import lax
from jax.experimental import pallas as pl
from jax.experimental.pallas import tpu as pltpu
from jax.sharding import PartitionSpec as P

F32 = jnp.float32
BF16 = jnp.bfloat16
LAYER_FACTOR = 1.0 - 78.0 / 79.0 + 1e-05
HEADS = 8
LENGTH = 512
SIZE = 128
HALF = 4
RING = 4
CHUNK = 128
PARTS = LENGTH // CHUNK
VMEM_LIMIT = 24 * 1024 * 1024

NN = ((1,), (0,))
NT = ((1,), (1,))
TN = ((0,), (0,))


def rate_of(slope_ref, head):
    slope = jnp.full((1, 1), slope_ref[head].astype(F32), F32)
    return jnp.exp((slope + 1.0) * (-8.0 / 64.0 * math.log(2.0))) * LAYER_FACTOR


def rows_of(shape, start=0):
    return (lax.broadcasted_iota(jnp.int32, shape, 0) + start).astype(F32)


def dot(a, b, dims):
    return lax.dot_general(a, b, (dims, ((), ())), preferred_element_type=F32)


def masks(rate, transposed=False):
    shape = (256, 256)
    gap = lax.broadcasted_iota(jnp.int32, shape, 0) - lax.broadcasted_iota(jnp.int32, shape, 1)
    if transposed:
        gap = -gap
    base = jnp.exp(-rate * gap.astype(F32))
    return jnp.where(gap >= 0, base, 0.0), base * jnp.exp(-256.0 * rate)


def hbm(x):
    return pltpu.with_memory_space_constraint(x, pltpu.HBM)


def near(x):
    return pltpu.with_memory_space_constraint(x, pltpu.VMEM)


def call(body, name, ins, outs, scratch=(), flops=0, moved=0):
    kinds = {"smem": pltpu.SMEM, "vmem": pltpu.VMEM, "hbm": pl.ANY, "any": pl.ANY}
    args, in_specs = [], []
    for kind, x in ins:
        in_specs.append(pl.BlockSpec(memory_space=kinds[kind]))
        args.append({"vmem": near, "hbm": hbm}.get(kind, lambda a: a)(x))
    out_shape, out_specs = [], []
    for kind, shape, dtype in outs:
        out_specs.append(pl.BlockSpec(memory_space=kinds[kind]))
        out_shape.append((pltpu.VMEM if kind == "vmem" else pltpu.HBM)(shape, dtype))
    return pl.pallas_call(
        body,
        in_specs=in_specs,
        out_specs=out_specs,
        out_shape=out_shape,
        scratch_shapes=list(scratch),
        compiler_params=pltpu.CompilerParams(vmem_limit_bytes=VMEM_LIMIT),
        cost_estimate=pl.CostEstimate(flops=flops, bytes_accessed=moved, transcendentals=0),
        name=name,
    )(*args)


STATE = (HEADS, SIZE, SIZE)
HALF_STATE = (HALF, SIZE, SIZE)
ONE = (SIZE, SIZE)
ROWS = (HEADS, LENGTH, SIZE)
WHOLE = (LENGTH, HEADS, SIZE)


def by_head(wide, part):
    return [wide[pl.ds(h + part * CHUNK * HEADS, CHUNK, stride=HEADS), :] for h in range(HEADS)]


def spread(wide, block, part):
    wide[pl.ds(part * CHUNK * HEADS, CHUNK * HEADS), :] = block.astype(F32).reshape(CHUNK * HEADS, SIZE)


def core_of():
    return lax.rem(lax.axis_index("ctx"), 2)


def x_of():
    return lax.rem(lax.axis_index("ctx") // 2, RING)


def y_of():
    return lax.axis_index("ctx") // (2 * RING)


def put(src, dst, part, sem):
    c = pltpu.make_async_copy(src.at[part], dst.at[part], sem)
    c.start()
    return c


def fetch_rows(src, dst, sems, base=0):
    return [put(src, dst, pl.ds(p * CHUNK, CHUNK), sems.at[base + p]) for p in range(PARTS)]


def wait_all(copies):
    for c in copies:
        c.wait()


def dma(count):
    return pltpu.SemaphoreType.DMA((count,))


def key_kernel(slope_hbm, k_hbm, v_hbm, keep_ref, send_ref, slope_ref, kin, vin, kw, vw, s, sems):
    first = pltpu.make_async_copy(slope_hbm, slope_ref, sems.at[2 * PARTS])
    first.start()
    k_copies = fetch_rows(k_hbm, kin, sems)
    v_copies = fetch_rows(v_hbm, vin, sems, PARTS)
    first.wait()
    rates = [rate_of(slope_ref, h) for h in range(HEADS)]
    for p in range(PARTS):
        rows = pl.ds(p * CHUNK, CHUNK)
        k_copies[p].wait()
        v_copies[p].wait()
        spread(kw, kin[rows], p)
        spread(vw, vin[rows], p)
        ks, vs = by_head(kw, p), by_head(vw, p)
        left = LENGTH - 1.0 - rows_of((CHUNK, SIZE), p * CHUNK)
        for h in range(HEADS):
            weighted = (ks[h] * jnp.exp(-rates[h] * left)).astype(BF16)
            part = dot(weighted, vs[h].astype(BF16), TN)
            s[h] = part if p == 0 else s[h] + part
    core = core_of()
    send_ref[...] = s[pl.ds((1 - core) * HALF, HALF)]
    keep_ref[...] = s[pl.ds(core * HALF, HALF)]


def key_states(slope, k, v):
    whole, wide = pltpu.VMEM(WHOLE, BF16), pltpu.VMEM((LENGTH * HEADS, SIZE), F32)
    return call(
        key_kernel,
        "key_states",
        [("hbm", slope), ("hbm", k), ("hbm", v)],
        [("vmem", HALF_STATE, F32), ("vmem", HALF_STATE, F32)],
        [pltpu.SMEM((HEADS,), jnp.int32), whole, whole, wide, wide, pltpu.VMEM(STATE, F32), dma(2 * PARTS + 1)],
    )


def turn_kernel(weigh, slope_ref, a_hbm, b_hbm, *refs):
    if weigh:
        q_ref, a_ref, b_ref, wq_ref, a_in, b_in, wide, sems = refs
    else:
        a_ref, b_ref, a_in, b_in, wide, sems = refs
    pairs = ((a_hbm, a_in, a_ref), (b_hbm, b_in, b_ref))
    copies = [fetch_rows(s, d, sems, i * PARTS) for i, (s, d, _) in enumerate(pairs)]
    if weigh:
        done = rows_of((LENGTH, SIZE))
        for h in range(HEADS):
            wq_ref[h] = (q_ref[h].astype(F32) * jnp.exp(-rate_of(slope_ref, h) * done)).T.astype(BF16)
    for i, (_, near_by, turned) in enumerate(pairs):
        for p in range(PARTS):
            rows = pl.ds(p * CHUNK, CHUNK)
            copies[i][p].wait()
            spread(wide.at[i], near_by[rows], p)
            for h, block in enumerate(by_head(wide.at[i], p)):
                turned[h, rows, :] = block.astype(BF16)


def turn(slope, a, b, q=None):
    whole = pltpu.VMEM(WHOLE, BF16)
    weigh = q is not None
    return call(
        functools.partial(turn_kernel, weigh),
        "turn",
        [("smem", slope), ("hbm", a), ("hbm", b)] + ([("vmem", q)] if weigh else []),
        [("vmem", ROWS, BF16)] * 2 + ([("vmem", (HEADS, SIZE, LENGTH), BF16)] if weigh else []),
        [whole, whole, pltpu.VMEM((2, LENGTH * HEADS, SIZE), F32), dma(2 * PARTS)],
        moved=8 * 2**20,
    )


def local_kernel(slope_ref, q_ref, k_ref, v_ref, loc_ref):
    for h in range(HEADS):
        diag, off = masks(rate_of(slope_ref, h))
        q0, q1 = q_ref[h, :256], q_ref[h, 256:]
        k0, k1 = k_ref[h, :256], k_ref[h, 256:]
        v0, v1 = v_ref[h, :256], v_ref[h, 256:]
        a00 = (dot(q0, k0, NT) * diag).astype(BF16)
        a10 = (dot(q1, k0, NT) * off).astype(BF16)
        a11 = (dot(q1, k1, NT) * diag).astype(BF16)
        loc_ref[h, :256] = dot(a00, v0, NN)
        loc_ref[h, 256:] = dot(a10, v0, NN) + dot(a11, v1, NN)


def local_part(slope, q, k, v):
    (out,) = call(
        local_kernel,
        "local_part",
        [("smem", slope), ("vmem", q), ("vmem", k), ("vmem", v)],
        [("vmem", ROWS, F32)],
        flops=2 * 10**9,
        moved=5 * 2**20,
    )
    return out


def decay_of(slope_ref, head, length):
    return jnp.exp(-float(length) * rate_of(slope_ref, head))


def around(place, d):
    return lax.rem(place + d + RING, RING)


def total_kernel(reverse, slope_ref, keep_ref, recv_ref, own_ref, to1, to2, to3, total):
    core, x = core_of(), x_of()
    flag = (core == 0) != reverse
    for h in range(HALF):
        decay = decay_of(slope_ref, core * HALF + h, LENGTH)
        total[h] = jnp.where(flag, decay, 1.0) * keep_ref[h] + jnp.where(flag, 1.0, decay) * recv_ref[h]
    own_ref[...] = total[x]
    for d, ref in ((1, to1), (2, to2), (3, to3)):
        ref[...] = total[around(x, d)]


def row_kernel(reverse, slope_ref, own_ref, from1, from2, from3, sum_ref, part_ref, held):
    x = x_of()
    decay = decay_of(slope_ref, core_of() * HALF + x, 2 * LENGTH)
    held[x] = own_ref[...]
    for d, ref in ((1, from1), (2, from2), (3, from3)):
        held[around(x, -d)] = ref[...]
    state = jnp.zeros(ONE, F32)
    for n in range(RING):
        place = RING - 1 - n if reverse else n
        part_ref[place] = state
        state = decay * state + held[place]
    sum_ref[...] = state


def column_kernel(reverse, slope_ref, own_ref, from1, from2, from3, part_ref, mine_ref, to1, to2, to3, held, done):
    x, y = x_of(), y_of()
    head = core_of() * HALF + x
    decay = decay_of(slope_ref, head, 2 * RING * LENGTH)
    held[y] = own_ref[...]
    for d, ref in ((1, from1), (2, from2), (3, from3)):
        held[around(y, -d)] = ref[...]
    state = jnp.zeros(ONE, F32)
    for n in range(RING - 1):
        place = RING - 1 - n if reverse else n
        before = place > y if reverse else place < y
        state = jnp.where(before, decay * state + held[place], state)
    for place in range(RING):
        steps = RING - 1 - place if reverse else place
        done[place] = decay_of(slope_ref, head, 2 * LENGTH * steps) * state + part_ref[place]
    mine_ref[...] = done[x]
    for d, ref in ((1, to1), (2, to2), (3, to3)):
        ref[...] = done[around(x, d)]


def after_kernel(reverse, slope_ref, own_ref, from1, from2, from3, keep_ref, recv_ref, out_ref, give_ref, held):
    core, x = core_of(), x_of()
    flag = (core == 0) != reverse
    held[x] = own_ref[...]
    for d, ref in ((1, from1), (2, from2), (3, from3)):
        held[around(x, -d)] = ref[...]
    for h in range(HALF):
        decay = decay_of(slope_ref, core * HALF + h, LENGTH)
        state = held[h]
        beyond = decay * state + jnp.where(flag, keep_ref[h], recv_ref[h])
        out_ref[h] = jnp.where(flag, state, beyond)
        give_ref[h] = jnp.where(flag, beyond, state)


def small(kernel, name, reverse, slope, ins, outs, scratch):
    return call(
        functools.partial(kernel, reverse),
        name,
        [("smem", slope)] + [("vmem", a) for a in ins],
        [("vmem", shape, F32) for shape in outs],
        [pltpu.VMEM(shape, F32) for shape in scratch],
    )


def states_of(own_ref, other_ref, state):
    core = core_of()
    state[pl.ds(core * HALF, HALF)] = own_ref[...].astype(BF16)
    state[pl.ds((1 - core) * HALF, HALF)] = other_ref[...].astype(BF16)


def output_kernel(slope_ref, q_ref, u_ref, gain_ref, own_ref, other_ref, loc, o_ref, sums_ref, state, sq, dt, sums):
    states_of(own_ref, other_ref, state)
    done = rows_of((LENGTH, SIZE), 1)
    for h in range(HEADS):
        decay_in = jnp.exp(-rate_of(slope_ref, h) * done)
        o_ref[h] = decay_in * dot(q_ref[h], state[h], NN)
    for r in range(0, LENGTH, 32):
        rows = pl.ds(r, 32)
        square = product = None
        for h in range(HEADS):
            out = o_ref[h, rows, :] + loc[h, rows, :]
            o_ref[h, rows, :] = out
            scaled = gain_ref[h : h + 1, :] * u_ref[h, rows, :].astype(F32)
            square = out * out if h == 0 else square + out * out
            product = out * scaled if h == 0 else product + out * scaled
        sq[rows, :] = square
        dt[rows, :] = product
    for b in range(4):
        rows = slice(b * 128, (b + 1) * 128)
        sums[b : b + 1, :] = jnp.sum(sq[rows, :].T, axis=0, keepdims=True)
        sums[4 + b : 5 + b, :] = jnp.sum(dt[rows, :].T, axis=0, keepdims=True)
    for i in range(sums_ref.shape[0]):
        sums_ref[i] = sums[...]


def outputs(slope, q, u, gain, own, other, loc, peers):
    return call(
        output_kernel,
        "outputs",
        [("smem", slope), ("vmem", q), ("vmem", u), ("vmem", gain), ("vmem", own), ("vmem", other), ("vmem", loc)],
        [("vmem", ROWS, F32), ("vmem", (peers, 8, SIZE), F32)],
        [
            pltpu.VMEM(STATE, BF16),
            pltpu.VMEM((LENGTH, SIZE), F32),
            pltpu.VMEM((LENGTH, SIZE), F32),
            pltpu.VMEM((8, SIZE), F32),
        ],
    )


def grad_kernel(sums_ref, wq_ref, u_ref, gain_ref, o_ref, g, keep_ref, send_ref, acc):
    peers = sums_ref.shape[0]
    features = float(peers * HEADS * SIZE)
    sums = sums_ref[0]
    for i in range(1, peers):
        sums = sums + sums_ref[i]
    root = lax.rsqrt(sums[0:4, :] * (1.0 / features) + 1e-06)
    factor = root * root * root * sums[4:8, :] * (1.0 / features)
    for b in range(4):
        rows = pl.ds(b * 128, 128)
        inv = jnp.broadcast_to(root[b : b + 1, :], (128, 128)).T
        coef = jnp.broadcast_to(factor[b : b + 1, :], (128, 128)).T
        for h in range(HEADS):
            scaled = gain_ref[h : h + 1, :] * u_ref[h, rows, :].astype(F32)
            g[h, rows, :] = (inv * scaled - o_ref[h, rows, :] * coef).astype(BF16)
    for h in range(HEADS):
        acc[h] = dot(wq_ref[h], g[h], NN)
    core = core_of()
    keep_ref[...] = acc[pl.ds(core * HALF, HALF)]
    send_ref[...] = acc[pl.ds((1 - core) * HALF, HALF)]


def grads(sums, wq, u, gain, o):
    return call(
        grad_kernel,
        "grads",
        [("vmem", sums), ("vmem", wq), ("vmem", u), ("vmem", gain), ("vmem", o)],
        [("vmem", ROWS, BF16), ("vmem", HALF_STATE, F32), ("vmem", HALF_STATE, F32)],
        [pltpu.VMEM(STATE, F32)],
    )


def query_kernel(slope_ref, g_ref, k_ref, v_ref, own_ref, other_ref, out_hbm, state, wide, block, sems):
    states_of(own_ref, other_ref, state)
    done = rows_of((LENGTH, SIZE), 1)
    for h in range(HEADS):
        rate = rate_of(slope_ref, h)
        diag, off = masks(rate)
        g0, g1 = g_ref[h, :256], g_ref[h, 256:]
        k0, k1 = k_ref[h, :256], k_ref[h, 256:]
        v0, v1 = v_ref[h, :256], v_ref[h, 256:]
        b00 = (dot(g0, v0, NT) * diag).astype(BF16)
        b10 = (dot(g1, v0, NT) * off).astype(BF16)
        b11 = (dot(g1, v1, NT) * diag).astype(BF16)
        carried = jnp.exp(-rate * done) * dot(g_ref[h], state[h], NT)
        wide[pl.ds(h, 256, stride=HEADS), :] = dot(b00, k0, NN) + carried[:256]
        wide[pl.ds(h + 256 * HEADS, 256, stride=HEADS), :] = (
            dot(b10, k0, NN) + dot(b11, k1, NN) + carried[256:]
        )
    copies = []
    for p in range(PARTS):
        rows = pl.ds(p * CHUNK, CHUNK)
        block[rows] = wide[pl.ds(p * CHUNK * HEADS, CHUNK * HEADS), :].reshape(CHUNK, HEADS, SIZE).astype(BF16)
        copies.append(put(block, out_hbm, rows, sems.at[p]))
    wait_all(copies)


def grad_query(slope, g, k, v, own, other):
    (out,) = call(
        query_kernel,
        "grad_query",
        [("smem", slope), ("vmem", g), ("vmem", k), ("vmem", v), ("vmem", own), ("vmem", other)],
        [("hbm", WHOLE, BF16)],
        [
            pltpu.VMEM((HEADS, SIZE, SIZE), BF16),
            pltpu.VMEM((LENGTH * HEADS, SIZE), F32),
            pltpu.VMEM(WHOLE, BF16),
            dma(PARTS),
        ],
        flops=3 * 10**9,
        moved=5 * 2**20,
    )
    return out


def back_kernel(slope_ref, a_ref, b_ref, c_ref, out_ref):
    for h in range(HEADS):
        diag, off = masks(rate_of(slope_ref, h), True)
        a0, a1 = a_ref[h, :256], a_ref[h, 256:]
        b0, b1 = b_ref[h, :256], b_ref[h, 256:]
        c0, c1 = c_ref[h, :256], c_ref[h, 256:]
        t00 = (dot(a0, b0, NT) * diag).astype(BF16)
        t01 = (dot(a0, b1, NT) * off).astype(BF16)
        t11 = (dot(a1, b1, NT) * diag).astype(BF16)
        out_ref[h, :256] = (dot(t00, c0, NN) + dot(t01, c1, NN)).astype(BF16)
        out_ref[h, 256:] = dot(t11, c1, NN).astype(BF16)


def back(slope, a, b, c, name):
    (out,) = call(
        back_kernel,
        name,
        [("smem", slope), ("vmem", a), ("vmem", b), ("vmem", c)],
        [("vmem", ROWS, BF16)],
        flops=2 * 10**9,
        moved=5 * 2**20,
    )
    return out


def finish_kernel(slope_ref, k, v, kl_ref, vl_ref, own_ref, other_ref, gk_hbm, gv_hbm, state, wk, wv, gk, gv, out_sems):
    states_of(own_ref, other_ref, state)
    rates = [rate_of(slope_ref, h) for h in range(HEADS)]
    left = LENGTH - rows_of((LENGTH, SIZE))
    writes = []
    for n, (x, add, wide, out, to, dims) in enumerate(
        ((v, kl_ref, wk, gk, gk_hbm, NT), (k, vl_ref, wv, gv, gv_hbm, NN))
    ):
        for h in range(HEADS):
            moved = jnp.exp(-rates[h] * left) * dot(x[h], state[h], dims)
            wide[pl.ds(h, LENGTH, stride=HEADS), :] = add[h].astype(F32) + moved
        for p in range(2):
            rows = pl.ds(p * 256, 256)
            flat = pl.ds(p * 256 * HEADS, 256 * HEADS)
            out[rows] = wide[flat, :].reshape(256, HEADS, SIZE).astype(BF16)
            writes.append(put(out, to, rows, out_sems.at[2 * n + p]))
    wait_all(writes)


def finish(slope, k, v, kl, vl, own, other):
    wide = pltpu.VMEM((LENGTH * HEADS, SIZE), F32)
    block = pltpu.VMEM(WHOLE, BF16)
    return call(
        finish_kernel,
        "finish",
        [("smem", slope), ("vmem", k), ("vmem", v), ("vmem", kl), ("vmem", vl), ("vmem", own), ("vmem", other)],
        [("hbm", WHOLE, BF16), ("hbm", WHOLE, BF16)],
        [pltpu.VMEM(STATE, BF16), wide, wide, block, block, dma(4)],
    )


def permute(a, dy, dx, dc):
    pairs = []
    for y in range(RING):
        for x in range(RING):
            for c in range(2):
                to = ((y + dy) % RING * RING + (x + dx) % RING) * 2 + (c ^ dc)
                pairs.append(((y * RING + x) * 2 + c, to))
    return lax.ppermute(a, "ctx", pairs)


def exchange(a):
    return permute(a, 0, 0, 1)


def along_x(parts):
    return [permute(a, 0, d + 1, 0) for d, a in enumerate(parts)]


def along_y(a):
    return [permute(a, d, 0, 0) for d in (1, 2, 3)]


def beside(moved, work):
    out = lax.optimization_barrier((tuple(moved), tuple(work)))
    return list(out[0]), list(out[1])


def scan(slope, keep, send, reverse, first, second, third):
    recv = exchange(send)
    one = [ONE] * 4
    own, *parts = small(total_kernel, "chip_total", reverse, slope, [keep, recv], one, [HALF_STATE])
    moved = along_x(parts)
    moved, done1 = beside(moved, first())
    row, part = small(row_kernel, "row_sum", reverse, slope, [own, *moved], [ONE, HALF_STATE], [HALF_STATE])
    moved = along_y(row)
    moved, done2 = beside(moved, second(done1))
    own, *parts = small(
        column_kernel, "column_sum", reverse, slope, [row, *moved, part], one, [HALF_STATE, HALF_STATE]
    )
    moved = along_x(parts)
    moved, done3 = beside(moved, third(done1, done2))
    mine, give = small(
        after_kernel, "after", reverse, slope, [own, *moved, keep, recv], [HALF_STATE] * 2, [HALF_STATE]
    )
    return mine, exchange(give), done1, done2, done3


def on_device(queries, key_rows, value_rows, upstream, norm_gain, slope_index):
    slope = slope_index

    keep, send = key_states(slope, key_rows, value_rows)
    e_own, e_other, (qh, kh), (vh, uh, wq), (loc,) = scan(
        slope,
        keep,
        send,
        False,
        lambda: turn(slope, queries, key_rows),
        lambda a: turn(slope, value_rows, upstream, a[0]),
        lambda a, b: [local_part(slope, a[0], a[1], b[0])],
    )

    peers = lax.axis_size("head")
    out, sums = outputs(slope, qh, uh, norm_gain, e_own, e_other, loc, peers)
    sums = lax.all_to_all(sums, "head", 0, 0, tiled=True)
    g, keep, send = grads(sums, wq, uh, norm_gain, out)

    l_own, l_other, (gv_local,), (gk_local,), (gq,) = scan(
        slope,
        keep,
        send,
        True,
        lambda: [back(slope, kh, qh, g, "gv_local")],
        lambda a: [back(slope, vh, g, qh, "gk_local")],
        lambda a, b: [grad_query(slope, g, kh, vh, e_own, e_other)],
    )
    gk, gv = finish(slope, kh, vh, gk_local, gv_local, l_own, l_other)
    return gq, gk, gv


def solution(mesh):
    rows = P("ctx", "head", None)
    return jax.shard_map(
        on_device,
        mesh=mesh,
        in_specs=(rows, rows, rows, rows, P("head", None), P("head")),
        out_specs=(rows, rows, rows),
        check_vma=False,
    )
```

time: 98.3 us -> 88.2 us (0.90)
  starting transfers between devices: 18.1 us -> 33.4 us
  blocking collectives: 30.1 us -> 14.9 us
  waiting for transfers between devices: 16.5 us -> 7.9 us
  Pallas kernels: 32.1 us -> 30.7 us
    ppermute x0 -> x22, starting transfers between devices: none -> 33.4 us  [permute(): return lax.ppermute(a, 'ctx', pairs)]
    all_to_all x3 -> x0, starting transfers between devices: 18.1 us -> none  [all_to_all(): lax.all_to_all(a.reshape(BLOCKS, SLICE, SIZE), 'ctx', 0, 0, tiled=True)]
    all_to_all x3 -> x0, waiting for transfers between devices: 16.5 us -> none  [all_to_all(): lax.all_to_all(a.reshape(BLOCKS, SLICE, SIZE), 'ctx', 0, 0, tiled=True)]
    all_to_all x1 -> x0, blocking collectives: 15.2 us -> none  [all_to_all(): lax.all_to_all(a.reshape(BLOCKS, SLICE, SIZE), 'ctx', 0, 0, tiled=True)]
    ppermute x0 -> x22, waiting for transfers between devices: none -> 7.9 us  [permute(): return lax.ppermute(a, 'ctx', pairs)]
    pallas_call x9 -> x18, Pallas kernels: 32.1 us -> 30.7 us  [call(): pl.pallas_call(body, in_specs=in_specs, out_specs=out_specs, out_shape=ou...]
  transfers between devices with their start and end apart: 3 -> 22, of which waited for: 3 -> 11; matrix products, arithmetic and copies ran while one was open for 0% -> 0% of each run, Pallas kernels for 19% -> 20%
where the time goes in v4:
time: 88.2 us; the launch traced here: 88 us
  starting transfers between devices  33.4 us (38%)
  Pallas kernels  30.7 us (35%)
  blocking collectives  14.9 us (17%)
  waiting for transfers between devices  7.9 us (9%)
  between operations  1.04 us (1%)
    ppermute x22, starting transfers between devices, permute(): return lax.ppermute(a, 'ctx', pairs)  33.4 us
    pallas_call x18, Pallas kernels, call(): pl.pallas_call(body, in_specs=in_specs, out_specs=out_specs, out_shape=ou...  30.7 us
    all_to_all x1, blocking collectives, on_device(): sums = lax.all_to_all(sums, 'head', 0, 0, tiled=True)  14.9 us
    ppermute x22, waiting for transfers between devices, permute(): return lax.ppermute(a, 'ctx', pairs)  7.9 us
  transfers between devices with their start and end apart: 22, of which 11 were waited for; matrix products, arithmetic and copies ran while one was open for 0% of the time, Pallas kernels for 20%

profile of v4, /device:TPU:1, one launch (start us, length us, event | category | flops | bytes accessed | tf_op | source)
XLA Modules:
  0.0 88.0 jit_solution(10667642863081081403)
XLA Ops:
  0.6 2.6 %key_states.1 = (f32[4,128,128]{2,1,0:T(8,128)S(1)}, f32[4,128,128]{2,1,0:T(8,128)S(1)}) custom-call(s32[8]{0:T(128)} %slope_ref.31, bf16[512,8,128]{2,1,0:T(8,128)(2,1)} %b_hbm.2, bf16[512,8,128]{2,1,0:T(8,128)(2,1)} %a_hbm.3), custom_call_target="tpu_custom_call" | custom-call | tf_op jit(solution)/shard_map/key_states/pallas_call | solution.py:68
  3.3 3.3 %collective-permute-start = (f32[4,128,128]{2,1,0:T(8,128)S(1)}, f32[4,128,128]{2,1,0:T(8,128)S(1)}, u32[]{:S(2)}, u32[]{:S(2)}) collective-permute-start(f32[4,128,128]{2,1,0:T(8,128)S(1)} %get-tuple-element.69), channel_id=1, source_target_pairs={{0,8},{8,0},{16,24},{24,16},{32,40},{40,32},{48,56},{56,48},{64,72... | collective-permute-start | bytes 786440 | tf_op jit(solution)/shard_map/ppermute | solution.py:480
  6.6 1.2 %collective-permute-done.recv_ref = f32[4,128,128]{2,1,0:T(8,128)S(1)} collective-permute-done((f32[4,128,128]{2,1,0:T(8,128)S(1)}, f32[4,128,128]{2,1,0:T(8,128)S(1)}, u32[]{:S(2)}, u32[]{:S(2)}) %collective-permute-start) | collective-permute-done | bytes 262176 | tf_op jit(solution)/shard_map/ppermute | solution.py:480
  8.5 1.9 %collective-permute-start.2 = (f32[128,128]{1,0:T(8,128)S(1)}, f32[128,128]{1,0:T(8,128)S(1)}, u32[]{:S(2)}, u32[]{:S(2)}) collective-permute-start(f32[128,128]{1,0:T(8,128)S(1)} %get-tuple-element.71), channel_id=1, source_target_pairs={{0,32},{8,40},{16,48},{24,56},{32,0},{40,8},{48,16},{56,24},{64,96... | collective-permute-start | bytes 196616 | tf_op jit(solution)/shard_map/ppermute | solution.py:480
  10.4 1.2 %collective-permute-start.3 = (f32[128,128]{1,0:T(8,128)S(1)}, f32[128,128]{1,0:T(8,128)S(1)}, u32[]{:S(2)}, u32[]{:S(2)}) collective-permute-start(f32[128,128]{1,0:T(8,128)S(1)} %get-tuple-element.72), channel_id=1, source_target_pairs={{0,48},{8,56},{16,0},{24,8},{32,16},{40,24},{48,32},{56,40},{64,11... | collective-permute-start | bytes 196616 | tf_op jit(solution)/shard_map/ppermute | solution.py:480
  11.6 2.5 %turn.2 = (bf16[8,512,128]{2,1,0:T(8,128)(2,1)S(1)}, bf16[8,512,128]{2,1,0:T(8,128)(2,1)S(1)}) custom-call(s32[8]{0:T(128)S(1)} %copy-done, bf16[512,8,128]{2,1,0:T(8,128)(2,1)} %a_hbm.2, bf16[512,8,128]{2,1,0:T(8,128)(2,1)} %b_hbm.2), custom_call_target="tpu_custom_call" | custom-call | bytes 8388608 | tf_op jit(solution)/shard_map/turn/pallas_call | solution.py:68
  15.3 2.2 %collective-permute-start.6 = (f32[128,128]{1,0:T(8,128)S(1)}, f32[128,128]{1,0:T(8,128)S(1)}, u32[]{:S(2)}, u32[]{:S(2)}) collective-permute-start(f32[128,128]{1,0:T(8,128)S(1)} %get-tuple-element.80.own_ref), channel_id=1, source_target_pairs={{0,192},{8,200},{16,208},{24,216},{32,224},{40,232},{48,240},{56,2... | collective-permute-start | bytes 196616 | tf_op jit(solution)/shard_map/ppermute | solution.py:480
  17.9 0.7 collective-permute-start.4
  18.6 2.8 %turn.3 = (bf16[8,512,128]{2,1,0:T(8,128)(2,1)S(1)}, bf16[8,512,128]{2,1,0:T(8,128)(2,1)S(1)}, bf16[8,128,512]{2,1,0:T(8,128)(2,1)S(1)}) custom-call(s32[8]{0:T(128)S(1)} %copy-done, bf16[512,8,128]{2,1,0:T(8,128)(2,1)} %a_hbm.3, bf16[512,8,128]{2,1,0:T(8,128)(2,1)} %b_hbm.3, bf16[8,512,128]{2,1,0:T(8,128)(2,1)S(1)} %get-tuple-element.75.refs_0_.q_ref.b_ref.c_ref), custom_call_target="tpu_custom_call" | custom-call | bytes 8388608 | tf_op jit(solution)/shard_map/turn/pallas_call | solution.py:68
  21.4 0.8 collective-permute-done.5.from2
  23.9 2.7 %collective-permute-start.8 = (f32[128,128]{1,0:T(8,128)S(1)}, f32[128,128]{1,0:T(8,128)S(1)}, u32[]{:S(2)}, u32[]{:S(2)}) collective-permute-start(f32[128,128]{1,0:T(8,128)S(1)} %get-tuple-element.91), channel_id=1, source_target_pairs={{0,32},{8,40},{16,48},{24,56},{32,0},{40,8},{48,16},{56,24},{64,96... | collective-permute-start | bytes 196616 | tf_op jit(solution)/shard_map/ppermute | solution.py:480
  26.9 2.8 %local_part.1.loc = f32[8,512,128]{2,1,0:T(8,128)S(1)} custom-call(s32[8]{0:T(128)S(1)} %copy-done, bf16[8,512,128]{2,1,0:T(8,128)(2,1)S(1)} %get-tuple-element.75.refs_0_.q_ref.b_ref.c_ref, bf16[8,512,128]{2,1,0:T(8,128)(2,1)S(1)} %get-tuple-element.93.k_ref.a_ref.k, bf16[8,512,128]{2,1,0:T(8,128)(2,1)S(1)} %get-tuple-element.94.v_ref.a_ref.v), custom_call_target="tpu_custom_call" | custom-call | flops 2000000000 | bytes 5242880 | tf_op jit(solution)/shard_map/local_part/pallas_call | solution.py:68
  30.4 5.2 %collective-permute-start.10 = (f32[4,128,128]{2,1,0:T(8,128)S(1)}, f32[4,128,128]{2,1,0:T(8,128)S(1)}, u32[]{:S(2)}, u32[]{:S(2)}) collective-permute-start(f32[4,128,128]{2,1,0:T(8,128)S(1)} %get-tuple-element.99), channel_id=1, source_target_pairs={{0,8},{8,0},{16,24},{24,16},{32,40},{40,32},{48,56},{56,48},{64,72... | collective-permute-start | bytes 786440 | tf_op jit(solution)/shard_map/ppermute | solution.py:480
  35.6 1.2 %collective-permute-done.10.other_ref = f32[4,128,128]{2,1,0:T(8,128)S(1)} collective-permute-done((f32[4,128,128]{2,1,0:T(8,128)S(1)}, f32[4,128,128]{2,1,0:T(8,128)S(1)}, u32[]{:S(2)}, u32[]{:S(2)}) %collective-permute-start.10) | collective-permute-done | bytes 262176 | tf_op jit(solution)/shard_map/ppermute | solution.py:480
  36.8 1.7 %outputs.1 = (f32[8,512,128]{2,1,0:T(8,128)S(1)}, f32[8,8,128]{2,1,0:T(8,128)S(1)}) custom-call(s32[8]{0:T(128)S(1)} %copy-done, bf16[8,512,128]{2,1,0:T(8,128)(2,1)S(1)} %get-tuple-element.75.refs_0_.q_ref.b_ref.c_ref, bf16[8,512,128]{2,1,0:T(8,128)(2,1)S(1)} %get-tuple-element.84.u_ref, f32[8,128]{1,0:T(8,128)S(1)} %copy-done.1, ...), custom_call_target="tpu_custom_call" | custom-call | tf_op jit(solution)/shard_map/outputs/pallas_call | solution.py:68
  38.5 14.9 %all_to_all.5.sums_ref = f32[8,8,128]{2,1,0:T(8,128)S(1)} all-to-all(f32[8,8,128]{2,1,0:T(8,128)S(1)} %get-tuple-element.101), channel_id=1, replica_groups=mesh['ctx'=32,'head'=8] {'head'}, dimensions={0} | all-to-all | bytes 65536 | tf_op jit(solution)/shard_map/all_to_all | solution.py:536
  53.4 1.0 %grads.1 = (bf16[8,512,128]{2,1,0:T(8,128)(2,1)S(1)}, f32[4,128,128]{2,1,0:T(8,128)S(1)}, f32[4,128,128]{2,1,0:T(8,128)S(1)}) custom-call(f32[8,8,128]{2,1,0:T(8,128)S(1)} %all_to_all.5.sums_ref, bf16[8,128,512]{2,1,0:T(8,128)(2,1)S(1)} %get-tuple-element.102.wq_ref, bf16[8,512,128]{2,1,0:T(8,128)(2,1)S(1)} %get-tuple-element.84.u_ref, ...), custom_call_target="tpu_custom_call" | custom-call | tf_op jit(solution)/shard_map/grads/pallas_call | solution.py:68
  54.4 1.8 %collective-permute-start.11 = (f32[4,128,128]{2,1,0:T(8,128)S(1)}, f32[4,128,128]{2,1,0:T(8,128)S(1)}, u32[]{:S(2)}, u32[]{:S(2)}) collective-permute-start(f32[4,128,128]{2,1,0:T(8,128)S(1)} %get-tuple-element.105), channel_id=1, source_target_pairs={{0,8},{8,0},{16,24},{24,16},{32,40},{40,32},{48,56},{56,48},{64,72... | collective-permute-start | bytes 786440 | tf_op jit(solution)/shard_map/ppermute | solution.py:480
  56.2 1.2 %collective-permute-done.11.recv_ref = f32[4,128,128]{2,1,0:T(8,128)S(1)} collective-permute-done((f32[4,128,128]{2,1,0:T(8,128)S(1)}, f32[4,128,128]{2,1,0:T(8,128)S(1)}, u32[]{:S(2)}, u32[]{:S(2)}) %collective-permute-start.11) | collective-permute-done | bytes 262176 | tf_op jit(solution)/shard_map/ppermute | solution.py:480
  58.4 2.2 %collective-permute-start.13 = (f32[128,128]{1,0:T(8,128)S(1)}, f32[128,128]{1,0:T(8,128)S(1)}, u32[]{:S(2)}, u32[]{:S(2)}) collective-permute-start(f32[128,128]{1,0:T(8,128)S(1)} %get-tuple-element.108), channel_id=1, source_target_pairs={{0,32},{8,40},{16,48},{24,56},{32,0},{40,8},{48,16},{56,24},{64,96... | collective-permute-start | bytes 196616 | tf_op jit(solution)/shard_map/ppermute | solution.py:480
  60.6 0.8 collective-permute-start.14
  61.4 2.8 %gv_local.1.vl_ref = bf16[8,512,128]{2,1,0:T(8,128)(2,1)S(1)} custom-call(s32[8]{0:T(128)S(1)} %copy-done, bf16[8,512,128]{2,1,0:T(8,128)(2,1)S(1)} %get-tuple-element.93.k_ref.a_ref.k, bf16[8,512,128]{2,1,0:T(8,128)(2,1)S(1)} %get-tuple-element.75.refs_0_.q_ref.b_ref.c_ref, bf16[8,512,128]{2,1,0:T(8,128)(2,1)S(1)} %get-tuple-element.110.c_ref.b_ref.g_ref), custom_call_target="tpu_custom_call" | custom-call | flops 2000000000 | bytes 5242880 | tf_op jit(solution)/shard_map/gv_local/pallas_call | solution.py:68
  65.3 1.0 %collective-permute-start.16 = (f32[128,128]{1,0:T(8,128)S(1)}, f32[128,128]{1,0:T(8,128)S(1)}, u32[]{:S(2)}, u32[]{:S(2)}) collective-permute-start(f32[128,128]{1,0:T(8,128)S(1)} %get-tuple-element.114.own_ref), channel_id=1, source_target_pairs={{0,128},{8,136},{16,144},{24,152},{32,160},{40,168},{48,176},{56,1... | collective-permute-start | bytes 196616 | tf_op jit(solution)/shard_map/ppermute | solution.py:480
  66.9 2.8 %gk_local.1.kl_ref = bf16[8,512,128]{2,1,0:T(8,128)(2,1)S(1)} custom-call(s32[8]{0:T(128)S(1)} %copy-done, bf16[8,512,128]{2,1,0:T(8,128)(2,1)S(1)} %get-tuple-element.94.v_ref.a_ref.v, bf16[8,512,128]{2,1,0:T(8,128)(2,1)S(1)} %get-tuple-element.110.c_ref.b_ref.g_ref, bf16[8,512,128]{2,1,0:T(8,128)(2,1)S(1)} %get-tuple-element.75.refs_0_.q_ref.b_ref.c_ref), custom_call_target="tpu_custom_call" | custom-call | flops 2000000000 | bytes 5242880 | tf_op jit(solution)/shard_map/gk_local/pallas_call | solution.py:68
  69.9 0.8 collective-permute-done.15.from1
  71.3 1.0 %collective-permute-start.18 = (f32[128,128]{1,0:T(8,128)S(1)}, f32[128,128]{1,0:T(8,128)S(1)}, u32[]{:S(2)}, u32[]{:S(2)}) collective-permute-start(f32[128,128]{1,0:T(8,128)S(1)} %get-tuple-element.119), channel_id=1, source_target_pairs={{0,16},{8,24},{16,32},{24,40},{32,48},{40,56},{48,0},{56,8},{64,80... | collective-permute-start | bytes 196616 | tf_op jit(solution)/shard_map/ppermute | solution.py:480
  72.4 2.6 %collective-permute-start.19 = (f32[128,128]{1,0:T(8,128)S(1)}, f32[128,128]{1,0:T(8,128)S(1)}, u32[]{:S(2)}, u32[]{:S(2)}) collective-permute-start(f32[128,128]{1,0:T(8,128)S(1)} %get-tuple-element.120), channel_id=1, source_target_pairs={{0,32},{8,40},{16,48},{24,56},{32,0},{40,8},{48,16},{56,24},{64,96... | collective-permute-start | bytes 196616 | tf_op jit(solution)/shard_map/ppermute | solution.py:480
  75.1 3.8 %grad_query.1 = bf16[512,8,128]{2,1,0:T(8,128)(2,1)} custom-call(s32[8]{0:T(128)S(1)} %copy-done, bf16[8,512,128]{2,1,0:T(8,128)(2,1)S(1)} %get-tuple-element.110.c_ref.b_ref.g_ref, bf16[8,512,128]{2,1,0:T(8,128)(2,1)S(1)} %get-tuple-element.93.k_ref.a_ref.k, bf16[8,512,128]{2,1,0:T(8,128)(2,1)S(1)} %get-tuple-element.94.v_ref.a_ref.v, ...), custom_call_target="tpu_custom_call" | custom-call | flops 3000000000 | bytes 5242880 | tf_op jit(solution)/shard_map/grad_query/pallas_call | solution.py:68
  79.0 0.7 after.3
  79.6 4.1 %collective-permute-start.21 = (f32[4,128,128]{2,1,0:T(8,128)S(1)}, f32[4,128,128]{2,1,0:T(8,128)S(1)}, u32[]{:S(2)}, u32[]{:S(2)}) collective-permute-start(f32[4,128,128]{2,1,0:T(8,128)S(1)} %get-tuple-element.130), channel_id=1, source_target_pairs={{0,8},{8,0},{16,24},{24,16},{32,40},{40,32},{48,56},{56,48},{64,72... | collective-permute-start | bytes 786440 | tf_op jit(solution)/shard_map/ppermute | solution.py:480
  83.7 1.2 %collective-permute-done.21.other_ref = f32[4,128,128]{2,1,0:T(8,128)S(1)} collective-permute-done((f32[4,128,128]{2,1,0:T(8,128)S(1)}, f32[4,128,128]{2,1,0:T(8,128)S(1)}, u32[]{:S(2)}, u32[]{:S(2)}) %collective-permute-start.21) | collective-permute-done | bytes 262176 | tf_op jit(solution)/shard_map/ppermute | solution.py:480
  84.9 3.0 %finish.1 = (bf16[512,8,128]{2,1,0:T(8,128)(2,1)}, bf16[512,8,128]{2,1,0:T(8,128)(2,1)}) custom-call(s32[8]{0:T(128)S(1)} %copy-done, bf16[8,512,128]{2,1,0:T(8,128)(2,1)S(1)} %get-tuple-element.93.k_ref.a_ref.k, bf16[8,512,128]{2,1,0:T(8,128)(2,1)S(1)} %get-tuple-element.94.v_ref.a_ref.v, bf16[8,512,128]{2,1,0:T(8,128)(2,1)S(1)} %gk_local.1.kl_ref, ...), custom_call_target="tpu_custom_call" | custom-call | tf_op jit(solution)/shard_map/finish/pallas_call | solution.py:68
  (35 shorter events, 8.6 us)
Async XLA Ops:
  0.6 7.2 %copy-start = (s32[8]{0:T(128)S(1)}, s32[8]{0:T(128)}, u32[]{:S(2)}) copy-start(s32[8]{0:T(128)} %slope_ref.31) | copy-start | bytes 100
  3.3 4.5 %collective-permute-start = (f32[4,128,128]{2,1,0:T(8,128)S(1)}, f32[4,128,128]{2,1,0:T(8,128)S(1)}, u32[]{:S(2)}, u32[]{:S(2)}) collective-permute-start(f32[4,128,128]{2,1,0:T(8,128)S(1)} %get-tuple-element.69), channel_id=1, source_target_pairs={{0,8},{8,0},{16,24},{24,16},{32,40},{40,32},{48,56},{56,48},{64,72... | collective-permute-start | bytes 786440 | tf_op jit(solution)/shard_map/ppermute | solution.py:480
  8.4 5.7 %collective-permute-start.1 = (f32[128,128]{1,0:T(8,128)S(1)}, f32[128,128]{1,0:T(8,128)S(1)}, u32[]{:S(2)}, u32[]{:S(2)}) collective-permute-start(f32[128,128]{1,0:T(8,128)S(1)} %get-tuple-element.70), channel_id=1, source_target_pairs={{0,16},{8,24},{16,32},{24,40},{32,48},{40,56},{48,0},{56,8},{64,80... | collective-permute-start | bytes 196616 | tf_op jit(solution)/shard_map/ppermute | solution.py:480
  8.5 5.7 %collective-permute-start.2 = (f32[128,128]{1,0:T(8,128)S(1)}, f32[128,128]{1,0:T(8,128)S(1)}, u32[]{:S(2)}, u32[]{:S(2)}) collective-permute-start(f32[128,128]{1,0:T(8,128)S(1)} %get-tuple-element.71), channel_id=1, source_target_pairs={{0,32},{8,40},{16,48},{24,56},{32,0},{40,8},{48,16},{56,24},{64,96... | collective-permute-start | bytes 196616 | tf_op jit(solution)/shard_map/ppermute | solution.py:480
  10.4 4.2 %collective-permute-start.3 = (f32[128,128]{1,0:T(8,128)S(1)}, f32[128,128]{1,0:T(8,128)S(1)}, u32[]{:S(2)}, u32[]{:S(2)}) collective-permute-start(f32[128,128]{1,0:T(8,128)S(1)} %get-tuple-element.72), channel_id=1, source_target_pairs={{0,48},{8,56},{16,0},{24,8},{32,16},{40,24},{48,32},{56,40},{64,11... | collective-permute-start | bytes 196616 | tf_op jit(solution)/shard_map/ppermute | solution.py:480
  15.3 6.1 %collective-permute-start.6 = (f32[128,128]{1,0:T(8,128)S(1)}, f32[128,128]{1,0:T(8,128)S(1)}, u32[]{:S(2)}, u32[]{:S(2)}) collective-permute-start(f32[128,128]{1,0:T(8,128)S(1)} %get-tuple-element.80.own_ref), channel_id=1, source_target_pairs={{0,192},{8,200},{16,208},{24,216},{32,224},{40,232},{48,240},{56,2... | collective-permute-start | bytes 196616 | tf_op jit(solution)/shard_map/ppermute | solution.py:480
  17.5 4.7 %collective-permute-start.5 = (f32[128,128]{1,0:T(8,128)S(1)}, f32[128,128]{1,0:T(8,128)S(1)}, u32[]{:S(2)}, u32[]{:S(2)}) collective-permute-start(f32[128,128]{1,0:T(8,128)S(1)} %get-tuple-element.80.own_ref), channel_id=1, source_target_pairs={{0,128},{8,136},{16,144},{24,152},{32,160},{40,168},{48,176},{56,1... | collective-permute-start | bytes 196616 | tf_op jit(solution)/shard_map/ppermute | solution.py:480
  17.9 5.0 %collective-permute-start.4 = (f32[128,128]{1,0:T(8,128)S(1)}, f32[128,128]{1,0:T(8,128)S(1)}, u32[]{:S(2)}, u32[]{:S(2)}) collective-permute-start(f32[128,128]{1,0:T(8,128)S(1)} %get-tuple-element.80.own_ref), channel_id=1, source_target_pairs={{0,64},{8,72},{16,80},{24,88},{32,96},{40,104},{48,112},{56,120},{... | collective-permute-start | bytes 196616 | tf_op jit(solution)/shard_map/ppermute | solution.py:480
  23.5 6.2 %collective-permute-start.7 = (f32[128,128]{1,0:T(8,128)S(1)}, f32[128,128]{1,0:T(8,128)S(1)}, u32[]{:S(2)}, u32[]{:S(2)}) collective-permute-start(f32[128,128]{1,0:T(8,128)S(1)} %get-tuple-element.90), channel_id=1, source_target_pairs={{0,16},{8,24},{16,32},{24,40},{32,48},{40,56},{48,0},{56,8},{64,80... | collective-permute-start | bytes 196616 | tf_op jit(solution)/shard_map/ppermute | solution.py:480
  23.9 5.8 %collective-permute-start.8 = (f32[128,128]{1,0:T(8,128)S(1)}, f32[128,128]{1,0:T(8,128)S(1)}, u32[]{:S(2)}, u32[]{:S(2)}) collective-permute-start(f32[128,128]{1,0:T(8,128)S(1)} %get-tuple-element.91), channel_id=1, source_target_pairs={{0,32},{8,40},{16,48},{24,56},{32,0},{40,8},{48,16},{56,24},{64,96... | collective-permute-start | bytes 196616 | tf_op jit(solution)/shard_map/ppermute | solution.py:480
  26.6 10.2 %copy-start.1 = (f32[8,128]{1,0:T(8,128)S(1)}, f32[8,128]{1,0:T(8,128)}, u32[]{:S(2)}) copy-start(f32[8,128]{1,0:T(8,128)} %gain_ref.3) | copy-start | bytes 12292
  26.6 3.2 %collective-permute-start.9 = (f32[128,128]{1,0:T(8,128)S(1)}, f32[128,128]{1,0:T(8,128)S(1)}, u32[]{:S(2)}, u32[]{:S(2)}) collective-permute-start(f32[128,128]{1,0:T(8,128)S(1)} %get-tuple-element.92), channel_id=1, source_target_pairs={{0,48},{8,56},{16,0},{24,8},{32,16},{40,24},{48,32},{56,40},{64,11... | collective-permute-start | bytes 196616 | tf_op jit(solution)/shard_map/ppermute | solution.py:480
  30.4 6.4 %collective-permute-start.10 = (f32[4,128,128]{2,1,0:T(8,128)S(1)}, f32[4,128,128]{2,1,0:T(8,128)S(1)}, u32[]{:S(2)}, u32[]{:S(2)}) collective-permute-start(f32[4,128,128]{2,1,0:T(8,128)S(1)} %get-tuple-element.99), channel_id=1, source_target_pairs={{0,8},{8,0},{16,24},{24,16},{32,40},{40,32},{48,56},{56,48},{64,72... | collective-permute-start | bytes 786440 | tf_op jit(solution)/shard_map/ppermute | solution.py:480
  54.4 3.0 %collective-permute-start.11 = (f32[4,128,128]{2,1,0:T(8,128)S(1)}, f32[4,128,128]{2,1,0:T(8,128)S(1)}, u32[]{:S(2)}, u32[]{:S(2)}) collective-permute-start(f32[4,128,128]{2,1,0:T(8,128)S(1)} %get-tuple-element.105), channel_id=1, source_target_pairs={{0,8},{8,0},{16,24},{24,16},{32,40},{40,32},{48,56},{56,48},{64,72... | collective-permute-start | bytes 786440 | tf_op jit(solution)/shard_map/ppermute | solution.py:480
  58.0 6.2 %collective-permute-start.12 = (f32[128,128]{1,0:T(8,128)S(1)}, f32[128,128]{1,0:T(8,128)S(1)}, u32[]{:S(2)}, u32[]{:S(2)}) collective-permute-start(f32[128,128]{1,0:T(8,128)S(1)} %get-tuple-element.107), channel_id=1, source_target_pairs={{0,16},{8,24},{16,32},{24,40},{32,48},{40,56},{48,0},{56,8},{64,80... | collective-permute-start | bytes 196616 | tf_op jit(solution)/shard_map/ppermute | solution.py:480
  58.4 5.8 %collective-permute-start.13 = (f32[128,128]{1,0:T(8,128)S(1)}, f32[128,128]{1,0:T(8,128)S(1)}, u32[]{:S(2)}, u32[]{:S(2)}) collective-permute-start(f32[128,128]{1,0:T(8,128)S(1)} %get-tuple-element.108), channel_id=1, source_target_pairs={{0,32},{8,40},{16,48},{24,56},{32,0},{40,8},{48,16},{56,24},{64,96... | collective-permute-start | bytes 196616 | tf_op jit(solution)/shard_map/ppermute | solution.py:480
  60.6 3.8 %collective-permute-start.14 = (f32[128,128]{1,0:T(8,128)S(1)}, f32[128,128]{1,0:T(8,128)S(1)}, u32[]{:S(2)}, u32[]{:S(2)}) collective-permute-start(f32[128,128]{1,0:T(8,128)S(1)} %get-tuple-element.109), channel_id=1, source_target_pairs={{0,48},{8,56},{16,0},{24,8},{32,16},{40,24},{48,32},{56,40},{64,11... | collective-permute-start | bytes 196616 | tf_op jit(solution)/shard_map/ppermute | solution.py:480
  65.0 4.8 %collective-permute-start.17 = (f32[128,128]{1,0:T(8,128)S(1)}, f32[128,128]{1,0:T(8,128)S(1)}, u32[]{:S(2)}, u32[]{:S(2)}) collective-permute-start(f32[128,128]{1,0:T(8,128)S(1)} %get-tuple-element.114.own_ref), channel_id=1, source_target_pairs={{0,192},{8,200},{16,208},{24,216},{32,224},{40,232},{48,240},{56,2... | collective-permute-start | bytes 196616 | tf_op jit(solution)/shard_map/ppermute | solution.py:480
  65.3 4.6 %collective-permute-start.16 = (f32[128,128]{1,0:T(8,128)S(1)}, f32[128,128]{1,0:T(8,128)S(1)}, u32[]{:S(2)}, u32[]{:S(2)}) collective-permute-start(f32[128,128]{1,0:T(8,128)S(1)} %get-tuple-element.114.own_ref), channel_id=1, source_target_pairs={{0,128},{8,136},{16,144},{24,152},{32,160},{40,168},{48,176},{56,1... | collective-permute-start | bytes 196616 | tf_op jit(solution)/shard_map/ppermute | solution.py:480
  66.4 4.3 %collective-permute-start.15 = (f32[128,128]{1,0:T(8,128)S(1)}, f32[128,128]{1,0:T(8,128)S(1)}, u32[]{:S(2)}, u32[]{:S(2)}) collective-permute-start(f32[128,128]{1,0:T(8,128)S(1)} %get-tuple-element.114.own_ref), channel_id=1, source_target_pairs={{0,64},{8,72},{16,80},{24,88},{32,96},{40,104},{48,112},{56,120},{... | collective-permute-start | bytes 196616 | tf_op jit(solution)/shard_map/ppermute | solution.py:480
  71.3 7.6 %collective-permute-start.18 = (f32[128,128]{1,0:T(8,128)S(1)}, f32[128,128]{1,0:T(8,128)S(1)}, u32[]{:S(2)}, u32[]{:S(2)}) collective-permute-start(f32[128,128]{1,0:T(8,128)S(1)} %get-tuple-element.119), channel_id=1, source_target_pairs={{0,16},{8,24},{16,32},{24,40},{32,48},{40,56},{48,0},{56,8},{64,80... | collective-permute-start | bytes 196616 | tf_op jit(solution)/shard_map/ppermute | solution.py:480
  72.4 6.6 %collective-permute-start.19 = (f32[128,128]{1,0:T(8,128)S(1)}, f32[128,128]{1,0:T(8,128)S(1)}, u32[]{:S(2)}, u32[]{:S(2)}) collective-permute-start(f32[128,128]{1,0:T(8,128)S(1)} %get-tuple-element.120), channel_id=1, source_target_pairs={{0,32},{8,40},{16,48},{24,56},{32,0},{40,8},{48,16},{56,24},{64,96... | collective-permute-start | bytes 196616 | tf_op jit(solution)/shard_map/ppermute | solution.py:480
  75.0 4.0 %collective-permute-start.20 = (f32[128,128]{1,0:T(8,128)S(1)}, f32[128,128]{1,0:T(8,128)S(1)}, u32[]{:S(2)}, u32[]{:S(2)}) collective-permute-start(f32[128,128]{1,0:T(8,128)S(1)} %get-tuple-element.121), channel_id=1, source_target_pairs={{0,48},{8,56},{16,0},{24,8},{32,16},{40,24},{48,32},{56,40},{64,11... | collective-permute-start | bytes 196616 | tf_op jit(solution)/shard_map/ppermute | solution.py:480
  79.6 5.2 %collective-permute-start.21 = (f32[4,128,128]{2,1,0:T(8,128)S(1)}, f32[4,128,128]{2,1,0:T(8,128)S(1)}, u32[]{:S(2)}, u32[]{:S(2)}) collective-permute-start(f32[4,128,128]{2,1,0:T(8,128)S(1)} %get-tuple-element.130), channel_id=1, source_target_pairs={{0,8},{8,0},{16,24},{24,16},{32,40},{40,32},{48,56},{56,48},{64,72... | collective-permute-start | bytes 786440 | tf_op jit(solution)/shard_map/ppermute | solution.py:480

commit v5 on v4

v5 whole, which is shorter than its diff:
```python
import functools
import math

import jax
import jax.numpy as jnp
from jax import lax
from jax.experimental import pallas as pl
from jax.experimental.pallas import tpu as pltpu
from jax.sharding import PartitionSpec as P

F32 = jnp.float32
BF16 = jnp.bfloat16
LAYER_FACTOR = 1.0 - 78.0 / 79.0 + 1e-05
HEADS = 8
LENGTH = 512
SIZE = 128
HALF = 4
RING = 4
CHUNK = 128
PARTS = LENGTH // CHUNK
VMEM_LIMIT = 24 * 1024 * 1024

NN = ((1,), (0,))
NT = ((1,), (1,))
TN = ((0,), (0,))


def rate_of(rates_ref, head):
    return rates_ref[head][:1, :1]


def rows_of(shape, start=0):
    return (lax.broadcasted_iota(jnp.int32, shape, 0) + start).astype(F32)


def dot(a, b, dims):
    return lax.dot_general(a, b, (dims, ((), ())), preferred_element_type=F32)


def masks(rate, transposed=False):
    shape = (256, 256)
    gap = lax.broadcasted_iota(jnp.int32, shape, 0) - lax.broadcasted_iota(jnp.int32, shape, 1)
    if transposed:
        gap = -gap
    base = jnp.exp(-rate * gap.astype(F32))
    return jnp.where(gap >= 0, base, 0.0), base * jnp.exp(-256.0 * rate)


def hbm(x):
    return pltpu.with_memory_space_constraint(x, pltpu.HBM)


def near(x):
    return pltpu.with_memory_space_constraint(x, pltpu.VMEM)


def call(body, name, ins, outs, scratch=(), flops=0, moved=0, aliases=None):
    kinds = {"vmem": pltpu.VMEM, "hbm": pl.ANY}
    args, in_specs = [], []
    for kind, x in ins:
        in_specs.append(pl.BlockSpec(memory_space=kinds[kind]))
        args.append({"vmem": near, "hbm": hbm}[kind](x))
    out_shape, out_specs = [], []
    for kind, shape, dtype in outs:
        out_specs.append(pl.BlockSpec(memory_space=kinds[kind]))
        out_shape.append((pltpu.VMEM if kind == "vmem" else pltpu.HBM)(shape, dtype))
    return pl.pallas_call(
        body,
        in_specs=in_specs,
        out_specs=out_specs,
        out_shape=out_shape,
        scratch_shapes=list(scratch),
        input_output_aliases=aliases or {},
        compiler_params=pltpu.CompilerParams(vmem_limit_bytes=VMEM_LIMIT),
        cost_estimate=pl.CostEstimate(flops=flops, bytes_accessed=moved, transcendentals=0),
        name=name,
    )(*args)


STATE = (HEADS, SIZE, SIZE)
HALF_STATE = (HALF, SIZE, SIZE)
RATES = (HEADS, 8, SIZE)
WIDE = (LENGTH * HEADS, SIZE)
ONE = (SIZE, SIZE)
ROWS = (HEADS, LENGTH, SIZE)
WHOLE = (LENGTH, HEADS, SIZE)


def by_head(wide, part):
    return [wide[pl.ds(h + part * CHUNK * HEADS, CHUNK, stride=HEADS), :] for h in range(HEADS)]


def spread(wide, block, part):
    wide[pl.ds(part * CHUNK * HEADS, CHUNK * HEADS), :] = block.astype(F32).reshape(CHUNK * HEADS, SIZE)


def core_of():
    return lax.rem(lax.axis_index("ctx"), 2)


def x_of():
    return lax.rem(lax.axis_index("ctx") // 2, RING)


def y_of():
    return lax.axis_index("ctx") // (2 * RING)


def put(src, dst, part, sem):
    c = pltpu.make_async_copy(src.at[part], dst.at[part], sem)
    c.start()
    return c


def fetch_rows(src, dst, sems, base=0):
    return [put(src, dst, pl.ds(p * CHUNK, CHUNK), sems.at[base + p]) for p in range(PARTS)]


def wait_all(copies):
    for c in copies:
        c.wait()


def dma(count):
    return pltpu.SemaphoreType.DMA((count,))


def half_states(kw, vw, rates_ref, first_head, rows, left, s):
    start, count = rows
    for j in range(HALF):
        strided = pl.ds(first_head + j + start * HEADS, count, stride=HEADS)
        weight = jnp.exp(-rate_of(rates_ref, first_head + j) * left)
        part = dot((kw[strided, :] * weight).astype(BF16), vw[strided, :].astype(BF16), TN)
        s[j] = part if start == 0 else s[j] + part


def send_kernel(slope_hbm, k_hbm, v_hbm, send_ref, kw, vw, rates_ref, slope_ref, kin, vin, sems):
    first = pltpu.make_async_copy(slope_hbm, slope_ref, sems.at[2 * PARTS])
    first.start()
    k_copies = fetch_rows(k_hbm, kin, sems)
    v_copies = fetch_rows(v_hbm, vin, sems, PARTS)
    first.wait()
    for h in range(HEADS):
        slope = jnp.full((8, SIZE), slope_ref[h].astype(F32), F32)
        rates_ref[h] = jnp.exp((slope + 1.0) * (-8.0 / 64.0 * math.log(2.0))) * LAYER_FACTOR
    other = (1 - core_of()) * HALF
    for p in range(PARTS):
        rows = pl.ds(p * CHUNK, CHUNK)
        k_copies[p].wait()
        v_copies[p].wait()
        spread(kw, kin[rows], p)
        spread(vw, vin[rows], p)
        left = LENGTH - 1.0 - rows_of((CHUNK, SIZE), p * CHUNK)
        half_states(kw, vw, rates_ref, other, (p * CHUNK, CHUNK), left, send_ref)


def send_states(slope, k, v):
    whole = pltpu.VMEM(WHOLE, BF16)
    return call(
        send_kernel,
        "send_states",
        [("hbm", slope), ("hbm", k), ("hbm", v)],
        [("vmem", HALF_STATE, F32), ("vmem", WIDE, F32), ("vmem", WIDE, F32), ("vmem", RATES, F32)],
        [pltpu.SMEM((HEADS,), jnp.int32), whole, whole, dma(2 * PARTS + 1)],
    )


def keep_kernel(rates_ref, kw, vw, keep_ref):
    left = LENGTH - 1.0 - rows_of((LENGTH, SIZE))
    half_states(kw, vw, rates_ref, core_of() * HALF, (0, LENGTH), left, keep_ref)


def keep_states(rates, kw, vw):
    (out,) = call(
        keep_kernel,
        "keep_states",
        [("vmem", rates), ("vmem", kw), ("vmem", vw)],
        [("vmem", HALF_STATE, F32)],
        flops=2 * 10**9,
        moved=4 * 2**20,
    )
    return out


def turn_kernel(weigh, rates_ref, a_wide, b_hbm, *refs):
    if weigh:
        q_ref, a_ref, b_ref, wq_ref, b_in, wide, sems = refs
    else:
        a_ref, b_ref, b_in, wide, sems = refs
    copies = fetch_rows(b_hbm, b_in, sems)
    if weigh:
        done = rows_of((LENGTH, SIZE))
        for h in range(HEADS):
            wq_ref[h] = (q_ref[h].astype(F32) * jnp.exp(-rate_of(rates_ref, h) * done)).T.astype(BF16)
    for p in range(PARTS):
        rows = pl.ds(p * CHUNK, CHUNK)
        for h, block in enumerate(by_head(a_wide, p)):
            a_ref[h, rows, :] = block.astype(BF16)
    for p in range(PARTS):
        rows = pl.ds(p * CHUNK, CHUNK)
        copies[p].wait()
        spread(wide, b_in[rows], p)
        for h, block in enumerate(by_head(wide, p)):
            b_ref[h, rows, :] = block.astype(BF16)


def turn(rates, a_wide, b, q=None):
    weigh = q is not None
    return call(
        functools.partial(turn_kernel, weigh),
        "turn",
        [("vmem", rates), ("vmem", a_wide), ("hbm", b)] + ([("vmem", q)] if weigh else []),
        [("vmem", ROWS, BF16)] * 2 + ([("vmem", (HEADS, SIZE, LENGTH), BF16)] if weigh else []),
        [pltpu.VMEM(WHOLE, BF16), pltpu.VMEM(WIDE, F32), dma(PARTS)],
        moved=8 * 2**20,
    )


def local_kernel(rates_ref, q_ref, k_ref, v_ref, loc_ref):
    for h in range(HEADS):
        diag, off = masks(rate_of(rates_ref, h))
        q0, q1 = q_ref[h, :256], q_ref[h, 256:]
        k0, k1 = k_ref[h, :256], k_ref[h, 256:]
        v0, v1 = v_ref[h, :256], v_ref[h, 256:]
        a00 = (dot(q0, k0, NT) * diag).astype(BF16)
        a10 = (dot(q1, k0, NT) * off).astype(BF16)
        a11 = (dot(q1, k1, NT) * diag).astype(BF16)
        loc_ref[h, :256] = dot(a00, v0, NN)
        loc_ref[h, 256:] = dot(a10, v0, NN) + dot(a11, v1, NN)


def local_part(rates, q, k, v):
    (out,) = call(
        local_kernel,
        "local_part",
        [("vmem", rates), ("vmem", q), ("vmem", k), ("vmem", v)],
        [("vmem", ROWS, F32)],
        flops=2 * 10**9,
        moved=5 * 2**20,
    )
    return out


def decay_of(rates_ref, head, length):
    return jnp.exp(-float(length) * rate_of(rates_ref, head))


def around(place, d):
    return lax.rem(place + d + RING, RING)


def total_kernel(reverse, rates_ref, keep_ref, recv_ref, own_ref, to1, to2, to3, total):
    core, x = core_of(), x_of()
    flag = (core == 0) != reverse
    for h in range(HALF):
        decay = decay_of(rates_ref, core * HALF + h, LENGTH)
        total[h] = jnp.where(flag, decay, 1.0) * keep_ref[h] + jnp.where(flag, 1.0, decay) * recv_ref[h]
    own_ref[...] = total[x]
    for d, ref in ((1, to1), (2, to2), (3, to3)):
        ref[...] = total[around(x, d)]


def row_kernel(reverse, rates_ref, own_ref, from1, from2, from3, sum_ref, part_ref, held):
    x = x_of()
    decay = decay_of(rates_ref, core_of() * HALF + x, 2 * LENGTH)
    held[x] = own_ref[...]
    for d, ref in ((1, from1), (2, from2), (3, from3)):
        held[around(x, -d)] = ref[...]
    state = jnp.zeros(ONE, F32)
    for n in range(RING):
        place = RING - 1 - n if reverse else n
        part_ref[place] = state
        state = decay * state + held[place]
    sum_ref[...] = state


def column_kernel(reverse, rates_ref, own_ref, from1, from2, from3, part_ref, mine_ref, to1, to2, to3, held, done):
    x, y = x_of(), y_of()
    head = core_of() * HALF + x
    decay = decay_of(rates_ref, head, 2 * RING * LENGTH)
    held[y] = own_ref[...]
    for d, ref in ((1, from1), (2, from2), (3, from3)):
        held[around(y, -d)] = ref[...]
    state = jnp.zeros(ONE, F32)
    for n in range(RING - 1):
        place = RING - 1 - n if reverse else n
        before = place > y if reverse else place < y
        state = jnp.where(before, decay * state + held[place], state)
    for place in range(RING):
        steps = RING - 1 - place if reverse else place
        done[place] = decay_of(rates_ref, head, 2 * LENGTH * steps) * state + part_ref[place]
    mine_ref[...] = done[x]
    for d, ref in ((1, to1), (2, to2), (3, to3)):
        ref[...] = done[around(x, d)]


def after_kernel(reverse, rates_ref, own_ref, from1, from2, from3, keep_ref, recv_ref, out_ref, give_ref, held):
    core, x = core_of(), x_of()
    flag = (core == 0) != reverse
    held[x] = own_ref[...]
    for d, ref in ((1, from1), (2, from2), (3, from3)):
        held[around(x, -d)] = ref[...]
    for h in range(HALF):
        decay = decay_of(rates_ref, core * HALF + h, LENGTH)
        state = held[h]
        beyond = decay * state + jnp.where(flag, keep_ref[h], recv_ref[h])
        out_ref[h] = jnp.where(flag, state, beyond)
        give_ref[h] = jnp.where(flag, beyond, state)


def small(kernel, name, reverse, rates, ins, outs, scratch):
    return call(
        functools.partial(kernel, reverse),
        name,
        [("vmem", rates)] + [("vmem", a) for a in ins],
        [("vmem", shape, F32) for shape in outs],
        [pltpu.VMEM(shape, F32) for shape in scratch],
    )


def states_of(own_ref, other_ref, state):
    core = core_of()
    state[pl.ds(core * HALF, HALF)] = own_ref[...].astype(BF16)
    state[pl.ds((1 - core) * HALF, HALF)] = other_ref[...].astype(BF16)


def half_outputs(rates_ref, q_ref, u_ref, gain_ref, state_ref, loc, first_head, o_ref, sq, dt, fresh):
    done = rows_of((LENGTH, SIZE), 1)
    for j in range(HALF):
        h = first_head + j
        decay_in = jnp.exp(-rate_of(rates_ref, h) * done)
        o_ref[j] = loc[h] + decay_in * dot(q_ref[h], state_ref[j].astype(BF16), NN)
    for r in range(0, LENGTH, 32):
        rows = pl.ds(r, 32)
        square, product = (None, None) if fresh else (sq[rows, :], dt[rows, :])
        for j in range(HALF):
            h = first_head + j
            out = o_ref[j, rows, :]
            scaled = gain_ref[pl.ds(h, 1), :] * u_ref[h, rows, :].astype(F32)
            square = out * out if square is None else square + out * out
            product = out * scaled if product is None else product + out * scaled
        sq[rows, :] = square
        dt[rows, :] = product


def own_output_kernel(rates_ref, q_ref, u_ref, gain_ref, state_ref, loc, o_ref, sq, dt):
    half_outputs(rates_ref, q_ref, u_ref, gain_ref, state_ref, loc, core_of() * HALF, o_ref, sq, dt, True)


def other_output_kernel(rates_ref, q_ref, u_ref, gain_ref, state_ref, loc, sq_ref, dt_ref, o_ref, sums_ref, sq, dt, sums):
    sq[...] = sq_ref[...]
    dt[...] = dt_ref[...]
    first_head = (1 - core_of()) * HALF
    half_outputs(rates_ref, q_ref, u_ref, gain_ref, state_ref, loc, first_head, o_ref, sq, dt, False)
    for b in range(4):
        rows = slice(b * 128, (b + 1) * 128)
        sums[b : b + 1, :] = jnp.sum(sq[rows, :].T, axis=0, keepdims=True)
        sums[4 + b : 5 + b, :] = jnp.sum(dt[rows, :].T, axis=0, keepdims=True)
    for i in range(sums_ref.shape[0]):
        sums_ref[i] = sums[...]


HALF_ROWS = (HALF, LENGTH, SIZE)


def own_outputs(rates, q, u, gain, state, loc):
    return call(
        own_output_kernel,
        "own_outputs",
        [("vmem", a) for a in (rates, q, u, gain, state, loc)],
        [("vmem", HALF_ROWS, F32), ("vmem", (LENGTH, SIZE), F32), ("vmem", (LENGTH, SIZE), F32)],
        flops=10**9,
        moved=4 * 2**20,
    )


def other_outputs(rates, q, u, gain, state, loc, sq, dt, peers):
    total = pltpu.VMEM((LENGTH, SIZE), F32)
    return call(
        other_output_kernel,
        "other_outputs",
        [("vmem", a) for a in (rates, q, u, gain, state, loc, sq, dt)],
        [("vmem", HALF_ROWS, F32), ("vmem", (peers, 8, SIZE), F32)],
        [total, total, pltpu.VMEM((8, SIZE), F32)],
    )


def grad_kernel(sums_ref, wq_ref, u_ref, gain_ref, own_ref, other_ref, g, keep_ref, send_ref, acc):
    core = core_of()
    peers = sums_ref.shape[0]
    features = float(peers * HEADS * SIZE)
    sums = sums_ref[0]
    for i in range(1, peers):
        sums = sums + sums_ref[i]
    root = lax.rsqrt(sums[0:4, :] * (1.0 / features) + 1e-06)
    factor = root * root * root * sums[4:8, :] * (1.0 / features)
    for b in range(4):
        rows = pl.ds(b * 128, 128)
        inv = jnp.broadcast_to(root[b : b + 1, :], (128, 128)).T
        coef = jnp.broadcast_to(factor[b : b + 1, :], (128, 128)).T
        for side, o_ref in ((core, own_ref), (1 - core, other_ref)):
            for j in range(HALF):
                h = side * HALF + j
                scaled = gain_ref[pl.ds(h, 1), :] * u_ref[h, rows, :].astype(F32)
                g[h, rows, :] = (inv * scaled - o_ref[j, rows, :] * coef).astype(BF16)
    for h in range(HEADS):
        acc[h] = dot(wq_ref[h], g[h], NN)
    keep_ref[...] = acc[pl.ds(core * HALF, HALF)]
    send_ref[...] = acc[pl.ds((1 - core) * HALF, HALF)]


def grads(sums, wq, u, gain, own, other):
    return call(
        grad_kernel,
        "grads",
        [("vmem", sums), ("vmem", wq), ("vmem", u), ("vmem", gain), ("vmem", own), ("vmem", other)],
        [("vmem", ROWS, BF16), ("vmem", HALF_STATE, F32), ("vmem", HALF_STATE, F32)],
        [pltpu.VMEM(STATE, F32)],
    )


def query_kernel(rates_ref, g_ref, k_ref, v_ref, own_ref, other_ref, out_hbm, state, wide, block, sems):
    states_of(own_ref, other_ref, state)
    done = rows_of((LENGTH, SIZE), 1)
    for h in range(HEADS):
        rate = rate_of(rates_ref, h)
        diag, off = masks(rate)
        g0, g1 = g_ref[h, :256], g_ref[h, 256:]
        k0, k1 = k_ref[h, :256], k_ref[h, 256:]
        v0, v1 = v_ref[h, :256], v_ref[h, 256:]
        b00 = (dot(g0, v0, NT) * diag).astype(BF16)
        b10 = (dot(g1, v0, NT) * off).astype(BF16)
        b11 = (dot(g1, v1, NT) * diag).astype(BF16)
        carried = jnp.exp(-rate * done) * dot(g_ref[h], state[h], NT)
        wide[pl.ds(h, 256, stride=HEADS), :] = dot(b00, k0, NN) + carried[:256]
        wide[pl.ds(h + 256 * HEADS, 256, stride=HEADS), :] = (
            dot(b10, k0, NN) + dot(b11, k1, NN) + carried[256:]
        )
    copies = []
    for p in range(PARTS):
        rows = pl.ds(p * CHUNK, CHUNK)
        block[rows] = wide[pl.ds(p * CHUNK * HEADS, CHUNK * HEADS), :].reshape(CHUNK, HEADS, SIZE).astype(BF16)
        copies.append(put(block, out_hbm, rows, sems.at[p]))
    wait_all(copies)


def grad_query(rates, g, k, v, own, other):
    (out,) = call(
        query_kernel,
        "grad_query",
        [("vmem", rates), ("vmem", g), ("vmem", k), ("vmem", v), ("vmem", own), ("vmem", other)],
        [("hbm", WHOLE, BF16)],
        [
            pltpu.VMEM((HEADS, SIZE, SIZE), BF16),
            pltpu.VMEM((LENGTH * HEADS, SIZE), F32),
            pltpu.VMEM(WHOLE, BF16),
            dma(PARTS),
        ],
        flops=3 * 10**9,
        moved=5 * 2**20,
    )
    return out


def back_kernel(rates_ref, a_ref, b_ref, c_ref, out_ref):
    for h in range(HEADS):
        diag, off = masks(rate_of(rates_ref, h), True)
        a0, a1 = a_ref[h, :256], a_ref[h, 256:]
        b0, b1 = b_ref[h, :256], b_ref[h, 256:]
        c0, c1 = c_ref[h, :256], c_ref[h, 256:]
        t00 = (dot(a0, b0, NT) * diag).astype(BF16)
        t01 = (dot(a0, b1, NT) * off).astype(BF16)
        t11 = (dot(a1, b1, NT) * diag).astype(BF16)
        out_ref[h, :256] = (dot(t00, c0, NN) + dot(t01, c1, NN)).astype(BF16)
        out_ref[h, 256:] = dot(t11, c1, NN).astype(BF16)


def back(rates, a, b, c, name):
    (out,) = call(
        back_kernel,
        name,
        [("vmem", rates), ("vmem", a), ("vmem", b), ("vmem", c)],
        [("vmem", ROWS, BF16)],
        flops=2 * 10**9,
        moved=5 * 2**20,
    )
    return out


def half_finish(rates_ref, k, v, kl_ref, vl_ref, state_ref, first_head, wk, wv):
    left = LENGTH - rows_of((LENGTH, SIZE))
    for x, add, wide, dims in ((v, kl_ref, wk, NT), (k, vl_ref, wv, NN)):
        for j in range(HALF):
            h = first_head + j
            moved = jnp.exp(-rate_of(rates_ref, h) * left) * dot(x[h], state_ref[j].astype(BF16), dims)
            wide[pl.ds(h, LENGTH, stride=HEADS), :] = add[h].astype(F32) + moved
        yield


def own_finish_kernel(rates_ref, k, v, kl_ref, vl_ref, state_ref, wk, wv):
    for _ in half_finish(rates_ref, k, v, kl_ref, vl_ref, state_ref, core_of() * HALF, wk, wv):
        pass


def other_finish_kernel(rates_ref, k, v, kl_ref, vl_ref, state_ref, wk_in, wv_in, gk_hbm, gv_hbm, wk, wv, gk, gv, sems):
    writes = []
    sides = ((wk, gk, gk_hbm), (wv, gv, gv_hbm))
    halves = half_finish(rates_ref, k, v, kl_ref, vl_ref, state_ref, (1 - core_of()) * HALF, wk, wv)
    for n, _ in enumerate(halves):
        wide, out, to = sides[n]
        for p in range(PARTS):
            rows = pl.ds(p * CHUNK, CHUNK)
            flat = pl.ds(p * CHUNK * HEADS, CHUNK * HEADS)
            out[rows] = wide[flat, :].reshape(CHUNK, HEADS, SIZE).astype(BF16)
            writes.append(put(out, to, rows, sems.at[PARTS * n + p]))
    wait_all(writes)


def own_finish(rates, k, v, kl, vl, state):
    return call(
        own_finish_kernel,
        "own_finish",
        [("vmem", a) for a in (rates, k, v, kl, vl, state)],
        [("vmem", WIDE, F32), ("vmem", WIDE, F32)],
        flops=10**9,
        moved=8 * 2**20,
    )


def other_finish(rates, k, v, kl, vl, state, wk, wv):
    block = pltpu.VMEM(WHOLE, BF16)
    return call(
        other_finish_kernel,
        "other_finish",
        [("vmem", a) for a in (rates, k, v, kl, vl, state, wk, wv)],
        [("hbm", WHOLE, BF16), ("hbm", WHOLE, BF16), ("vmem", WIDE, F32), ("vmem", WIDE, F32)],
        [block, block, dma(2 * PARTS)],
        aliases={6: 2, 7: 3},
    )[:2]


def permute(a, dy, dx, dc):
    pairs = []
    for y in range(RING):
        for x in range(RING):
            for c in range(2):
                to = ((y + dy) % RING * RING + (x + dx) % RING) * 2 + (c ^ dc)
                pairs.append(((y * RING + x) * 2 + c, to))
    return lax.ppermute(a, "ctx", pairs)


def exchange(a):
    return permute(a, 0, 0, 1)


def along_x(parts):
    return [permute(a, 0, d + 1, 0) for d, a in enumerate(parts)]


def along_y(a):
    return [permute(a, d, 0, 0) for d in (1, 2, 3)]


def beside(moved, work):
    out = lax.optimization_barrier((tuple(moved), tuple(work)))
    return list(out[0]), list(out[1])


def scan(rates, keep, send, reverse, first, second, third, last):
    recv = exchange(send)
    recv, keep = lax.optimization_barrier((recv, keep()))
    one = [ONE] * 4
    own, *parts = small(total_kernel, "chip_total", reverse, rates, [keep, recv], one, [HALF_STATE])
    moved = along_x(parts)
    moved, done1 = beside(moved, first())
    row, part = small(row_kernel, "row_sum", reverse, rates, [own, *moved], [ONE, HALF_STATE], [HALF_STATE])
    moved = along_y(row)
    moved, done2 = beside(moved, second(done1))
    own, *parts = small(
        column_kernel, "column_sum", reverse, rates, [row, *moved, part], one, [HALF_STATE, HALF_STATE]
    )
    moved = along_x(parts)
    moved, done3 = beside(moved, third(done1, done2))
    mine, give = small(
        after_kernel, "after", reverse, rates, [own, *moved, keep, recv], [HALF_STATE] * 2, [HALF_STATE]
    )
    (other,), done4 = beside([exchange(give)], last(mine, done1, done2, done3))
    return mine, other, done1, done2, done3, done4


def on_device(queries, key_rows, value_rows, upstream, norm_gain, slope_index):
    send, kw, vw, rates = send_states(slope_index, key_rows, value_rows)
    e_own, e_other, (kh, qh), (vh, uh, wq), (loc,), (out_own, sq, dt) = scan(
        rates,
        lambda: keep_states(rates, kw, vw),
        send,
        False,
        lambda: turn(rates, kw, queries),
        lambda a: turn(rates, vw, upstream, a[1]),
        lambda a, b: [local_part(rates, a[1], a[0], b[0])],
        lambda e, a, b, c: own_outputs(rates, a[1], b[1], norm_gain, e, c[0]),
    )

    peers = lax.axis_size("head")
    out_other, sums = other_outputs(rates, qh, uh, norm_gain, e_other, loc, sq, dt, peers)
    sums = lax.all_to_all(sums, "head", 0, 0, tiled=True)
    g, keep, send = grads(sums, wq, uh, norm_gain, out_own, out_other)

    l_own, l_other, (gv_local,), (gk_local,), (gq,), (wk, wv) = scan(
        rates,
        lambda: keep,
        send,
        True,
        lambda: [back(rates, kh, qh, g, "gv_local")],
        lambda a: [back(rates, vh, g, qh, "gk_local")],
        lambda a, b: [grad_query(rates, g, kh, vh, e_own, e_other)],
        lambda l, a, b, c: own_finish(rates, kh, vh, b[0], a[0], l),
    )
    gk, gv = other_finish(rates, kh, vh, gk_local, gv_local, l_other, wk, wv)
    return gq, gk, gv


def solution(mesh):
    rows = P("ctx", "head", None)
    return jax.shard_map(
        on_device,
        mesh=mesh,
        in_specs=(rows, rows, rows, rows, P("head", None), P("head")),
        out_specs=(rows, rows, rows),
        check_vma=False,
    )
```

time: 88.2 us -> 81.7 us (0.926)
  Pallas kernels: 30.7 us -> 22.4 us
  waiting for transfers between devices: 7.9 us -> 9.22 us
    pallas_call x18 -> x21, Pallas kernels: 30.7 us -> 22.4 us  [call(): pl.pallas_call(body, in_specs=in_specs, out_specs=out_specs, out_shape=ou...]
    ppermute x22, waiting for transfers between devices: 7.9 us -> 9.22 us  [permute(): return lax.ppermute(a, 'ctx', pairs)]
  transfers between devices with their start and end apart: 22 -> 22, of which waited for: 11 -> 13; matrix products, arithmetic and copies ran while one was open for 0% -> 0% of each run, Pallas kernels for 20% -> 19%
where the time goes in v5:
time: 81.7 us; the launch traced here: 81.6 us
  starting transfers between devices  34 us (42%)
  Pallas kernels  22.4 us (27%)
  blocking collectives  14.9 us (18%)
  waiting for transfers between devices  9.22 us (11%)
  between operations  1.05 us (1%)
    ppermute x22, starting transfers between devices, permute(): return lax.ppermute(a, 'ctx', pairs)  34 us
    pallas_call x21, Pallas kernels, call(): pl.pallas_call(body, in_specs=in_specs, out_specs=out_specs, out_shape=ou...  22.4 us
    all_to_all x1, blocking collectives, on_device(): sums = lax.all_to_all(sums, 'head', 0, 0, tiled=True)  14.9 us
    ppermute x22, waiting for transfers between devices, permute(): return lax.ppermute(a, 'ctx', pairs)  9.22 us
  transfers between devices with their start and end apart: 22, of which 13 were waited for; matrix products, arithmetic and copies ran while one was open for 0% of the time, Pallas kernels for 19%

profile of v5, /device:TPU:1, one launch (start us, length us, event | category | flops | bytes accessed | tf_op | source)
XLA Modules:
  0.0 81.6 jit_solution(14529215792341379437)
XLA Ops:
  0.6 2.5 %send_states.1 = (f32[4,128,128]{2,1,0:T(8,128)S(1)}, f32[4096,128]{1,0:T(8,128)S(1)}, f32[4096,128]{1,0:T(8,128)S(1)}, f32[8,8,128]{2,1,0:T(8,128)S(1)}) custom-call(s32[8]{0:T(128)} %slope_hbm.1, bf16[512,8,128]{2,1,0:T(8,128)(2,1)} %k_hbm.1, bf16[512,8,128]{2,1,0:T(8,128)(2,1)} %v_hbm.1), custom_call_target="tpu_custom_call" | custom-call | tf_op jit(solution)/shard_map/send_states/pallas_call | solution.py:67
  3.1 3.3 %collective-permute-start = (f32[4,128,128]{2,1,0:T(8,128)S(1)}, f32[4,128,128]{2,1,0:T(8,128)S(1)}, u32[]{:S(2)}, u32[]{:S(2)}) collective-permute-start(f32[4,128,128]{2,1,0:T(8,128)S(1)} %get-tuple-element.87), channel_id=1, source_target_pairs={{0,8},{8,0},{16,24},{24,16},{32,40},{40,32},{48,56},{56,48},{64,72... | collective-permute-start | bytes 786440 | tf_op jit(solution)/shard_map/ppermute | solution.py:549
  6.4 0.7 keep_states.1.keep_ref
  7.8 1.9 %collective-permute-start.2 = (f32[128,128]{1,0:T(8,128)S(1)}, f32[128,128]{1,0:T(8,128)S(1)}, u32[]{:S(2)}, u32[]{:S(2)}) collective-permute-start(f32[128,128]{1,0:T(8,128)S(1)} %get-tuple-element.93), channel_id=1, source_target_pairs={{0,32},{8,40},{16,48},{24,56},{32,0},{40,8},{48,16},{56,24},{64,96... | collective-permute-start | bytes 196616 | tf_op jit(solution)/shard_map/ppermute | solution.py:549
  9.7 1.2 %collective-permute-start.3 = (f32[128,128]{1,0:T(8,128)S(1)}, f32[128,128]{1,0:T(8,128)S(1)}, u32[]{:S(2)}, u32[]{:S(2)}) collective-permute-start(f32[128,128]{1,0:T(8,128)S(1)} %get-tuple-element.94), channel_id=1, source_target_pairs={{0,48},{8,56},{16,0},{24,8},{32,16},{40,24},{48,32},{56,40},{64,11... | collective-permute-start | bytes 196616 | tf_op jit(solution)/shard_map/ppermute | solution.py:549
  10.9 1.4 %turn.2 = (bf16[8,512,128]{2,1,0:T(8,128)(2,1)S(1)}, bf16[8,512,128]{2,1,0:T(8,128)(2,1)S(1)}) custom-call(f32[8,8,128]{2,1,0:T(8,128)S(1)} %get-tuple-element.86.rates_ref, f32[4096,128]{1,0:T(8,128)S(1)} %get-tuple-element.88.kw.a_wide, bf16[512,8,128]{2,1,0:T(8,128)(2,1)} %b_hbm.2), custom_call_target="tpu_custom_call" | custom-call | bytes 8388608 | tf_op jit(solution)/shard_map/turn/pallas_call | solution.py:67
  14.1 2.0 %collective-permute-start.6 = (f32[128,128]{1,0:T(8,128)S(1)}, f32[128,128]{1,0:T(8,128)S(1)}, u32[]{:S(2)}, u32[]{:S(2)}) collective-permute-start(f32[128,128]{1,0:T(8,128)S(1)} %get-tuple-element.102.own_ref), channel_id=1, source_target_pairs={{0,192},{8,200},{16,208},{24,216},{32,224},{40,232},{48,240},{56,2... | collective-permute-start | bytes 196616 | tf_op jit(solution)/shard_map/ppermute | solution.py:549
  16.4 0.7 collective-permute-start.4
  17.1 1.8 %turn.3 = (bf16[8,512,128]{2,1,0:T(8,128)(2,1)S(1)}, bf16[8,512,128]{2,1,0:T(8,128)(2,1)S(1)}, bf16[8,128,512]{2,1,0:T(8,128)(2,1)S(1)}) custom-call(f32[8,8,128]{2,1,0:T(8,128)S(1)} %get-tuple-element.86.rates_ref, f32[4096,128]{1,0:T(8,128)S(1)} %get-tuple-element.89.vw.a_wide, bf16[512,8,128]{2,1,0:T(8,128)(2,1)} %b_hbm.3, ...), custom_call_target="tpu_custom_call" | custom-call | bytes 8388608 | tf_op jit(solution)/shard_map/turn/pallas_call | solution.py:67
  18.9 1.8 %collective-permute-done.5.from2 = f32[128,128]{1,0:T(8,128)S(1)} collective-permute-done((f32[128,128]{1,0:T(8,128)S(1)}, f32[128,128]{1,0:T(8,128)S(1)}, u32[]{:S(2)}, u32[]{:S(2)}) %collective-permute-start.5) | collective-permute-done | bytes 65568 | tf_op jit(solution)/shard_map/ppermute | solution.py:549
  21.6 3.2 %collective-permute-start.8 = (f32[128,128]{1,0:T(8,128)S(1)}, f32[128,128]{1,0:T(8,128)S(1)}, u32[]{:S(2)}, u32[]{:S(2)}) collective-permute-start(f32[128,128]{1,0:T(8,128)S(1)} %get-tuple-element.113), channel_id=1, source_target_pairs={{0,32},{8,40},{16,48},{24,56},{32,0},{40,8},{48,16},{56,24},{64,96... | collective-permute-start | bytes 196616 | tf_op jit(solution)/shard_map/ppermute | solution.py:549
  25.2 2.3 %local_part.1.loc = f32[8,512,128]{2,1,0:T(8,128)S(1)} custom-call(f32[8,8,128]{2,1,0:T(8,128)S(1)} %get-tuple-element.86.rates_ref, bf16[8,512,128]{2,1,0:T(8,128)(2,1)S(1)} %get-tuple-element.97.refs_0_.q_ref.b_ref.c_ref, bf16[8,512,128]{2,1,0:T(8,128)(2,1)S(1)} %get-tuple-element.115.k_ref.a_ref.k, bf16[8,512,128]{2,1,0:T(8,128)(2,1)S(1)} %get-tuple-element.116.v_ref.a_ref.v), custom_call_target="tpu_custom_call" | custom-call | flops 2000000000 | bytes 5242880 | tf_op jit(solution)/shard_map/local_part/pallas_call | solution.py:67
  28.1 5.3 %collective-permute-start.10 = (f32[4,128,128]{2,1,0:T(8,128)S(1)}, f32[4,128,128]{2,1,0:T(8,128)S(1)}, u32[]{:S(2)}, u32[]{:S(2)}) collective-permute-start(f32[4,128,128]{2,1,0:T(8,128)S(1)} %get-tuple-element.120), channel_id=1, source_target_pairs={{0,8},{8,0},{16,24},{24,16},{32,40},{40,32},{48,56},{56,48},{64,72... | collective-permute-start | bytes 786440 | tf_op jit(solution)/shard_map/ppermute | solution.py:549
  33.9 0.7 collective-permute-done.10.state_ref.other_ref
  35.1 14.9 %all_to_all.5.sums_ref = f32[8,8,128]{2,1,0:T(8,128)S(1)} all-to-all(f32[8,8,128]{2,1,0:T(8,128)S(1)} %get-tuple-element.129), channel_id=1, replica_groups=mesh['ctx'=32,'head'=8] {'head'}, dimensions={0} | all-to-all | bytes 65536 | tf_op jit(solution)/shard_map/all_to_all | solution.py:606
  50.1 1.0 %grads.1 = (bf16[8,512,128]{2,1,0:T(8,128)(2,1)S(1)}, f32[4,128,128]{2,1,0:T(8,128)S(1)}, f32[4,128,128]{2,1,0:T(8,128)S(1)}) custom-call(f32[8,8,128]{2,1,0:T(8,128)S(1)} %all_to_all.5.sums_ref, bf16[8,128,512]{2,1,0:T(8,128)(2,1)S(1)} %get-tuple-element.130.wq_ref, bf16[8,512,128]{2,1,0:T(8,128)(2,1)S(1)} %get-tuple-element.106.u_ref, ...), custom_call_target="tpu_custom_call" | custom-call | tf_op jit(solution)/shard_map/grads/pallas_call | solution.py:67
  51.1 1.8 %collective-permute-start.11 = (f32[4,128,128]{2,1,0:T(8,128)S(1)}, f32[4,128,128]{2,1,0:T(8,128)S(1)}, u32[]{:S(2)}, u32[]{:S(2)}) collective-permute-start(f32[4,128,128]{2,1,0:T(8,128)S(1)} %get-tuple-element.133), channel_id=1, source_target_pairs={{0,8},{8,0},{16,24},{24,16},{32,40},{40,32},{48,56},{56,48},{64,72... | collective-permute-start | bytes 786440 | tf_op jit(solution)/shard_map/ppermute | solution.py:549
  52.8 1.2 %collective-permute-done.11.recv_ref = f32[4,128,128]{2,1,0:T(8,128)S(1)} collective-permute-done((f32[4,128,128]{2,1,0:T(8,128)S(1)}, f32[4,128,128]{2,1,0:T(8,128)S(1)}, u32[]{:S(2)}, u32[]{:S(2)}) %collective-permute-start.11) | collective-permute-done | bytes 262176 | tf_op jit(solution)/shard_map/ppermute | solution.py:549
  54.2 2.5 %collective-permute-start.13 = (f32[128,128]{1,0:T(8,128)S(1)}, f32[128,128]{1,0:T(8,128)S(1)}, u32[]{:S(2)}, u32[]{:S(2)}) collective-permute-start(f32[128,128]{1,0:T(8,128)S(1)} %get-tuple-element.139), channel_id=1, source_target_pairs={{0,32},{8,40},{16,48},{24,56},{32,0},{40,8},{48,16},{56,24},{64,96... | collective-permute-start | bytes 196616 | tf_op jit(solution)/shard_map/ppermute | solution.py:549
  56.7 0.8 collective-permute-start.14
  57.5 2.3 %gv_local.1.vl_ref = bf16[8,512,128]{2,1,0:T(8,128)(2,1)S(1)} custom-call(f32[8,8,128]{2,1,0:T(8,128)S(1)} %get-tuple-element.86.rates_ref, bf16[8,512,128]{2,1,0:T(8,128)(2,1)S(1)} %get-tuple-element.115.k_ref.a_ref.k, bf16[8,512,128]{2,1,0:T(8,128)(2,1)S(1)} %get-tuple-element.97.refs_0_.q_ref.b_ref.c_ref, ...), custom_call_target="tpu_custom_call" | custom-call | flops 2000000000 | bytes 5242880 | tf_op jit(solution)/shard_map/gv_local/pallas_call | solution.py:67
  60.9 0.9 %collective-permute-start.16 = (f32[128,128]{1,0:T(8,128)S(1)}, f32[128,128]{1,0:T(8,128)S(1)}, u32[]{:S(2)}, u32[]{:S(2)}) collective-permute-start(f32[128,128]{1,0:T(8,128)S(1)} %get-tuple-element.145.own_ref), channel_id=1, source_target_pairs={{0,128},{8,136},{16,144},{24,152},{32,160},{40,168},{48,176},{56,1... | collective-permute-start | bytes 196616 | tf_op jit(solution)/shard_map/ppermute | solution.py:549
  61.8 0.8 collective-permute-start.15
  62.6 2.3 %gk_local.1.kl_ref = bf16[8,512,128]{2,1,0:T(8,128)(2,1)S(1)} custom-call(f32[8,8,128]{2,1,0:T(8,128)S(1)} %get-tuple-element.86.rates_ref, bf16[8,512,128]{2,1,0:T(8,128)(2,1)S(1)} %get-tuple-element.116.v_ref.a_ref.v, bf16[8,512,128]{2,1,0:T(8,128)(2,1)S(1)} %get-tuple-element.141.c_ref.b_ref.g_ref, ...), custom_call_target="tpu_custom_call" | custom-call | flops 2000000000 | bytes 5242880 | tf_op jit(solution)/shard_map/gk_local/pallas_call | solution.py:67
  64.9 0.7 collective-permute-done.16.from2
  65.6 0.7 collective-permute-done.15.from1
  66.4 1.0 %collective-permute-start.18 = (f32[128,128]{1,0:T(8,128)S(1)}, f32[128,128]{1,0:T(8,128)S(1)}, u32[]{:S(2)}, u32[]{:S(2)}) collective-permute-start(f32[128,128]{1,0:T(8,128)S(1)} %get-tuple-element.150), channel_id=1, source_target_pairs={{0,16},{8,24},{16,32},{24,40},{32,48},{40,56},{48,0},{56,8},{64,80... | collective-permute-start | bytes 196616 | tf_op jit(solution)/shard_map/ppermute | solution.py:549
  67.4 2.6 %collective-permute-start.19 = (f32[128,128]{1,0:T(8,128)S(1)}, f32[128,128]{1,0:T(8,128)S(1)}, u32[]{:S(2)}, u32[]{:S(2)}) collective-permute-start(f32[128,128]{1,0:T(8,128)S(1)} %get-tuple-element.151), channel_id=1, source_target_pairs={{0,32},{8,40},{16,48},{24,56},{32,0},{40,8},{48,16},{56,24},{64,96... | collective-permute-start | bytes 196616 | tf_op jit(solution)/shard_map/ppermute | solution.py:549
  70.0 3.3 %grad_query.1 = bf16[512,8,128]{2,1,0:T(8,128)(2,1)} custom-call(f32[8,8,128]{2,1,0:T(8,128)S(1)} %get-tuple-element.86.rates_ref, bf16[8,512,128]{2,1,0:T(8,128)(2,1)S(1)} %get-tuple-element.141.c_ref.b_ref.g_ref, bf16[8,512,128]{2,1,0:T(8,128)(2,1)S(1)} %get-tuple-element.115.k_ref.a_ref.k, bf16[8,512,128]{2,1,0:T(8,128)(2,1)S(1)} %get-tuple-element.116.v_ref.a_ref.v, ...), custom_call_target="tpu_custom_call" | custom-call | flops 3000000000 | bytes 5242880 | tf_op jit(solution)/shard_map/grad_query/pallas_call | solution.py:67
  73.5 4.7 %collective-permute-start.21 = (f32[4,128,128]{2,1,0:T(8,128)S(1)}, f32[4,128,128]{2,1,0:T(8,128)S(1)}, u32[]{:S(2)}, u32[]{:S(2)}) collective-permute-start(f32[4,128,128]{2,1,0:T(8,128)S(1)} %get-tuple-element.160), channel_id=1, source_target_pairs={{0,8},{8,0},{16,24},{24,16},{32,40},{40,32},{48,56},{56,48},{64,72... | collective-permute-start | bytes 786440 | tf_op jit(solution)/shard_map/ppermute | solution.py:549
  78.2 0.7 own_finish.1
  79.3 2.1 %other_finish.1 = (bf16[512,8,128]{2,1,0:T(8,128)(2,1)}, bf16[512,8,128]{2,1,0:T(8,128)(2,1)}, f32[4096,128]{1,0:T(8,128)S(1)}, f32[4096,128]{1,0:T(8,128)S(1)}) custom-call(f32[8,8,128]{2,1,0:T(8,128)S(1)} %get-tuple-element.86.rates_ref, bf16[8,512,128]{2,1,0:T(8,128)(2,1)S(1)} %get-tuple-element.115.k_ref.a_ref.k, ...), custom_call_target="tpu_custom_call", output_to_operand_aliasing={{2}: (6, {}), {3}: (7, {})} | custom-call | tf_op jit(solution)/shard_map/other_finish/pallas_call | solution.py:67
  (36 shorter events, 7.6 us)
Async XLA Ops:
  3.1 4.5 %collective-permute-start = (f32[4,128,128]{2,1,0:T(8,128)S(1)}, f32[4,128,128]{2,1,0:T(8,128)S(1)}, u32[]{:S(2)}, u32[]{:S(2)}) collective-permute-start(f32[4,128,128]{2,1,0:T(8,128)S(1)} %get-tuple-element.87), channel_id=1, source_target_pairs={{0,8},{8,0},{16,24},{24,16},{32,40},{40,32},{48,56},{56,48},{64,72... | collective-permute-start | bytes 786440 | tf_op jit(solution)/shard_map/ppermute | solution.py:549
  7.7 5.2 %collective-permute-start.1 = (f32[128,128]{1,0:T(8,128)S(1)}, f32[128,128]{1,0:T(8,128)S(1)}, u32[]{:S(2)}, u32[]{:S(2)}) collective-permute-start(f32[128,128]{1,0:T(8,128)S(1)} %get-tuple-element.92), channel_id=1, source_target_pairs={{0,16},{8,24},{16,32},{24,40},{32,48},{40,56},{48,0},{56,8},{64,80... | collective-permute-start | bytes 196616 | tf_op jit(solution)/shard_map/ppermute | solution.py:549
  7.8 5.7 %collective-permute-start.2 = (f32[128,128]{1,0:T(8,128)S(1)}, f32[128,128]{1,0:T(8,128)S(1)}, u32[]{:S(2)}, u32[]{:S(2)}) collective-permute-start(f32[128,128]{1,0:T(8,128)S(1)} %get-tuple-element.93), channel_id=1, source_target_pairs={{0,32},{8,40},{16,48},{24,56},{32,0},{40,8},{48,16},{56,24},{64,96... | collective-permute-start | bytes 196616 | tf_op jit(solution)/shard_map/ppermute | solution.py:549
  9.7 4.2 %collective-permute-start.3 = (f32[128,128]{1,0:T(8,128)S(1)}, f32[128,128]{1,0:T(8,128)S(1)}, u32[]{:S(2)}, u32[]{:S(2)}) collective-permute-start(f32[128,128]{1,0:T(8,128)S(1)} %get-tuple-element.94), channel_id=1, source_target_pairs={{0,48},{8,56},{16,0},{24,8},{32,16},{40,24},{48,32},{56,40},{64,11... | collective-permute-start | bytes 196616 | tf_op jit(solution)/shard_map/ppermute | solution.py:549
  14.1 4.9 %collective-permute-start.6 = (f32[128,128]{1,0:T(8,128)S(1)}, f32[128,128]{1,0:T(8,128)S(1)}, u32[]{:S(2)}, u32[]{:S(2)}) collective-permute-start(f32[128,128]{1,0:T(8,128)S(1)} %get-tuple-element.102.own_ref), channel_id=1, source_target_pairs={{0,192},{8,200},{16,208},{24,216},{32,224},{40,232},{48,240},{56,2... | collective-permute-start | bytes 196616 | tf_op jit(solution)/shard_map/ppermute | solution.py:549
  16.0 4.7 %collective-permute-start.5 = (f32[128,128]{1,0:T(8,128)S(1)}, f32[128,128]{1,0:T(8,128)S(1)}, u32[]{:S(2)}, u32[]{:S(2)}) collective-permute-start(f32[128,128]{1,0:T(8,128)S(1)} %get-tuple-element.102.own_ref), channel_id=1, source_target_pairs={{0,128},{8,136},{16,144},{24,152},{32,160},{40,168},{48,176},{56,1... | collective-permute-start | bytes 196616 | tf_op jit(solution)/shard_map/ppermute | solution.py:549
  16.4 5.0 %collective-permute-start.4 = (f32[128,128]{1,0:T(8,128)S(1)}, f32[128,128]{1,0:T(8,128)S(1)}, u32[]{:S(2)}, u32[]{:S(2)}) collective-permute-start(f32[128,128]{1,0:T(8,128)S(1)} %get-tuple-element.102.own_ref), channel_id=1, source_target_pairs={{0,64},{8,72},{16,80},{24,88},{32,96},{40,104},{48,112},{56,120},{... | collective-permute-start | bytes 196616 | tf_op jit(solution)/shard_map/ppermute | solution.py:549
  21.5 6.0 %collective-permute-start.7 = (f32[128,128]{1,0:T(8,128)S(1)}, f32[128,128]{1,0:T(8,128)S(1)}, u32[]{:S(2)}, u32[]{:S(2)}) collective-permute-start(f32[128,128]{1,0:T(8,128)S(1)} %get-tuple-element.112), channel_id=1, source_target_pairs={{0,16},{8,24},{16,32},{24,40},{32,48},{40,56},{48,0},{56,8},{64,80... | collective-permute-start | bytes 196616 | tf_op jit(solution)/shard_map/ppermute | solution.py:549
  21.6 6.0 %collective-permute-start.8 = (f32[128,128]{1,0:T(8,128)S(1)}, f32[128,128]{1,0:T(8,128)S(1)}, u32[]{:S(2)}, u32[]{:S(2)}) collective-permute-start(f32[128,128]{1,0:T(8,128)S(1)} %get-tuple-element.113), channel_id=1, source_target_pairs={{0,32},{8,40},{16,48},{24,56},{32,0},{40,8},{48,16},{56,24},{64,96... | collective-permute-start | bytes 196616 | tf_op jit(solution)/shard_map/ppermute | solution.py:549
  24.8 8.6 %copy-start = (f32[8,128]{1,0:T(8,128)S(1)}, f32[8,128]{1,0:T(8,128)}, u32[]{:S(2)}) copy-start(f32[8,128]{1,0:T(8,128)} %gain_ref.5) | copy-start | bytes 12292
  24.8 3.1 %collective-permute-start.9 = (f32[128,128]{1,0:T(8,128)S(1)}, f32[128,128]{1,0:T(8,128)S(1)}, u32[]{:S(2)}, u32[]{:S(2)}) collective-permute-start(f32[128,128]{1,0:T(8,128)S(1)} %get-tuple-element.114), channel_id=1, source_target_pairs={{0,48},{8,56},{16,0},{24,8},{32,16},{40,24},{48,32},{56,40},{64,11... | collective-permute-start | bytes 196616 | tf_op jit(solution)/shard_map/ppermute | solution.py:549
  28.1 6.5 %collective-permute-start.10 = (f32[4,128,128]{2,1,0:T(8,128)S(1)}, f32[4,128,128]{2,1,0:T(8,128)S(1)}, u32[]{:S(2)}, u32[]{:S(2)}) collective-permute-start(f32[4,128,128]{2,1,0:T(8,128)S(1)} %get-tuple-element.120), channel_id=1, source_target_pairs={{0,8},{8,0},{16,24},{24,16},{32,40},{40,32},{48,56},{56,48},{64,72... | collective-permute-start | bytes 786440 | tf_op jit(solution)/shard_map/ppermute | solution.py:549
  51.1 2.9 %collective-permute-start.11 = (f32[4,128,128]{2,1,0:T(8,128)S(1)}, f32[4,128,128]{2,1,0:T(8,128)S(1)}, u32[]{:S(2)}, u32[]{:S(2)}) collective-permute-start(f32[4,128,128]{2,1,0:T(8,128)S(1)} %get-tuple-element.133), channel_id=1, source_target_pairs={{0,8},{8,0},{16,24},{24,16},{32,40},{40,32},{48,56},{56,48},{64,72... | collective-permute-start | bytes 786440 | tf_op jit(solution)/shard_map/ppermute | solution.py:549
  54.1 5.7 %collective-permute-start.12 = (f32[128,128]{1,0:T(8,128)S(1)}, f32[128,128]{1,0:T(8,128)S(1)}, u32[]{:S(2)}, u32[]{:S(2)}) collective-permute-start(f32[128,128]{1,0:T(8,128)S(1)} %get-tuple-element.138), channel_id=1, source_target_pairs={{0,16},{8,24},{16,32},{24,40},{32,48},{40,56},{48,0},{56,8},{64,80... | collective-permute-start | bytes 196616 | tf_op jit(solution)/shard_map/ppermute | solution.py:549
  54.2 5.6 %collective-permute-start.13 = (f32[128,128]{1,0:T(8,128)S(1)}, f32[128,128]{1,0:T(8,128)S(1)}, u32[]{:S(2)}, u32[]{:S(2)}) collective-permute-start(f32[128,128]{1,0:T(8,128)S(1)} %get-tuple-element.139), channel_id=1, source_target_pairs={{0,32},{8,40},{16,48},{24,56},{32,0},{40,8},{48,16},{56,24},{64,96... | collective-permute-start | bytes 196616 | tf_op jit(solution)/shard_map/ppermute | solution.py:549
  56.7 3.8 %collective-permute-start.14 = (f32[128,128]{1,0:T(8,128)S(1)}, f32[128,128]{1,0:T(8,128)S(1)}, u32[]{:S(2)}, u32[]{:S(2)}) collective-permute-start(f32[128,128]{1,0:T(8,128)S(1)} %get-tuple-element.140), channel_id=1, source_target_pairs={{0,48},{8,56},{16,0},{24,8},{32,16},{40,24},{48,32},{56,40},{64,11... | collective-permute-start | bytes 196616 | tf_op jit(solution)/shard_map/ppermute | solution.py:549
  60.6 4.3 %collective-permute-start.17 = (f32[128,128]{1,0:T(8,128)S(1)}, f32[128,128]{1,0:T(8,128)S(1)}, u32[]{:S(2)}, u32[]{:S(2)}) collective-permute-start(f32[128,128]{1,0:T(8,128)S(1)} %get-tuple-element.145.own_ref), channel_id=1, source_target_pairs={{0,192},{8,200},{16,208},{24,216},{32,224},{40,232},{48,240},{56,2... | collective-permute-start | bytes 196616 | tf_op jit(solution)/shard_map/ppermute | solution.py:549
  60.9 4.6 %collective-permute-start.16 = (f32[128,128]{1,0:T(8,128)S(1)}, f32[128,128]{1,0:T(8,128)S(1)}, u32[]{:S(2)}, u32[]{:S(2)}) collective-permute-start(f32[128,128]{1,0:T(8,128)S(1)} %get-tuple-element.145.own_ref), channel_id=1, source_target_pairs={{0,128},{8,136},{16,144},{24,152},{32,160},{40,168},{48,176},{56,1... | collective-permute-start | bytes 196616 | tf_op jit(solution)/shard_map/ppermute | solution.py:549
  61.8 4.5 %collective-permute-start.15 = (f32[128,128]{1,0:T(8,128)S(1)}, f32[128,128]{1,0:T(8,128)S(1)}, u32[]{:S(2)}, u32[]{:S(2)}) collective-permute-start(f32[128,128]{1,0:T(8,128)S(1)} %get-tuple-element.145.own_ref), channel_id=1, source_target_pairs={{0,64},{8,72},{16,80},{24,88},{32,96},{40,104},{48,112},{56,120},{... | collective-permute-start | bytes 196616 | tf_op jit(solution)/shard_map/ppermute | solution.py:549
  66.4 6.9 %collective-permute-start.18 = (f32[128,128]{1,0:T(8,128)S(1)}, f32[128,128]{1,0:T(8,128)S(1)}, u32[]{:S(2)}, u32[]{:S(2)}) collective-permute-start(f32[128,128]{1,0:T(8,128)S(1)} %get-tuple-element.150), channel_id=1, source_target_pairs={{0,16},{8,24},{16,32},{24,40},{32,48},{40,56},{48,0},{56,8},{64,80... | collective-permute-start | bytes 196616 | tf_op jit(solution)/shard_map/ppermute | solution.py:549
  67.4 5.9 %collective-permute-start.19 = (f32[128,128]{1,0:T(8,128)S(1)}, f32[128,128]{1,0:T(8,128)S(1)}, u32[]{:S(2)}, u32[]{:S(2)}) collective-permute-start(f32[128,128]{1,0:T(8,128)S(1)} %get-tuple-element.151), channel_id=1, source_target_pairs={{0,32},{8,40},{16,48},{24,56},{32,0},{40,8},{48,16},{56,24},{64,96... | collective-permute-start | bytes 196616 | tf_op jit(solution)/shard_map/ppermute | solution.py:549
  70.0 3.3 %collective-permute-start.20 = (f32[128,128]{1,0:T(8,128)S(1)}, f32[128,128]{1,0:T(8,128)S(1)}, u32[]{:S(2)}, u32[]{:S(2)}) collective-permute-start(f32[128,128]{1,0:T(8,128)S(1)} %get-tuple-element.152), channel_id=1, source_target_pairs={{0,48},{8,56},{16,0},{24,8},{32,16},{40,24},{48,32},{56,40},{64,11... | collective-permute-start | bytes 196616 | tf_op jit(solution)/shard_map/ppermute | solution.py:549
  73.5 5.9 %collective-permute-start.21 = (f32[4,128,128]{2,1,0:T(8,128)S(1)}, f32[4,128,128]{2,1,0:T(8,128)S(1)}, u32[]{:S(2)}, u32[]{:S(2)}) collective-permute-start(f32[4,128,128]{2,1,0:T(8,128)S(1)} %get-tuple-element.160), channel_id=1, source_target_pairs={{0,8},{8,0},{16,24},{24,16},{32,40},{40,32},{48,56},{56,48},{64,72... | collective-permute-start | bytes 786440 | tf_op jit(solution)/shard_map/ppermute | solution.py:549

commit v6 on v5

--- a/solution.py
+++ b/solution.py
@@ -137,8 +137,10 @@
 def send_kernel(slope_hbm, k_hbm, v_hbm, send_ref, kw, vw, rates_ref, slope_ref, kin, vin, sems):
     first = pltpu.make_async_copy(slope_hbm, slope_ref, sems.at[2 * PARTS])
     first.start()
-    k_copies = fetch_rows(k_hbm, kin, sems)
-    v_copies = fetch_rows(v_hbm, vin, sems, PARTS)
+    copies = []
+    for p in range(PARTS):
+        rows = pl.ds(p * CHUNK, CHUNK)
+        copies.append((put(k_hbm, kin, rows, sems.at[p]), put(v_hbm, vin, rows, sems.at[PARTS + p])))
     first.wait()
     for h in range(HEADS):
         slope = jnp.full((8, SIZE), slope_ref[h].astype(F32), F32)
@@ -146,8 +148,7 @@
     other = (1 - core_of()) * HALF
     for p in range(PARTS):
         rows = pl.ds(p * CHUNK, CHUNK)
-        k_copies[p].wait()
-        v_copies[p].wait()
+        wait_all(copies[p])
         spread(kw, kin[rows], p)
         spread(vw, vin[rows], p)
         left = LENGTH - 1.0 - rows_of((CHUNK, SIZE), p * CHUNK)
@@ -385,8 +386,7 @@
     )
 
 
-def grad_kernel(sums_ref, wq_ref, u_ref, gain_ref, own_ref, other_ref, g, keep_ref, send_ref, acc):
-    core = core_of()
+def half_grads(sums_ref, wq_ref, u_ref, gain_ref, o_ref, side, g, s):
     peers = sums_ref.shape[0]
     features = float(peers * HEADS * SIZE)
     sums = sums_ref[0]
@@ -398,24 +398,41 @@
         rows = pl.ds(b * 128, 128)
         inv = jnp.broadcast_to(root[b : b + 1, :], (128, 128)).T
         coef = jnp.broadcast_to(factor[b : b + 1, :], (128, 128)).T
-        for side, o_ref in ((core, own_ref), (1 - core, other_ref)):
-            for j in range(HALF):
-                h = side * HALF + j
-                scaled = gain_ref[pl.ds(h, 1), :] * u_ref[h, rows, :].astype(F32)
-                g[h, rows, :] = (inv * scaled - o_ref[j, rows, :] * coef).astype(BF16)
-    for h in range(HEADS):
-        acc[h] = dot(wq_ref[h], g[h], NN)
-    keep_ref[...] = acc[pl.ds(core * HALF, HALF)]
-    send_ref[...] = acc[pl.ds((1 - core) * HALF, HALF)]
-
-
-def grads(sums, wq, u, gain, own, other):
-    return call(
-        grad_kernel,
-        "grads",
-        [("vmem", sums), ("vmem", wq), ("vmem", u), ("vmem", gain), ("vmem", own), ("vmem", other)],
-        [("vmem", ROWS, BF16), ("vmem", HALF_STATE, F32), ("vmem", HALF_STATE, F32)],
-        [pltpu.VMEM(STATE, F32)],
+        for j in range(HALF):
+            h = side * HALF + j
+            scaled = gain_ref[pl.ds(h, 1), :] * u_ref[h, rows, :].astype(F32)
+            g[h, rows, :] = (inv * scaled - o_ref[j, rows, :] * coef).astype(BF16)
+    for j in range(HALF):
+        h = side * HALF + j
+        s[j] = dot(wq_ref[h], g[h], NN)
+
+
+def send_grad_kernel(sums_ref, wq_ref, u_ref, gain_ref, o_ref, g, s):
+    half_grads(sums_ref, wq_ref, u_ref, gain_ref, o_ref, 1 - core_of(), g, s)
+
+
+def keep_grad_kernel(sums_ref, wq_ref, u_ref, gain_ref, o_ref, g_in, g, s):
+    half_grads(sums_ref, wq_ref, u_ref, gain_ref, o_ref, core_of(), g, s)
+
+
+def send_grads(sums, wq, u, gain, other):
+    return call(
+        send_grad_kernel,
+        "send_grads",
+        [("vmem", a) for a in (sums, wq, u, gain, other)],
+        [("vmem", ROWS, BF16), ("vmem", HALF_STATE, F32)],
+    )
+
+
+def keep_grads(sums, wq, u, gain, own, g):
+    return call(
+        keep_grad_kernel,
+        "keep_grads",
+        [("vmem", a) for a in (sums, wq, u, gain, own, g)],
+        [("vmem", ROWS, BF16), ("vmem", HALF_STATE, F32)],
+        flops=10**9,
+        moved=4 * 2**20,
+        aliases={5: 0},
     )
 
 
@@ -568,11 +585,11 @@
 
 def scan(rates, keep, send, reverse, first, second, third, last):
     recv = exchange(send)
-    recv, keep = lax.optimization_barrier((recv, keep()))
+    recv, (keep, *done0) = lax.optimization_barrier((recv, keep()))
     one = [ONE] * 4
     own, *parts = small(total_kernel, "chip_total", reverse, rates, [keep, recv], one, [HALF_STATE])
     moved = along_x(parts)
-    moved, done1 = beside(moved, first())
+    moved, done1 = beside(moved, first(*done0))
     row, part = small(row_kernel, "row_sum", reverse, rates, [own, *moved], [ONE, HALF_STATE], [HALF_STATE])
     moved = along_y(row)
     moved, done2 = beside(moved, second(done1))
@@ -584,15 +601,15 @@
     mine, give = small(
         after_kernel, "after", reverse, rates, [own, *moved, keep, recv], [HALF_STATE] * 2, [HALF_STATE]
     )
-    (other,), done4 = beside([exchange(give)], last(mine, done1, done2, done3))
-    return mine, other, done1, done2, done3, done4
+    (other,), done4 = beside([exchange(give)], last(mine, *done0, done1, done2, done3))
+    return mine, other, done0, done1, done2, done3, done4
 
 
 def on_device(queries, key_rows, value_rows, upstream, norm_gain, slope_index):
     send, kw, vw, rates = send_states(slope_index, key_rows, value_rows)
-    e_own, e_other, (kh, qh), (vh, uh, wq), (loc,), (out_own, sq, dt) = scan(
+    e_own, e_other, _, (kh, qh), (vh, uh, wq), (loc,), (out_own, sq, dt) = scan(
         rates,
-        lambda: keep_states(rates, kw, vw),
+        lambda: [keep_states(rates, kw, vw)],
         send,
         False,
         lambda: turn(rates, kw, queries),
@@ -604,17 +621,21 @@
     peers = lax.axis_size("head")
     out_other, sums = other_outputs(rates, qh, uh, norm_gain, e_other, loc, sq, dt, peers)
     sums = lax.all_to_all(sums, "head", 0, 0, tiled=True)
-    g, keep, send = grads(sums, wq, uh, norm_gain, out_own, out_other)
-
-    l_own, l_other, (gv_local,), (gk_local,), (gq,), (wk, wv) = scan(
+    g_part, send = send_grads(sums, wq, uh, norm_gain, out_other)
+
+    def keep_part():
+        g, keep = keep_grads(sums, wq, uh, norm_gain, out_own, g_part)
+        return [keep, g]
+
+    l_own, l_other, _, (gv_local, _), (gk_local,), (gq,), (wk, wv) = scan(
         rates,
-        lambda: keep,
+        keep_part,
         send,
         True,
-        lambda: [back(rates, kh, qh, g, "gv_local")],
-        lambda a: [back(rates, vh, g, qh, "gk_local")],
-        lambda a, b: [grad_query(rates, g, kh, vh, e_own, e_other)],
-        lambda l, a, b, c: own_finish(rates, kh, vh, b[0], a[0], l),
+        lambda g: [back(rates, kh, qh, g, "gv_local"), g],
+        lambda a: [back(rates, vh, a[1], qh, "gk_local")],
+        lambda a, b: [grad_query(rates, a[1], kh, vh, e_own, e_other)],
+        lambda l, g, a, b, c: own_finish(rates, kh, vh, b[0], a[0], l),
     )
     gk, gv = other_finish(rates, kh, vh, gk_local, gv_local, l_other, wk, wv)
     return gq, gk, gv

time: 81.7 us -> 81.1 us (level)
    pallas_call x21 -> x22, Pallas kernels: 22.4 us -> 22.3 us  [call(): pl.pallas_call(body, in_specs=in_specs, out_specs=out_specs, out_shape=ou...]
  transfers between devices with their start and end apart: 22 -> 22, of which waited for: 13 -> 13; matrix products, arithmetic and copies ran while one was open for 0% -> 0% of each run, Pallas kernels for 19% -> 20%
where the time goes in v6:
time: 81.1 us; the launch traced here: 81 us
  starting transfers between devices  34 us (42%)
  Pallas kernels  22.3 us (27%)
  blocking collectives  14.9 us (18%)
  waiting for transfers between devices  8.7 us (11%)
  between operations  1.06 us (1%)
    ppermute x22, starting transfers between devices, permute(): return lax.ppermute(a, 'ctx', pairs)  34 us
    pallas_call x22, Pallas kernels, call(): pl.pallas_call(body, in_specs=in_specs, out_specs=out_specs, out_shape=ou...  22.3 us
    all_to_all x1, blocking collectives, on_device(): sums = lax.all_to_all(sums, 'head', 0, 0, tiled=True)  14.9 us
    ppermute x22, waiting for transfers between devices, permute(): return lax.ppermute(a, 'ctx', pairs)  8.7 us
  transfers between devices with their start and end apart: 22, of which 13 were waited for; matrix products, arithmetic and copies ran while one was open for 0% of the time, Pallas kernels for 20%

profile of v6, /device:TPU:1, one launch (start us, length us, event | category | flops | bytes accessed | tf_op | source)
XLA Modules:
  0.0 81.0 jit_solution(10938639433863150443)
XLA Ops:
  0.6 2.2 %send_states.1 = (f32[4,128,128]{2,1,0:T(8,128)S(1)}, f32[4096,128]{1,0:T(8,128)S(1)}, f32[4096,128]{1,0:T(8,128)S(1)}, f32[8,8,128]{2,1,0:T(8,128)S(1)}) custom-call(s32[8]{0:T(128)} %slope_hbm.1, bf16[512,8,128]{2,1,0:T(8,128)(2,1)} %k_hbm.1, bf16[512,8,128]{2,1,0:T(8,128)(2,1)} %v_hbm.1), custom_call_target="tpu_custom_call" | custom-call | tf_op jit(solution)/shard_map/send_states/pallas_call | solution.py:67
  2.9 3.3 %collective-permute-start = (f32[4,128,128]{2,1,0:T(8,128)S(1)}, f32[4,128,128]{2,1,0:T(8,128)S(1)}, u32[]{:S(2)}, u32[]{:S(2)}) collective-permute-start(f32[4,128,128]{2,1,0:T(8,128)S(1)} %get-tuple-element.90), channel_id=1, source_target_pairs={{0,8},{8,0},{16,24},{24,16},{32,40},{40,32},{48,56},{56,48},{64,72... | collective-permute-start | bytes 786440 | tf_op jit(solution)/shard_map/ppermute | solution.py:566
  6.2 0.7 keep_states.1.keep_ref
  7.6 1.9 %collective-permute-start.2 = (f32[128,128]{1,0:T(8,128)S(1)}, f32[128,128]{1,0:T(8,128)S(1)}, u32[]{:S(2)}, u32[]{:S(2)}) collective-permute-start(f32[128,128]{1,0:T(8,128)S(1)} %get-tuple-element.96), channel_id=1, source_target_pairs={{0,32},{8,40},{16,48},{24,56},{32,0},{40,8},{48,16},{56,24},{64,96... | collective-permute-start | bytes 196616 | tf_op jit(solution)/shard_map/ppermute | solution.py:566
  9.5 1.2 %collective-permute-start.3 = (f32[128,128]{1,0:T(8,128)S(1)}, f32[128,128]{1,0:T(8,128)S(1)}, u32[]{:S(2)}, u32[]{:S(2)}) collective-permute-start(f32[128,128]{1,0:T(8,128)S(1)} %get-tuple-element.97), channel_id=1, source_target_pairs={{0,48},{8,56},{16,0},{24,8},{32,16},{40,24},{48,32},{56,40},{64,11... | collective-permute-start | bytes 196616 | tf_op jit(solution)/shard_map/ppermute | solution.py:566
  10.6 1.4 %turn.2 = (bf16[8,512,128]{2,1,0:T(8,128)(2,1)S(1)}, bf16[8,512,128]{2,1,0:T(8,128)(2,1)S(1)}) custom-call(f32[8,8,128]{2,1,0:T(8,128)S(1)} %get-tuple-element.89.rates_ref, f32[4096,128]{1,0:T(8,128)S(1)} %get-tuple-element.91.kw.a_wide, bf16[512,8,128]{2,1,0:T(8,128)(2,1)} %b_hbm.2), custom_call_target="tpu_custom_call" | custom-call | bytes 8388608 | tf_op jit(solution)/shard_map/turn/pallas_call | solution.py:67
  13.8 2.0 %collective-permute-start.6 = (f32[128,128]{1,0:T(8,128)S(1)}, f32[128,128]{1,0:T(8,128)S(1)}, u32[]{:S(2)}, u32[]{:S(2)}) collective-permute-start(f32[128,128]{1,0:T(8,128)S(1)} %get-tuple-element.105.own_ref), channel_id=1, source_target_pairs={{0,192},{8,200},{16,208},{24,216},{32,224},{40,232},{48,240},{56,2... | collective-permute-start | bytes 196616 | tf_op jit(solution)/shard_map/ppermute | solution.py:566
  16.1 0.7 collective-permute-start.4
  16.8 1.8 %turn.3 = (bf16[8,512,128]{2,1,0:T(8,128)(2,1)S(1)}, bf16[8,512,128]{2,1,0:T(8,128)(2,1)S(1)}, bf16[8,128,512]{2,1,0:T(8,128)(2,1)S(1)}) custom-call(f32[8,8,128]{2,1,0:T(8,128)S(1)} %get-tuple-element.89.rates_ref, f32[4096,128]{1,0:T(8,128)S(1)} %get-tuple-element.92.vw.a_wide, bf16[512,8,128]{2,1,0:T(8,128)(2,1)} %b_hbm.3, ...), custom_call_target="tpu_custom_call" | custom-call | bytes 8388608 | tf_op jit(solution)/shard_map/turn/pallas_call | solution.py:67
  18.7 1.8 %collective-permute-done.5.from2 = f32[128,128]{1,0:T(8,128)S(1)} collective-permute-done((f32[128,128]{1,0:T(8,128)S(1)}, f32[128,128]{1,0:T(8,128)S(1)}, u32[]{:S(2)}, u32[]{:S(2)}) %collective-permute-start.5) | collective-permute-done | bytes 65568 | tf_op jit(solution)/shard_map/ppermute | solution.py:566
  20.5 0.6 collective-permute-done.4.from1
  21.3 3.2 %collective-permute-start.8 = (f32[128,128]{1,0:T(8,128)S(1)}, f32[128,128]{1,0:T(8,128)S(1)}, u32[]{:S(2)}, u32[]{:S(2)}) collective-permute-start(f32[128,128]{1,0:T(8,128)S(1)} %get-tuple-element.116), channel_id=1, source_target_pairs={{0,32},{8,40},{16,48},{24,56},{32,0},{40,8},{48,16},{56,24},{64,96... | collective-permute-start | bytes 196616 | tf_op jit(solution)/shard_map/ppermute | solution.py:566
  25.0 2.3 %local_part.1.loc = f32[8,512,128]{2,1,0:T(8,128)S(1)} custom-call(f32[8,8,128]{2,1,0:T(8,128)S(1)} %get-tuple-element.89.rates_ref, bf16[8,512,128]{2,1,0:T(8,128)(2,1)S(1)} %get-tuple-element.100.refs_0_.q_ref.b_ref.c_ref, bf16[8,512,128]{2,1,0:T(8,128)(2,1)S(1)} %get-tuple-element.118.k_ref.a_ref.k, bf16[8,512,128]{2,1,0:T(8,128)(2,1)S(1)} %get-tuple-element.119.v_ref.a_ref.v), custom_call_target="tpu_custom_call" | custom-call | flops 2000000000 | bytes 5242880 | tf_op jit(solution)/shard_map/local_part/pallas_call | solution.py:67
  27.8 5.3 %collective-permute-start.10 = (f32[4,128,128]{2,1,0:T(8,128)S(1)}, f32[4,128,128]{2,1,0:T(8,128)S(1)}, u32[]{:S(2)}, u32[]{:S(2)}) collective-permute-start(f32[4,128,128]{2,1,0:T(8,128)S(1)} %get-tuple-element.123), channel_id=1, source_target_pairs={{0,8},{8,0},{16,24},{24,16},{32,40},{40,32},{48,56},{56,48},{64,72... | collective-permute-start | bytes 786440 | tf_op jit(solution)/shard_map/ppermute | solution.py:566
  33.6 0.7 collective-permute-done.10.state_ref.other_ref
  34.9 14.9 %all_to_all.5.sums_ref = f32[8,8,128]{2,1,0:T(8,128)S(1)} all-to-all(f32[8,8,128]{2,1,0:T(8,128)S(1)} %get-tuple-element.132), channel_id=1, replica_groups=mesh['ctx'=32,'head'=8] {'head'}, dimensions={0} | all-to-all | bytes 65536 | tf_op jit(solution)/shard_map/all_to_all | solution.py:623
  50.4 1.8 %collective-permute-start.11 = (f32[4,128,128]{2,1,0:T(8,128)S(1)}, f32[4,128,128]{2,1,0:T(8,128)S(1)}, u32[]{:S(2)}, u32[]{:S(2)}) collective-permute-start(f32[4,128,128]{2,1,0:T(8,128)S(1)} %get-tuple-element.135), channel_id=1, source_target_pairs={{0,8},{8,0},{16,24},{24,16},{32,40},{40,32},{48,56},{56,48},{64,72... | collective-permute-start | bytes 786440 | tf_op jit(solution)/shard_map/ppermute | solution.py:566
  53.6 2.5 %collective-permute-start.13 = (f32[128,128]{1,0:T(8,128)S(1)}, f32[128,128]{1,0:T(8,128)S(1)}, u32[]{:S(2)}, u32[]{:S(2)}) collective-permute-start(f32[128,128]{1,0:T(8,128)S(1)} %get-tuple-element.144), channel_id=1, source_target_pairs={{0,32},{8,40},{16,48},{24,56},{32,0},{40,8},{48,16},{56,24},{64,96... | collective-permute-start | bytes 196616 | tf_op jit(solution)/shard_map/ppermute | solution.py:566
  56.1 0.8 collective-permute-start.14
  56.9 2.3 %gv_local.1.vl_ref = bf16[8,512,128]{2,1,0:T(8,128)(2,1)S(1)} custom-call(f32[8,8,128]{2,1,0:T(8,128)S(1)} %get-tuple-element.89.rates_ref, bf16[8,512,128]{2,1,0:T(8,128)(2,1)S(1)} %get-tuple-element.118.k_ref.a_ref.k, bf16[8,512,128]{2,1,0:T(8,128)(2,1)S(1)} %get-tuple-element.100.refs_0_.q_ref.b_ref.c_ref, ...), custom_call_target="tpu_custom_call" | custom-call | flops 2000000000 | bytes 5242880 | tf_op jit(solution)/shard_map/gv_local/pallas_call | solution.py:67
  59.2 0.7 collective-permute-done.14.from3
  60.3 0.9 %collective-permute-start.16 = (f32[128,128]{1,0:T(8,128)S(1)}, f32[128,128]{1,0:T(8,128)S(1)}, u32[]{:S(2)}, u32[]{:S(2)}) collective-permute-start(f32[128,128]{1,0:T(8,128)S(1)} %get-tuple-element.150.own_ref), channel_id=1, source_target_pairs={{0,128},{8,136},{16,144},{24,152},{32,160},{40,168},{48,176},{56,1... | collective-permute-start | bytes 196616 | tf_op jit(solution)/shard_map/ppermute | solution.py:566
  61.2 0.8 collective-permute-start.15
  61.9 2.3 %gk_local.1.kl_ref = bf16[8,512,128]{2,1,0:T(8,128)(2,1)S(1)} custom-call(f32[8,8,128]{2,1,0:T(8,128)S(1)} %get-tuple-element.89.rates_ref, bf16[8,512,128]{2,1,0:T(8,128)(2,1)S(1)} %get-tuple-element.119.v_ref.a_ref.v, bf16[8,512,128]{2,1,0:T(8,128)(2,1)S(1)} %get-tuple-element.151.c_ref.b_ref.g_ref, ...), custom_call_target="tpu_custom_call" | custom-call | flops 2000000000 | bytes 5242880 | tf_op jit(solution)/shard_map/gk_local/pallas_call | solution.py:67
  64.3 0.7 collective-permute-done.16.from2
  64.9 0.7 collective-permute-done.15.from1
  65.8 1.0 %collective-permute-start.18 = (f32[128,128]{1,0:T(8,128)S(1)}, f32[128,128]{1,0:T(8,128)S(1)}, u32[]{:S(2)}, u32[]{:S(2)}) collective-permute-start(f32[128,128]{1,0:T(8,128)S(1)} %get-tuple-element.156), channel_id=1, source_target_pairs={{0,16},{8,24},{16,32},{24,40},{32,48},{40,56},{48,0},{56,8},{64,80... | collective-permute-start | bytes 196616 | tf_op jit(solution)/shard_map/ppermute | solution.py:566
  66.8 2.6 %collective-permute-start.19 = (f32[128,128]{1,0:T(8,128)S(1)}, f32[128,128]{1,0:T(8,128)S(1)}, u32[]{:S(2)}, u32[]{:S(2)}) collective-permute-start(f32[128,128]{1,0:T(8,128)S(1)} %get-tuple-element.157), channel_id=1, source_target_pairs={{0,32},{8,40},{16,48},{24,56},{32,0},{40,8},{48,16},{56,24},{64,96... | collective-permute-start | bytes 196616 | tf_op jit(solution)/shard_map/ppermute | solution.py:566
  69.4 3.3 %grad_query.1 = bf16[512,8,128]{2,1,0:T(8,128)(2,1)} custom-call(f32[8,8,128]{2,1,0:T(8,128)S(1)} %get-tuple-element.89.rates_ref, bf16[8,512,128]{2,1,0:T(8,128)(2,1)S(1)} %get-tuple-element.151.c_ref.b_ref.g_ref, bf16[8,512,128]{2,1,0:T(8,128)(2,1)S(1)} %get-tuple-element.118.k_ref.a_ref.k, bf16[8,512,128]{2,1,0:T(8,128)(2,1)S(1)} %get-tuple-element.119.v_ref.a_ref.v, ...), custom_call_target="tpu_custom_call" | custom-call | flops 3000000000 | bytes 5242880 | tf_op jit(solution)/shard_map/grad_query/pallas_call | solution.py:67
  72.9 4.7 %collective-permute-start.21 = (f32[4,128,128]{2,1,0:T(8,128)S(1)}, f32[4,128,128]{2,1,0:T(8,128)S(1)}, u32[]{:S(2)}, u32[]{:S(2)}) collective-permute-start(f32[4,128,128]{2,1,0:T(8,128)S(1)} %get-tuple-element.166), channel_id=1, source_target_pairs={{0,8},{8,0},{16,24},{24,16},{32,40},{40,32},{48,56},{56,48},{64,72... | collective-permute-start | bytes 786440 | tf_op jit(solution)/shard_map/ppermute | solution.py:566
  77.6 0.7 own_finish.1
  78.7 2.0 %other_finish.1 = (bf16[512,8,128]{2,1,0:T(8,128)(2,1)}, bf16[512,8,128]{2,1,0:T(8,128)(2,1)}, f32[4096,128]{1,0:T(8,128)S(1)}, f32[4096,128]{1,0:T(8,128)S(1)}) custom-call(f32[8,8,128]{2,1,0:T(8,128)S(1)} %get-tuple-element.89.rates_ref, bf16[8,512,128]{2,1,0:T(8,128)(2,1)S(1)} %get-tuple-element.118.k_ref.a_ref.k, ...), custom_call_target="tpu_custom_call", output_to_operand_aliasing={{2}: (6, {}), {3}: (7, {})} | custom-call | tf_op jit(solution)/shard_map/other_finish/pallas_call | solution.py:67
  (37 shorter events, 8.0 us)
Async XLA Ops:
  2.9 4.5 %collective-permute-start = (f32[4,128,128]{2,1,0:T(8,128)S(1)}, f32[4,128,128]{2,1,0:T(8,128)S(1)}, u32[]{:S(2)}, u32[]{:S(2)}) collective-permute-start(f32[4,128,128]{2,1,0:T(8,128)S(1)} %get-tuple-element.90), channel_id=1, source_target_pairs={{0,8},{8,0},{16,24},{24,16},{32,40},{40,32},{48,56},{56,48},{64,72... | collective-permute-start | bytes 786440 | tf_op jit(solution)/shard_map/ppermute | solution.py:566
  7.5 5.2 %collective-permute-start.1 = (f32[128,128]{1,0:T(8,128)S(1)}, f32[128,128]{1,0:T(8,128)S(1)}, u32[]{:S(2)}, u32[]{:S(2)}) collective-permute-start(f32[128,128]{1,0:T(8,128)S(1)} %get-tuple-element.95), channel_id=1, source_target_pairs={{0,16},{8,24},{16,32},{24,40},{32,48},{40,56},{48,0},{56,8},{64,80... | collective-permute-start | bytes 196616 | tf_op jit(solution)/shard_map/ppermute | solution.py:566
  7.6 5.7 %collective-permute-start.2 = (f32[128,128]{1,0:T(8,128)S(1)}, f32[128,128]{1,0:T(8,128)S(1)}, u32[]{:S(2)}, u32[]{:S(2)}) collective-permute-start(f32[128,128]{1,0:T(8,128)S(1)} %get-tuple-element.96), channel_id=1, source_target_pairs={{0,32},{8,40},{16,48},{24,56},{32,0},{40,8},{48,16},{56,24},{64,96... | collective-permute-start | bytes 196616 | tf_op jit(solution)/shard_map/ppermute | solution.py:566
  9.5 4.2 %collective-permute-start.3 = (f32[128,128]{1,0:T(8,128)S(1)}, f32[128,128]{1,0:T(8,128)S(1)}, u32[]{:S(2)}, u32[]{:S(2)}) collective-permute-start(f32[128,128]{1,0:T(8,128)S(1)} %get-tuple-element.97), channel_id=1, source_target_pairs={{0,48},{8,56},{16,0},{24,8},{32,16},{40,24},{48,32},{56,40},{64,11... | collective-permute-start | bytes 196616 | tf_op jit(solution)/shard_map/ppermute | solution.py:566
  13.8 4.9 %collective-permute-start.6 = (f32[128,128]{1,0:T(8,128)S(1)}, f32[128,128]{1,0:T(8,128)S(1)}, u32[]{:S(2)}, u32[]{:S(2)}) collective-permute-start(f32[128,128]{1,0:T(8,128)S(1)} %get-tuple-element.105.own_ref), channel_id=1, source_target_pairs={{0,192},{8,200},{16,208},{24,216},{32,224},{40,232},{48,240},{56,2... | collective-permute-start | bytes 196616 | tf_op jit(solution)/shard_map/ppermute | solution.py:566
  15.8 4.7 %collective-permute-start.5 = (f32[128,128]{1,0:T(8,128)S(1)}, f32[128,128]{1,0:T(8,128)S(1)}, u32[]{:S(2)}, u32[]{:S(2)}) collective-permute-start(f32[128,128]{1,0:T(8,128)S(1)} %get-tuple-element.105.own_ref), channel_id=1, source_target_pairs={{0,128},{8,136},{16,144},{24,152},{32,160},{40,168},{48,176},{56,1... | collective-permute-start | bytes 196616 | tf_op jit(solution)/shard_map/ppermute | solution.py:566
  16.1 5.0 %collective-permute-start.4 = (f32[128,128]{1,0:T(8,128)S(1)}, f32[128,128]{1,0:T(8,128)S(1)}, u32[]{:S(2)}, u32[]{:S(2)}) collective-permute-start(f32[128,128]{1,0:T(8,128)S(1)} %get-tuple-element.105.own_ref), channel_id=1, source_target_pairs={{0,64},{8,72},{16,80},{24,88},{32,96},{40,104},{48,112},{56,120},{... | collective-permute-start | bytes 196616 | tf_op jit(solution)/shard_map/ppermute | solution.py:566
  21.3 6.0 %collective-permute-start.7 = (f32[128,128]{1,0:T(8,128)S(1)}, f32[128,128]{1,0:T(8,128)S(1)}, u32[]{:S(2)}, u32[]{:S(2)}) collective-permute-start(f32[128,128]{1,0:T(8,128)S(1)} %get-tuple-element.115), channel_id=1, source_target_pairs={{0,16},{8,24},{16,32},{24,40},{32,48},{40,56},{48,0},{56,8},{64,80... | collective-permute-start | bytes 196616 | tf_op jit(solution)/shard_map/ppermute | solution.py:566
  21.3 6.0 %collective-permute-start.8 = (f32[128,128]{1,0:T(8,128)S(1)}, f32[128,128]{1,0:T(8,128)S(1)}, u32[]{:S(2)}, u32[]{:S(2)}) collective-permute-start(f32[128,128]{1,0:T(8,128)S(1)} %get-tuple-element.116), channel_id=1, source_target_pairs={{0,32},{8,40},{16,48},{24,56},{32,0},{40,8},{48,16},{56,24},{64,96... | collective-permute-start | bytes 196616 | tf_op jit(solution)/shard_map/ppermute | solution.py:566
  24.6 8.6 %copy-start = (f32[8,128]{1,0:T(8,128)S(1)}, f32[8,128]{1,0:T(8,128)}, u32[]{:S(2)}) copy-start(f32[8,128]{1,0:T(8,128)} %gain_ref.7) | copy-start | bytes 12292
  24.6 3.1 %collective-permute-start.9 = (f32[128,128]{1,0:T(8,128)S(1)}, f32[128,128]{1,0:T(8,128)S(1)}, u32[]{:S(2)}, u32[]{:S(2)}) collective-permute-start(f32[128,128]{1,0:T(8,128)S(1)} %get-tuple-element.117), channel_id=1, source_target_pairs={{0,48},{8,56},{16,0},{24,8},{32,16},{40,24},{48,32},{56,40},{64,11... | collective-permute-start | bytes 196616 | tf_op jit(solution)/shard_map/ppermute | solution.py:566
  27.8 6.5 %collective-permute-start.10 = (f32[4,128,128]{2,1,0:T(8,128)S(1)}, f32[4,128,128]{2,1,0:T(8,128)S(1)}, u32[]{:S(2)}, u32[]{:S(2)}) collective-permute-start(f32[4,128,128]{2,1,0:T(8,128)S(1)} %get-tuple-element.123), channel_id=1, source_target_pairs={{0,8},{8,0},{16,24},{24,16},{32,40},{40,32},{48,56},{56,48},{64,72... | collective-permute-start | bytes 786440 | tf_op jit(solution)/shard_map/ppermute | solution.py:566
  50.4 3.0 %collective-permute-start.11 = (f32[4,128,128]{2,1,0:T(8,128)S(1)}, f32[4,128,128]{2,1,0:T(8,128)S(1)}, u32[]{:S(2)}, u32[]{:S(2)}) collective-permute-start(f32[4,128,128]{2,1,0:T(8,128)S(1)} %get-tuple-element.135), channel_id=1, source_target_pairs={{0,8},{8,0},{16,24},{24,16},{32,40},{40,32},{48,56},{56,48},{64,72... | collective-permute-start | bytes 786440 | tf_op jit(solution)/shard_map/ppermute | solution.py:566
  53.5 5.7 %collective-permute-start.12 = (f32[128,128]{1,0:T(8,128)S(1)}, f32[128,128]{1,0:T(8,128)S(1)}, u32[]{:S(2)}, u32[]{:S(2)}) collective-permute-start(f32[128,128]{1,0:T(8,128)S(1)} %get-tuple-element.143), channel_id=1, source_target_pairs={{0,16},{8,24},{16,32},{24,40},{32,48},{40,56},{48,0},{56,8},{64,80... | collective-permute-start | bytes 196616 | tf_op jit(solution)/shard_map/ppermute | solution.py:566
  53.6 5.6 %collective-permute-start.13 = (f32[128,128]{1,0:T(8,128)S(1)}, f32[128,128]{1,0:T(8,128)S(1)}, u32[]{:S(2)}, u32[]{:S(2)}) collective-permute-start(f32[128,128]{1,0:T(8,128)S(1)} %get-tuple-element.144), channel_id=1, source_target_pairs={{0,32},{8,40},{16,48},{24,56},{32,0},{40,8},{48,16},{56,24},{64,96... | collective-permute-start | bytes 196616 | tf_op jit(solution)/shard_map/ppermute | solution.py:566
  56.1 3.8 %collective-permute-start.14 = (f32[128,128]{1,0:T(8,128)S(1)}, f32[128,128]{1,0:T(8,128)S(1)}, u32[]{:S(2)}, u32[]{:S(2)}) collective-permute-start(f32[128,128]{1,0:T(8,128)S(1)} %get-tuple-element.145), channel_id=1, source_target_pairs={{0,48},{8,56},{16,0},{24,8},{32,16},{40,24},{48,32},{56,40},{64,11... | collective-permute-start | bytes 196616 | tf_op jit(solution)/shard_map/ppermute | solution.py:566
  60.0 4.3 %collective-permute-start.17 = (f32[128,128]{1,0:T(8,128)S(1)}, f32[128,128]{1,0:T(8,128)S(1)}, u32[]{:S(2)}, u32[]{:S(2)}) collective-permute-start(f32[128,128]{1,0:T(8,128)S(1)} %get-tuple-element.150.own_ref), channel_id=1, source_target_pairs={{0,192},{8,200},{16,208},{24,216},{32,224},{40,232},{48,240},{56,2... | collective-permute-start | bytes 196616 | tf_op jit(solution)/shard_map/ppermute | solution.py:566
  60.3 4.6 %collective-permute-start.16 = (f32[128,128]{1,0:T(8,128)S(1)}, f32[128,128]{1,0:T(8,128)S(1)}, u32[]{:S(2)}, u32[]{:S(2)}) collective-permute-start(f32[128,128]{1,0:T(8,128)S(1)} %get-tuple-element.150.own_ref), channel_id=1, source_target_pairs={{0,128},{8,136},{16,144},{24,152},{32,160},{40,168},{48,176},{56,1... | collective-permute-start | bytes 196616 | tf_op jit(solution)/shard_map/ppermute | solution.py:566
  61.2 4.5 %collective-permute-start.15 = (f32[128,128]{1,0:T(8,128)S(1)}, f32[128,128]{1,0:T(8,128)S(1)}, u32[]{:S(2)}, u32[]{:S(2)}) collective-permute-start(f32[128,128]{1,0:T(8,128)S(1)} %get-tuple-element.150.own_ref), channel_id=1, source_target_pairs={{0,64},{8,72},{16,80},{24,88},{32,96},{40,104},{48,112},{56,120},{... | collective-permute-start | bytes 196616 | tf_op jit(solution)/shard_map/ppermute | solution.py:566
  65.8 6.9 %collective-permute-start.18 = (f32[128,128]{1,0:T(8,128)S(1)}, f32[128,128]{1,0:T(8,128)S(1)}, u32[]{:S(2)}, u32[]{:S(2)}) collective-permute-start(f32[128,128]{1,0:T(8,128)S(1)} %get-tuple-element.156), channel_id=1, source_target_pairs={{0,16},{8,24},{16,32},{24,40},{32,48},{40,56},{48,0},{56,8},{64,80... | collective-permute-start | bytes 196616 | tf_op jit(solution)/shard_map/ppermute | solution.py:566
  66.8 5.9 %collective-permute-start.19 = (f32[128,128]{1,0:T(8,128)S(1)}, f32[128,128]{1,0:T(8,128)S(1)}, u32[]{:S(2)}, u32[]{:S(2)}) collective-permute-start(f32[128,128]{1,0:T(8,128)S(1)} %get-tuple-element.157), channel_id=1, source_target_pairs={{0,32},{8,40},{16,48},{24,56},{32,0},{40,8},{48,16},{56,24},{64,96... | collective-permute-start | bytes 196616 | tf_op jit(solution)/shard_map/ppermute | solution.py:566
  69.4 3.3 %collective-permute-start.20 = (f32[128,128]{1,0:T(8,128)S(1)}, f32[128,128]{1,0:T(8,128)S(1)}, u32[]{:S(2)}, u32[]{:S(2)}) collective-permute-start(f32[128,128]{1,0:T(8,128)S(1)} %get-tuple-element.158), channel_id=1, source_target_pairs={{0,48},{8,56},{16,0},{24,8},{32,16},{40,24},{48,32},{56,40},{64,11... | collective-permute-start | bytes 196616 | tf_op jit(solution)/shard_map/ppermute | solution.py:566
  72.9 5.9 %collective-permute-start.21 = (f32[4,128,128]{2,1,0:T(8,128)S(1)}, f32[4,128,128]{2,1,0:T(8,128)S(1)}, u32[]{:S(2)}, u32[]{:S(2)}) collective-permute-start(f32[4,128,128]{2,1,0:T(8,128)S(1)} %get-tuple-element.166), channel_id=1, source_target_pairs={{0,8},{8,0},{16,24},{24,16},{32,40},{40,32},{48,56},{56,48},{64,72... | collective-permute-start | bytes 786440 | tf_op jit(solution)/shard_map/ppermute | solution.py:566

commit v7 on v6

--- a/solution.py
+++ b/solution.py
@@ -125,6 +125,11 @@
     return pltpu.SemaphoreType.DMA((count,))
 
 
+def by_core(body):
+    for core in range(2):
+        pl.when(core_of() == core)(functools.partial(body, core))
+
+
 def half_states(kw, vw, rates_ref, first_head, rows, left, s):
     start, count = rows
     for j in range(HALF):
@@ -145,14 +150,17 @@
     for h in range(HEADS):
         slope = jnp.full((8, SIZE), slope_ref[h].astype(F32), F32)
         rates_ref[h] = jnp.exp((slope + 1.0) * (-8.0 / 64.0 * math.log(2.0))) * LAYER_FACTOR
-    other = (1 - core_of()) * HALF
-    for p in range(PARTS):
-        rows = pl.ds(p * CHUNK, CHUNK)
-        wait_all(copies[p])
-        spread(kw, kin[rows], p)
-        spread(vw, vin[rows], p)
-        left = LENGTH - 1.0 - rows_of((CHUNK, SIZE), p * CHUNK)
-        half_states(kw, vw, rates_ref, other, (p * CHUNK, CHUNK), left, send_ref)
+
+    def form(core):
+        for p in range(PARTS):
+            rows = pl.ds(p * CHUNK, CHUNK)
+            wait_all(copies[p])
+            spread(kw, kin[rows], p)
+            spread(vw, vin[rows], p)
+            left = LENGTH - 1.0 - rows_of((CHUNK, SIZE), p * CHUNK)
+            half_states(kw, vw, rates_ref, (1 - core) * HALF, (p * CHUNK, CHUNK), left, send_ref)
+
+    by_core(form)
 
 
 def send_states(slope, k, v):
@@ -168,7 +176,7 @@
 
 def keep_kernel(rates_ref, kw, vw, keep_ref):
     left = LENGTH - 1.0 - rows_of((LENGTH, SIZE))
-    half_states(kw, vw, rates_ref, core_of() * HALF, (0, LENGTH), left, keep_ref)
+    by_core(lambda core: half_states(kw, vw, rates_ref, core * HALF, (0, LENGTH), left, keep_ref))
 
 
 def keep_states(rates, kw, vw):
@@ -515,22 +523,29 @@
 
 
 def own_finish_kernel(rates_ref, k, v, kl_ref, vl_ref, state_ref, wk, wv):
-    for _ in half_finish(rates_ref, k, v, kl_ref, vl_ref, state_ref, core_of() * HALF, wk, wv):
-        pass
+    def form(core):
+        for _ in half_finish(rates_ref, k, v, kl_ref, vl_ref, state_ref, core * HALF, wk, wv):
+            pass
+
+    by_core(form)
 
 
 def other_finish_kernel(rates_ref, k, v, kl_ref, vl_ref, state_ref, wk_in, wv_in, gk_hbm, gv_hbm, wk, wv, gk, gv, sems):
-    writes = []
     sides = ((wk, gk, gk_hbm), (wv, gv, gv_hbm))
-    halves = half_finish(rates_ref, k, v, kl_ref, vl_ref, state_ref, (1 - core_of()) * HALF, wk, wv)
-    for n, _ in enumerate(halves):
-        wide, out, to = sides[n]
-        for p in range(PARTS):
-            rows = pl.ds(p * CHUNK, CHUNK)
-            flat = pl.ds(p * CHUNK * HEADS, CHUNK * HEADS)
-            out[rows] = wide[flat, :].reshape(CHUNK, HEADS, SIZE).astype(BF16)
-            writes.append(put(out, to, rows, sems.at[PARTS * n + p]))
-    wait_all(writes)
+
+    def form(core):
+        writes = []
+        halves = half_finish(rates_ref, k, v, kl_ref, vl_ref, state_ref, (1 - core) * HALF, wk, wv)
+        for n, _ in enumerate(halves):
+            wide, out, to = sides[n]
+            for p in range(PARTS):
+                rows = pl.ds(p * CHUNK, CHUNK)
+                flat = pl.ds(p * CHUNK * HEADS, CHUNK * HEADS)
+                out[rows] = wide[flat, :].reshape(CHUNK, HEADS, SIZE).astype(BF16)
+                writes.append(put(out, to, rows, sems.at[PARTS * n + p]))
+        wait_all(writes)
+
+    by_core(form)
 
 
 def own_finish(rates, k, v, kl, vl, state):

time: 81.1 us -> 80.7 us (level)
  no operation moved by 1% of the time
where the time goes in v7:
time: 80.7 us; the launch traced here: 80.5 us
  starting transfers between devices  34 us (42%)
  Pallas kernels  21.8 us (27%)
  blocking collectives  14.9 us (18%)
  waiting for transfers between devices  8.66 us (11%)
  between operations  1.06 us (1%)
    ppermute x22, starting transfers between devices, permute(): return lax.ppermute(a, 'ctx', pairs)  34 us
    pallas_call x22, Pallas kernels, call(): pl.pallas_call(body, in_specs=in_specs, out_specs=out_specs, out_shape=ou...  21.8 us
    all_to_all x1, blocking collectives, on_device(): sums = lax.all_to_all(sums, 'head', 0, 0, tiled=True)  14.9 us
    ppermute x22, waiting for transfers between devices, permute(): return lax.ppermute(a, 'ctx', pairs)  8.66 us
  transfers between devices with their start and end apart: 22, of which 13 were waited for; matrix products, arithmetic and copies ran while one was open for 0% of the time, Pallas kernels for 20%

profile of v7, /device:TPU:1, one launch (start us, length us, event | category | flops | bytes accessed | tf_op | source)
XLA Modules:
  0.0 80.5 jit_solution(1424424446864224938)
XLA Ops:
  0.6 2.1 %send_states.1 = (f32[4,128,128]{2,1,0:T(8,128)S(1)}, f32[4096,128]{1,0:T(8,128)S(1)}, f32[4096,128]{1,0:T(8,128)S(1)}, f32[8,8,128]{2,1,0:T(8,128)S(1)}) custom-call(s32[8]{0:T(128)} %slope_hbm.1, bf16[512,8,128]{2,1,0:T(8,128)(2,1)} %k_hbm.1, bf16[512,8,128]{2,1,0:T(8,128)(2,1)} %v_hbm.1), custom_call_target="tpu_custom_call" | custom-call | tf_op jit(solution)/shard_map/send_states/pallas_call | solution.py:67
  2.7 3.3 %collective-permute-start = (f32[4,128,128]{2,1,0:T(8,128)S(1)}, f32[4,128,128]{2,1,0:T(8,128)S(1)}, u32[]{:S(2)}, u32[]{:S(2)}) collective-permute-start(f32[4,128,128]{2,1,0:T(8,128)S(1)} %get-tuple-element.90), channel_id=1, source_target_pairs={{0,8},{8,0},{16,24},{24,16},{32,40},{40,32},{48,56},{56,48},{64,72... | collective-permute-start | bytes 786440 | tf_op jit(solution)/shard_map/ppermute | solution.py:581
  6.0 0.7 keep_states.1.keep_ref
  7.4 1.9 %collective-permute-start.2 = (f32[128,128]{1,0:T(8,128)S(1)}, f32[128,128]{1,0:T(8,128)S(1)}, u32[]{:S(2)}, u32[]{:S(2)}) collective-permute-start(f32[128,128]{1,0:T(8,128)S(1)} %get-tuple-element.96), channel_id=1, source_target_pairs={{0,32},{8,40},{16,48},{24,56},{32,0},{40,8},{48,16},{56,24},{64,96... | collective-permute-start | bytes 196616 | tf_op jit(solution)/shard_map/ppermute | solution.py:581
  9.3 1.2 %collective-permute-start.3 = (f32[128,128]{1,0:T(8,128)S(1)}, f32[128,128]{1,0:T(8,128)S(1)}, u32[]{:S(2)}, u32[]{:S(2)}) collective-permute-start(f32[128,128]{1,0:T(8,128)S(1)} %get-tuple-element.97), channel_id=1, source_target_pairs={{0,48},{8,56},{16,0},{24,8},{32,16},{40,24},{48,32},{56,40},{64,11... | collective-permute-start | bytes 196616 | tf_op jit(solution)/shard_map/ppermute | solution.py:581
  10.4 1.4 %turn.2 = (bf16[8,512,128]{2,1,0:T(8,128)(2,1)S(1)}, bf16[8,512,128]{2,1,0:T(8,128)(2,1)S(1)}) custom-call(f32[8,8,128]{2,1,0:T(8,128)S(1)} %get-tuple-element.89.rates_ref, f32[4096,128]{1,0:T(8,128)S(1)} %get-tuple-element.91.kw.a_wide, bf16[512,8,128]{2,1,0:T(8,128)(2,1)} %b_hbm.2), custom_call_target="tpu_custom_call" | custom-call | bytes 8388608 | tf_op jit(solution)/shard_map/turn/pallas_call | solution.py:67
  13.6 2.0 %collective-permute-start.6 = (f32[128,128]{1,0:T(8,128)S(1)}, f32[128,128]{1,0:T(8,128)S(1)}, u32[]{:S(2)}, u32[]{:S(2)}) collective-permute-start(f32[128,128]{1,0:T(8,128)S(1)} %get-tuple-element.105.own_ref), channel_id=1, source_target_pairs={{0,192},{8,200},{16,208},{24,216},{32,224},{40,232},{48,240},{56,2... | collective-permute-start | bytes 196616 | tf_op jit(solution)/shard_map/ppermute | solution.py:581
  16.0 0.7 collective-permute-start.4
  16.6 1.8 %turn.3 = (bf16[8,512,128]{2,1,0:T(8,128)(2,1)S(1)}, bf16[8,512,128]{2,1,0:T(8,128)(2,1)S(1)}, bf16[8,128,512]{2,1,0:T(8,128)(2,1)S(1)}) custom-call(f32[8,8,128]{2,1,0:T(8,128)S(1)} %get-tuple-element.89.rates_ref, f32[4096,128]{1,0:T(8,128)S(1)} %get-tuple-element.92.vw.a_wide, bf16[512,8,128]{2,1,0:T(8,128)(2,1)} %b_hbm.3, ...), custom_call_target="tpu_custom_call" | custom-call | bytes 8388608 | tf_op jit(solution)/shard_map/turn/pallas_call | solution.py:67
  18.5 1.8 %collective-permute-done.5.from2 = f32[128,128]{1,0:T(8,128)S(1)} collective-permute-done((f32[128,128]{1,0:T(8,128)S(1)}, f32[128,128]{1,0:T(8,128)S(1)}, u32[]{:S(2)}, u32[]{:S(2)}) %collective-permute-start.5) | collective-permute-done | bytes 65568 | tf_op jit(solution)/shard_map/ppermute | solution.py:581
  20.3 0.6 collective-permute-done.4.from1
  21.1 3.2 %collective-permute-start.8 = (f32[128,128]{1,0:T(8,128)S(1)}, f32[128,128]{1,0:T(8,128)S(1)}, u32[]{:S(2)}, u32[]{:S(2)}) collective-permute-start(f32[128,128]{1,0:T(8,128)S(1)} %get-tuple-element.116), channel_id=1, source_target_pairs={{0,32},{8,40},{16,48},{24,56},{32,0},{40,8},{48,16},{56,24},{64,96... | collective-permute-start | bytes 196616 | tf_op jit(solution)/shard_map/ppermute | solution.py:581
  24.8 2.3 %local_part.1.loc = f32[8,512,128]{2,1,0:T(8,128)S(1)} custom-call(f32[8,8,128]{2,1,0:T(8,128)S(1)} %get-tuple-element.89.rates_ref, bf16[8,512,128]{2,1,0:T(8,128)(2,1)S(1)} %get-tuple-element.100.refs_0_.q_ref.b_ref.c_ref, bf16[8,512,128]{2,1,0:T(8,128)(2,1)S(1)} %get-tuple-element.118.k_ref.a_ref.k, bf16[8,512,128]{2,1,0:T(8,128)(2,1)S(1)} %get-tuple-element.119.v_ref.a_ref.v), custom_call_target="tpu_custom_call" | custom-call | flops 2000000000 | bytes 5242880 | tf_op jit(solution)/shard_map/local_part/pallas_call | solution.py:67
  27.6 5.3 %collective-permute-start.10 = (f32[4,128,128]{2,1,0:T(8,128)S(1)}, f32[4,128,128]{2,1,0:T(8,128)S(1)}, u32[]{:S(2)}, u32[]{:S(2)}) collective-permute-start(f32[4,128,128]{2,1,0:T(8,128)S(1)} %get-tuple-element.123), channel_id=1, source_target_pairs={{0,8},{8,0},{16,24},{24,16},{32,40},{40,32},{48,56},{56,48},{64,72... | collective-permute-start | bytes 786440 | tf_op jit(solution)/shard_map/ppermute | solution.py:581
  33.4 0.7 collective-permute-done.10.state_ref.other_ref
  34.7 14.9 %all_to_all.5.sums_ref = f32[8,8,128]{2,1,0:T(8,128)S(1)} all-to-all(f32[8,8,128]{2,1,0:T(8,128)S(1)} %get-tuple-element.132), channel_id=1, replica_groups=mesh['ctx'=32,'head'=8] {'head'}, dimensions={0} | all-to-all | bytes 65536 | tf_op jit(solution)/shard_map/all_to_all | solution.py:638
  50.2 1.8 %collective-permute-start.11 = (f32[4,128,128]{2,1,0:T(8,128)S(1)}, f32[4,128,128]{2,1,0:T(8,128)S(1)}, u32[]{:S(2)}, u32[]{:S(2)}) collective-permute-start(f32[4,128,128]{2,1,0:T(8,128)S(1)} %get-tuple-element.135), channel_id=1, source_target_pairs={{0,8},{8,0},{16,24},{24,16},{32,40},{40,32},{48,56},{56,48},{64,72... | collective-permute-start | bytes 786440 | tf_op jit(solution)/shard_map/ppermute | solution.py:581
  53.4 2.5 %collective-permute-start.13 = (f32[128,128]{1,0:T(8,128)S(1)}, f32[128,128]{1,0:T(8,128)S(1)}, u32[]{:S(2)}, u32[]{:S(2)}) collective-permute-start(f32[128,128]{1,0:T(8,128)S(1)} %get-tuple-element.144), channel_id=1, source_target_pairs={{0,32},{8,40},{16,48},{24,56},{32,0},{40,8},{48,16},{56,24},{64,96... | collective-permute-start | bytes 196616 | tf_op jit(solution)/shard_map/ppermute | solution.py:581
  55.9 0.8 collective-permute-start.14
  56.7 2.3 %gv_local.1.vl_ref = bf16[8,512,128]{2,1,0:T(8,128)(2,1)S(1)} custom-call(f32[8,8,128]{2,1,0:T(8,128)S(1)} %get-tuple-element.89.rates_ref, bf16[8,512,128]{2,1,0:T(8,128)(2,1)S(1)} %get-tuple-element.118.k_ref.a_ref.k, bf16[8,512,128]{2,1,0:T(8,128)(2,1)S(1)} %get-tuple-element.100.refs_0_.q_ref.b_ref.c_ref, ...), custom_call_target="tpu_custom_call" | custom-call | flops 2000000000 | bytes 5242880 | tf_op jit(solution)/shard_map/gv_local/pallas_call | solution.py:67
  59.0 0.7 collective-permute-done.14.from3
  60.1 0.9 %collective-permute-start.16 = (f32[128,128]{1,0:T(8,128)S(1)}, f32[128,128]{1,0:T(8,128)S(1)}, u32[]{:S(2)}, u32[]{:S(2)}) collective-permute-start(f32[128,128]{1,0:T(8,128)S(1)} %get-tuple-element.150.own_ref), channel_id=1, source_target_pairs={{0,128},{8,136},{16,144},{24,152},{32,160},{40,168},{48,176},{56,1... | collective-permute-start | bytes 196616 | tf_op jit(solution)/shard_map/ppermute | solution.py:581
  61.0 0.8 collective-permute-start.15
  61.8 2.3 %gk_local.1.kl_ref = bf16[8,512,128]{2,1,0:T(8,128)(2,1)S(1)} custom-call(f32[8,8,128]{2,1,0:T(8,128)S(1)} %get-tuple-element.89.rates_ref, bf16[8,512,128]{2,1,0:T(8,128)(2,1)S(1)} %get-tuple-element.119.v_ref.a_ref.v, bf16[8,512,128]{2,1,0:T(8,128)(2,1)S(1)} %get-tuple-element.151.c_ref.b_ref.g_ref, ...), custom_call_target="tpu_custom_call" | custom-call | flops 2000000000 | bytes 5242880 | tf_op jit(solution)/shard_map/gk_local/pallas_call | solution.py:67
  64.1 0.7 collective-permute-done.16.from2
  64.8 0.7 collective-permute-done.15.from1
  65.6 1.0 %collective-permute-start.18 = (f32[128,128]{1,0:T(8,128)S(1)}, f32[128,128]{1,0:T(8,128)S(1)}, u32[]{:S(2)}, u32[]{:S(2)}) collective-permute-start(f32[128,128]{1,0:T(8,128)S(1)} %get-tuple-element.156), channel_id=1, source_target_pairs={{0,16},{8,24},{16,32},{24,40},{32,48},{40,56},{48,0},{56,8},{64,80... | collective-permute-start | bytes 196616 | tf_op jit(solution)/shard_map/ppermute | solution.py:581
  66.6 2.6 %collective-permute-start.19 = (f32[128,128]{1,0:T(8,128)S(1)}, f32[128,128]{1,0:T(8,128)S(1)}, u32[]{:S(2)}, u32[]{:S(2)}) collective-permute-start(f32[128,128]{1,0:T(8,128)S(1)} %get-tuple-element.157), channel_id=1, source_target_pairs={{0,32},{8,40},{16,48},{24,56},{32,0},{40,8},{48,16},{56,24},{64,96... | collective-permute-start | bytes 196616 | tf_op jit(solution)/shard_map/ppermute | solution.py:581
  69.2 3.3 %grad_query.1 = bf16[512,8,128]{2,1,0:T(8,128)(2,1)} custom-call(f32[8,8,128]{2,1,0:T(8,128)S(1)} %get-tuple-element.89.rates_ref, bf16[8,512,128]{2,1,0:T(8,128)(2,1)S(1)} %get-tuple-element.151.c_ref.b_ref.g_ref, bf16[8,512,128]{2,1,0:T(8,128)(2,1)S(1)} %get-tuple-element.118.k_ref.a_ref.k, bf16[8,512,128]{2,1,0:T(8,128)(2,1)S(1)} %get-tuple-element.119.v_ref.a_ref.v, ...), custom_call_target="tpu_custom_call" | custom-call | flops 3000000000 | bytes 5242880 | tf_op jit(solution)/shard_map/grad_query/pallas_call | solution.py:67
  72.7 4.7 %collective-permute-start.21 = (f32[4,128,128]{2,1,0:T(8,128)S(1)}, f32[4,128,128]{2,1,0:T(8,128)S(1)}, u32[]{:S(2)}, u32[]{:S(2)}) collective-permute-start(f32[4,128,128]{2,1,0:T(8,128)S(1)} %get-tuple-element.166), channel_id=1, source_target_pairs={{0,8},{8,0},{16,24},{24,16},{32,40},{40,32},{48,56},{56,48},{64,72... | collective-permute-start | bytes 786440 | tf_op jit(solution)/shard_map/ppermute | solution.py:581
  77.4 0.7 own_finish.1
  78.5 1.8 %other_finish.1 = (bf16[512,8,128]{2,1,0:T(8,128)(2,1)}, bf16[512,8,128]{2,1,0:T(8,128)(2,1)}, f32[4096,128]{1,0:T(8,128)S(1)}, f32[4096,128]{1,0:T(8,128)S(1)}) custom-call(f32[8,8,128]{2,1,0:T(8,128)S(1)} %get-tuple-element.89.rates_ref, bf16[8,512,128]{2,1,0:T(8,128)(2,1)S(1)} %get-tuple-element.118.k_ref.a_ref.k, ...), custom_call_target="tpu_custom_call", output_to_operand_aliasing={{2}: (6, {}), {3}: (7, {})} | custom-call | tf_op jit(solution)/shard_map/other_finish/pallas_call | solution.py:67
  (37 shorter events, 7.9 us)
Async XLA Ops:
  2.7 4.5 %collective-permute-start = (f32[4,128,128]{2,1,0:T(8,128)S(1)}, f32[4,128,128]{2,1,0:T(8,128)S(1)}, u32[]{:S(2)}, u32[]{:S(2)}) collective-permute-start(f32[4,128,128]{2,1,0:T(8,128)S(1)} %get-tuple-element.90), channel_id=1, source_target_pairs={{0,8},{8,0},{16,24},{24,16},{32,40},{40,32},{48,56},{56,48},{64,72... | collective-permute-start | bytes 786440 | tf_op jit(solution)/shard_map/ppermute | solution.py:581
  7.3 5.2 %collective-permute-start.1 = (f32[128,128]{1,0:T(8,128)S(1)}, f32[128,128]{1,0:T(8,128)S(1)}, u32[]{:S(2)}, u32[]{:S(2)}) collective-permute-start(f32[128,128]{1,0:T(8,128)S(1)} %get-tuple-element.95), channel_id=1, source_target_pairs={{0,16},{8,24},{16,32},{24,40},{32,48},{40,56},{48,0},{56,8},{64,80... | collective-permute-start | bytes 196616 | tf_op jit(solution)/shard_map/ppermute | solution.py:581
  7.4 5.7 %collective-permute-start.2 = (f32[128,128]{1,0:T(8,128)S(1)}, f32[128,128]{1,0:T(8,128)S(1)}, u32[]{:S(2)}, u32[]{:S(2)}) collective-permute-start(f32[128,128]{1,0:T(8,128)S(1)} %get-tuple-element.96), channel_id=1, source_target_pairs={{0,32},{8,40},{16,48},{24,56},{32,0},{40,8},{48,16},{56,24},{64,96... | collective-permute-start | bytes 196616 | tf_op jit(solution)/shard_map/ppermute | solution.py:581
  9.3 4.2 %collective-permute-start.3 = (f32[128,128]{1,0:T(8,128)S(1)}, f32[128,128]{1,0:T(8,128)S(1)}, u32[]{:S(2)}, u32[]{:S(2)}) collective-permute-start(f32[128,128]{1,0:T(8,128)S(1)} %get-tuple-element.97), channel_id=1, source_target_pairs={{0,48},{8,56},{16,0},{24,8},{32,16},{40,24},{48,32},{56,40},{64,11... | collective-permute-start | bytes 196616 | tf_op jit(solution)/shard_map/ppermute | solution.py:581
  13.6 4.9 %collective-permute-start.6 = (f32[128,128]{1,0:T(8,128)S(1)}, f32[128,128]{1,0:T(8,128)S(1)}, u32[]{:S(2)}, u32[]{:S(2)}) collective-permute-start(f32[128,128]{1,0:T(8,128)S(1)} %get-tuple-element.105.own_ref), channel_id=1, source_target_pairs={{0,192},{8,200},{16,208},{24,216},{32,224},{40,232},{48,240},{56,2... | collective-permute-start | bytes 196616 | tf_op jit(solution)/shard_map/ppermute | solution.py:581
  15.6 4.7 %collective-permute-start.5 = (f32[128,128]{1,0:T(8,128)S(1)}, f32[128,128]{1,0:T(8,128)S(1)}, u32[]{:S(2)}, u32[]{:S(2)}) collective-permute-start(f32[128,128]{1,0:T(8,128)S(1)} %get-tuple-element.105.own_ref), channel_id=1, source_target_pairs={{0,128},{8,136},{16,144},{24,152},{32,160},{40,168},{48,176},{56,1... | collective-permute-start | bytes 196616 | tf_op jit(solution)/shard_map/ppermute | solution.py:581
  16.0 5.0 %collective-permute-start.4 = (f32[128,128]{1,0:T(8,128)S(1)}, f32[128,128]{1,0:T(8,128)S(1)}, u32[]{:S(2)}, u32[]{:S(2)}) collective-permute-start(f32[128,128]{1,0:T(8,128)S(1)} %get-tuple-element.105.own_ref), channel_id=1, source_target_pairs={{0,64},{8,72},{16,80},{24,88},{32,96},{40,104},{48,112},{56,120},{... | collective-permute-start | bytes 196616 | tf_op jit(solution)/shard_map/ppermute | solution.py:581
  21.1 6.0 %collective-permute-start.7 = (f32[128,128]{1,0:T(8,128)S(1)}, f32[128,128]{1,0:T(8,128)S(1)}, u32[]{:S(2)}, u32[]{:S(2)}) collective-permute-start(f32[128,128]{1,0:T(8,128)S(1)} %get-tuple-element.115), channel_id=1, source_target_pairs={{0,16},{8,24},{16,32},{24,40},{32,48},{40,56},{48,0},{56,8},{64,80... | collective-permute-start | bytes 196616 | tf_op jit(solution)/shard_map/ppermute | solution.py:581
  21.1 6.0 %collective-permute-start.8 = (f32[128,128]{1,0:T(8,128)S(1)}, f32[128,128]{1,0:T(8,128)S(1)}, u32[]{:S(2)}, u32[]{:S(2)}) collective-permute-start(f32[128,128]{1,0:T(8,128)S(1)} %get-tuple-element.116), channel_id=1, source_target_pairs={{0,32},{8,40},{16,48},{24,56},{32,0},{40,8},{48,16},{56,24},{64,96... | collective-permute-start | bytes 196616 | tf_op jit(solution)/shard_map/ppermute | solution.py:581
  24.4 8.6 %copy-start = (f32[8,128]{1,0:T(8,128)S(1)}, f32[8,128]{1,0:T(8,128)}, u32[]{:S(2)}) copy-start(f32[8,128]{1,0:T(8,128)} %gain_ref.7) | copy-start | bytes 12292
  24.4 3.1 %collective-permute-start.9 = (f32[128,128]{1,0:T(8,128)S(1)}, f32[128,128]{1,0:T(8,128)S(1)}, u32[]{:S(2)}, u32[]{:S(2)}) collective-permute-start(f32[128,128]{1,0:T(8,128)S(1)} %get-tuple-element.117), channel_id=1, source_target_pairs={{0,48},{8,56},{16,0},{24,8},{32,16},{40,24},{48,32},{56,40},{64,11... | collective-permute-start | bytes 196616 | tf_op jit(solution)/shard_map/ppermute | solution.py:581
  27.6 6.5 %collective-permute-start.10 = (f32[4,128,128]{2,1,0:T(8,128)S(1)}, f32[4,128,128]{2,1,0:T(8,128)S(1)}, u32[]{:S(2)}, u32[]{:S(2)}) collective-permute-start(f32[4,128,128]{2,1,0:T(8,128)S(1)} %get-tuple-element.123), channel_id=1, source_target_pairs={{0,8},{8,0},{16,24},{24,16},{32,40},{40,32},{48,56},{56,48},{64,72... | collective-permute-start | bytes 786440 | tf_op jit(solution)/shard_map/ppermute | solution.py:581
  50.2 3.0 %collective-permute-start.11 = (f32[4,128,128]{2,1,0:T(8,128)S(1)}, f32[4,128,128]{2,1,0:T(8,128)S(1)}, u32[]{:S(2)}, u32[]{:S(2)}) collective-permute-start(f32[4,128,128]{2,1,0:T(8,128)S(1)} %get-tuple-element.135), channel_id=1, source_target_pairs={{0,8},{8,0},{16,24},{24,16},{32,40},{40,32},{48,56},{56,48},{64,72... | collective-permute-start | bytes 786440 | tf_op jit(solution)/shard_map/ppermute | solution.py:581
  53.3 5.7 %collective-permute-start.12 = (f32[128,128]{1,0:T(8,128)S(1)}, f32[128,128]{1,0:T(8,128)S(1)}, u32[]{:S(2)}, u32[]{:S(2)}) collective-permute-start(f32[128,128]{1,0:T(8,128)S(1)} %get-tuple-element.143), channel_id=1, source_target_pairs={{0,16},{8,24},{16,32},{24,40},{32,48},{40,56},{48,0},{56,8},{64,80... | collective-permute-start | bytes 196616 | tf_op jit(solution)/shard_map/ppermute | solution.py:581
  53.4 5.6 %collective-permute-start.13 = (f32[128,128]{1,0:T(8,128)S(1)}, f32[128,128]{1,0:T(8,128)S(1)}, u32[]{:S(2)}, u32[]{:S(2)}) collective-permute-start(f32[128,128]{1,0:T(8,128)S(1)} %get-tuple-element.144), channel_id=1, source_target_pairs={{0,32},{8,40},{16,48},{24,56},{32,0},{40,8},{48,16},{56,24},{64,96... | collective-permute-start | bytes 196616 | tf_op jit(solution)/shard_map/ppermute | solution.py:581
  55.9 3.8 %collective-permute-start.14 = (f32[128,128]{1,0:T(8,128)S(1)}, f32[128,128]{1,0:T(8,128)S(1)}, u32[]{:S(2)}, u32[]{:S(2)}) collective-permute-start(f32[128,128]{1,0:T(8,128)S(1)} %get-tuple-element.145), channel_id=1, source_target_pairs={{0,48},{8,56},{16,0},{24,8},{32,16},{40,24},{48,32},{56,40},{64,11... | collective-permute-start | bytes 196616 | tf_op jit(solution)/shard_map/ppermute | solution.py:581
  59.8 4.3 %collective-permute-start.17 = (f32[128,128]{1,0:T(8,128)S(1)}, f32[128,128]{1,0:T(8,128)S(1)}, u32[]{:S(2)}, u32[]{:S(2)}) collective-permute-start(f32[128,128]{1,0:T(8,128)S(1)} %get-tuple-element.150.own_ref), channel_id=1, source_target_pairs={{0,192},{8,200},{16,208},{24,216},{32,224},{40,232},{48,240},{56,2... | collective-permute-start | bytes 196616 | tf_op jit(solution)/shard_map/ppermute | solution.py:581
  60.1 4.6 %collective-permute-start.16 = (f32[128,128]{1,0:T(8,128)S(1)}, f32[128,128]{1,0:T(8,128)S(1)}, u32[]{:S(2)}, u32[]{:S(2)}) collective-permute-start(f32[128,128]{1,0:T(8,128)S(1)} %get-tuple-element.150.own_ref), channel_id=1, source_target_pairs={{0,128},{8,136},{16,144},{24,152},{32,160},{40,168},{48,176},{56,1... | collective-permute-start | bytes 196616 | tf_op jit(solution)/shard_map/ppermute | solution.py:581
  61.0 4.5 %collective-permute-start.15 = (f32[128,128]{1,0:T(8,128)S(1)}, f32[128,128]{1,0:T(8,128)S(1)}, u32[]{:S(2)}, u32[]{:S(2)}) collective-permute-start(f32[128,128]{1,0:T(8,128)S(1)} %get-tuple-element.150.own_ref), channel_id=1, source_target_pairs={{0,64},{8,72},{16,80},{24,88},{32,96},{40,104},{48,112},{56,120},{... | collective-permute-start | bytes 196616 | tf_op jit(solution)/shard_map/ppermute | solution.py:581
  65.6 6.9 %collective-permute-start.18 = (f32[128,128]{1,0:T(8,128)S(1)}, f32[128,128]{1,0:T(8,128)S(1)}, u32[]{:S(2)}, u32[]{:S(2)}) collective-permute-start(f32[128,128]{1,0:T(8,128)S(1)} %get-tuple-element.156), channel_id=1, source_target_pairs={{0,16},{8,24},{16,32},{24,40},{32,48},{40,56},{48,0},{56,8},{64,80... | collective-permute-start | bytes 196616 | tf_op jit(solution)/shard_map/ppermute | solution.py:581
  66.6 5.9 %collective-permute-start.19 = (f32[128,128]{1,0:T(8,128)S(1)}, f32[128,128]{1,0:T(8,128)S(1)}, u32[]{:S(2)}, u32[]{:S(2)}) collective-permute-start(f32[128,128]{1,0:T(8,128)S(1)} %get-tuple-element.157), channel_id=1, source_target_pairs={{0,32},{8,40},{16,48},{24,56},{32,0},{40,8},{48,16},{56,24},{64,96... | collective-permute-start | bytes 196616 | tf_op jit(solution)/shard_map/ppermute | solution.py:581
  69.2 3.3 %collective-permute-start.20 = (f32[128,128]{1,0:T(8,128)S(1)}, f32[128,128]{1,0:T(8,128)S(1)}, u32[]{:S(2)}, u32[]{:S(2)}) collective-permute-start(f32[128,128]{1,0:T(8,128)S(1)} %get-tuple-element.158), channel_id=1, source_target_pairs={{0,48},{8,56},{16,0},{24,8},{32,16},{40,24},{48,32},{56,40},{64,11... | collective-permute-start | bytes 196616 | tf_op jit(solution)/shard_map/ppermute | solution.py:581
  72.7 5.9 %collective-permute-start.21 = (f32[4,128,128]{2,1,0:T(8,128)S(1)}, f32[4,128,128]{2,1,0:T(8,128)S(1)}, u32[]{:S(2)}, u32[]{:S(2)}) collective-permute-start(f32[4,128,128]{2,1,0:T(8,128)S(1)} %get-tuple-element.166), channel_id=1, source_target_pairs={{0,8},{8,0},{16,24},{24,16},{32,40},{40,32},{48,56},{56,48},{64,72... | collective-permute-start | bytes 786440 | tf_op jit(solution)/shard_map/ppermute | solution.py:581

commit v8 on v7

--- a/solution.py
+++ b/solution.py
@@ -536,11 +536,12 @@
     def form(core):
         writes = []
         halves = half_finish(rates_ref, k, v, kl_ref, vl_ref, state_ref, (1 - core) * HALF, wk, wv)
-        for n, _ in enumerate(halves):
-            wide, out, to = sides[n]
-            for p in range(PARTS):
-                rows = pl.ds(p * CHUNK, CHUNK)
-                flat = pl.ds(p * CHUNK * HEADS, CHUNK * HEADS)
+        for _ in halves:
+            pass
+        for p in range(PARTS):
+            rows = pl.ds(p * CHUNK, CHUNK)
+            flat = pl.ds(p * CHUNK * HEADS, CHUNK * HEADS)
+            for n, (wide, out, to) in enumerate(sides):
                 out[rows] = wide[flat, :].reshape(CHUNK, HEADS, SIZE).astype(BF16)
                 writes.append(put(out, to, rows, sems.at[PARTS * n + p]))
         wait_all(writes)

time: 80.7 us -> 80.9 us (level)
  no operation moved by 1% of the time
where the time goes in v8:
time: 80.9 us; the launch traced here: 80.8 us
  starting transfers between devices  34 us (42%)
  Pallas kernels  22.1 us (27%)
  blocking collectives  14.9 us (18%)
  waiting for transfers between devices  8.66 us (11%)
  between operations  1.06 us (1%)
    ppermute x22, starting transfers between devices, permute(): return lax.ppermute(a, 'ctx', pairs)  34 us
    pallas_call x22, Pallas kernels, call(): pl.pallas_call(body, in_specs=in_specs, out_specs=out_specs, out_shape=ou...  22.1 us
    all_to_all x1, blocking collectives, on_device(): sums = lax.all_to_all(sums, 'head', 0, 0, tiled=True)  14.9 us
    ppermute x22, waiting for transfers between devices, permute(): return lax.ppermute(a, 'ctx', pairs)  8.66 us
  transfers between devices with their start and end apart: 22, of which 13 were waited for; matrix products, arithmetic and copies ran while one was open for 0% of the time, Pallas kernels for 20%

profile of v8, /device:TPU:1, one launch (start us, length us, event | category | flops | bytes accessed | tf_op | source)
XLA Modules:
  0.0 80.8 jit_solution(16635482359041448257)
XLA Ops:
  0.6 2.1 %send_states.1 = (f32[4,128,128]{2,1,0:T(8,128)S(1)}, f32[4096,128]{1,0:T(8,128)S(1)}, f32[4096,128]{1,0:T(8,128)S(1)}, f32[8,8,128]{2,1,0:T(8,128)S(1)}) custom-call(s32[8]{0:T(128)} %slope_hbm.1, bf16[512,8,128]{2,1,0:T(8,128)(2,1)} %k_hbm.1, bf16[512,8,128]{2,1,0:T(8,128)(2,1)} %v_hbm.1), custom_call_target="tpu_custom_call" | custom-call | tf_op jit(solution)/shard_map/send_states/pallas_call | solution.py:67
  2.7 3.3 %collective-permute-start = (f32[4,128,128]{2,1,0:T(8,128)S(1)}, f32[4,128,128]{2,1,0:T(8,128)S(1)}, u32[]{:S(2)}, u32[]{:S(2)}) collective-permute-start(f32[4,128,128]{2,1,0:T(8,128)S(1)} %get-tuple-element.90), channel_id=1, source_target_pairs={{0,8},{8,0},{16,24},{24,16},{32,40},{40,32},{48,56},{56,48},{64,72... | collective-permute-start | bytes 786440 | tf_op jit(solution)/shard_map/ppermute | solution.py:582
  6.0 0.7 keep_states.1.keep_ref
  7.4 1.9 %collective-permute-start.2 = (f32[128,128]{1,0:T(8,128)S(1)}, f32[128,128]{1,0:T(8,128)S(1)}, u32[]{:S(2)}, u32[]{:S(2)}) collective-permute-start(f32[128,128]{1,0:T(8,128)S(1)} %get-tuple-element.96), channel_id=1, source_target_pairs={{0,32},{8,40},{16,48},{24,56},{32,0},{40,8},{48,16},{56,24},{64,96... | collective-permute-start | bytes 196616 | tf_op jit(solution)/shard_map/ppermute | solution.py:582
  9.3 1.2 %collective-permute-start.3 = (f32[128,128]{1,0:T(8,128)S(1)}, f32[128,128]{1,0:T(8,128)S(1)}, u32[]{:S(2)}, u32[]{:S(2)}) collective-permute-start(f32[128,128]{1,0:T(8,128)S(1)} %get-tuple-element.97), channel_id=1, source_target_pairs={{0,48},{8,56},{16,0},{24,8},{32,16},{40,24},{48,32},{56,40},{64,11... | collective-permute-start | bytes 196616 | tf_op jit(solution)/shard_map/ppermute | solution.py:582
  10.4 1.4 %turn.2 = (bf16[8,512,128]{2,1,0:T(8,128)(2,1)S(1)}, bf16[8,512,128]{2,1,0:T(8,128)(2,1)S(1)}) custom-call(f32[8,8,128]{2,1,0:T(8,128)S(1)} %get-tuple-element.89.rates_ref, f32[4096,128]{1,0:T(8,128)S(1)} %get-tuple-element.91.kw.a_wide, bf16[512,8,128]{2,1,0:T(8,128)(2,1)} %b_hbm.2), custom_call_target="tpu_custom_call" | custom-call | bytes 8388608 | tf_op jit(solution)/shard_map/turn/pallas_call | solution.py:67
  13.6 2.0 %collective-permute-start.6 = (f32[128,128]{1,0:T(8,128)S(1)}, f32[128,128]{1,0:T(8,128)S(1)}, u32[]{:S(2)}, u32[]{:S(2)}) collective-permute-start(f32[128,128]{1,0:T(8,128)S(1)} %get-tuple-element.105.own_ref), channel_id=1, source_target_pairs={{0,192},{8,200},{16,208},{24,216},{32,224},{40,232},{48,240},{56,2... | collective-permute-start | bytes 196616 | tf_op jit(solution)/shard_map/ppermute | solution.py:582
  16.0 0.7 collective-permute-start.4
  16.6 1.8 %turn.3 = (bf16[8,512,128]{2,1,0:T(8,128)(2,1)S(1)}, bf16[8,512,128]{2,1,0:T(8,128)(2,1)S(1)}, bf16[8,128,512]{2,1,0:T(8,128)(2,1)S(1)}) custom-call(f32[8,8,128]{2,1,0:T(8,128)S(1)} %get-tuple-element.89.rates_ref, f32[4096,128]{1,0:T(8,128)S(1)} %get-tuple-element.92.vw.a_wide, bf16[512,8,128]{2,1,0:T(8,128)(2,1)} %b_hbm.3, ...), custom_call_target="tpu_custom_call" | custom-call | bytes 8388608 | tf_op jit(solution)/shard_map/turn/pallas_call | solution.py:67
  18.5 1.8 %collective-permute-done.5.from2 = f32[128,128]{1,0:T(8,128)S(1)} collective-permute-done((f32[128,128]{1,0:T(8,128)S(1)}, f32[128,128]{1,0:T(8,128)S(1)}, u32[]{:S(2)}, u32[]{:S(2)}) %collective-permute-start.5) | collective-permute-done | bytes 65568 | tf_op jit(solution)/shard_map/ppermute | solution.py:582
  20.3 0.6 collective-permute-done.4.from1
  21.1 3.2 %collective-permute-start.8 = (f32[128,128]{1,0:T(8,128)S(1)}, f32[128,128]{1,0:T(8,128)S(1)}, u32[]{:S(2)}, u32[]{:S(2)}) collective-permute-start(f32[128,128]{1,0:T(8,128)S(1)} %get-tuple-element.116), channel_id=1, source_target_pairs={{0,32},{8,40},{16,48},{24,56},{32,0},{40,8},{48,16},{56,24},{64,96... | collective-permute-start | bytes 196616 | tf_op jit(solution)/shard_map/ppermute | solution.py:582
  24.8 2.3 %local_part.1.loc = f32[8,512,128]{2,1,0:T(8,128)S(1)} custom-call(f32[8,8,128]{2,1,0:T(8,128)S(1)} %get-tuple-element.89.rates_ref, bf16[8,512,128]{2,1,0:T(8,128)(2,1)S(1)} %get-tuple-element.100.refs_0_.q_ref.b_ref.c_ref, bf16[8,512,128]{2,1,0:T(8,128)(2,1)S(1)} %get-tuple-element.118.k_ref.a_ref.k, bf16[8,512,128]{2,1,0:T(8,128)(2,1)S(1)} %get-tuple-element.119.v_ref.a_ref.v), custom_call_target="tpu_custom_call" | custom-call | flops 2000000000 | bytes 5242880 | tf_op jit(solution)/shard_map/local_part/pallas_call | solution.py:67
  27.6 5.3 %collective-permute-start.10 = (f32[4,128,128]{2,1,0:T(8,128)S(1)}, f32[4,128,128]{2,1,0:T(8,128)S(1)}, u32[]{:S(2)}, u32[]{:S(2)}) collective-permute-start(f32[4,128,128]{2,1,0:T(8,128)S(1)} %get-tuple-element.123), channel_id=1, source_target_pairs={{0,8},{8,0},{16,24},{24,16},{32,40},{40,32},{48,56},{56,48},{64,72... | collective-permute-start | bytes 786440 | tf_op jit(solution)/shard_map/ppermute | solution.py:582
  33.4 0.7 collective-permute-done.10.state_ref.other_ref
  34.7 14.9 %all_to_all.5.sums_ref = f32[8,8,128]{2,1,0:T(8,128)S(1)} all-to-all(f32[8,8,128]{2,1,0:T(8,128)S(1)} %get-tuple-element.132), channel_id=1, replica_groups=mesh['ctx'=32,'head'=8] {'head'}, dimensions={0} | all-to-all | bytes 65536 | tf_op jit(solution)/shard_map/all_to_all | solution.py:639
  50.2 1.8 %collective-permute-start.11 = (f32[4,128,128]{2,1,0:T(8,128)S(1)}, f32[4,128,128]{2,1,0:T(8,128)S(1)}, u32[]{:S(2)}, u32[]{:S(2)}) collective-permute-start(f32[4,128,128]{2,1,0:T(8,128)S(1)} %get-tuple-element.135), channel_id=1, source_target_pairs={{0,8},{8,0},{16,24},{24,16},{32,40},{40,32},{48,56},{56,48},{64,72... | collective-permute-start | bytes 786440 | tf_op jit(solution)/shard_map/ppermute | solution.py:582
  53.4 2.5 %collective-permute-start.13 = (f32[128,128]{1,0:T(8,128)S(1)}, f32[128,128]{1,0:T(8,128)S(1)}, u32[]{:S(2)}, u32[]{:S(2)}) collective-permute-start(f32[128,128]{1,0:T(8,128)S(1)} %get-tuple-element.144), channel_id=1, source_target_pairs={{0,32},{8,40},{16,48},{24,56},{32,0},{40,8},{48,16},{56,24},{64,96... | collective-permute-start | bytes 196616 | tf_op jit(solution)/shard_map/ppermute | solution.py:582
  55.9 0.8 collective-permute-start.14
  56.7 2.3 %gv_local.1.vl_ref = bf16[8,512,128]{2,1,0:T(8,128)(2,1)S(1)} custom-call(f32[8,8,128]{2,1,0:T(8,128)S(1)} %get-tuple-element.89.rates_ref, bf16[8,512,128]{2,1,0:T(8,128)(2,1)S(1)} %get-tuple-element.118.k_ref.a_ref.k, bf16[8,512,128]{2,1,0:T(8,128)(2,1)S(1)} %get-tuple-element.100.refs_0_.q_ref.b_ref.c_ref, ...), custom_call_target="tpu_custom_call" | custom-call | flops 2000000000 | bytes 5242880 | tf_op jit(solution)/shard_map/gv_local/pallas_call | solution.py:67
  59.0 0.7 collective-permute-done.14.from3
  60.1 0.9 %collective-permute-start.16 = (f32[128,128]{1,0:T(8,128)S(1)}, f32[128,128]{1,0:T(8,128)S(1)}, u32[]{:S(2)}, u32[]{:S(2)}) collective-permute-start(f32[128,128]{1,0:T(8,128)S(1)} %get-tuple-element.150.own_ref), channel_id=1, source_target_pairs={{0,128},{8,136},{16,144},{24,152},{32,160},{40,168},{48,176},{56,1... | collective-permute-start | bytes 196616 | tf_op jit(solution)/shard_map/ppermute | solution.py:582
  61.0 0.8 collective-permute-start.15
  61.8 2.3 %gk_local.1.kl_ref = bf16[8,512,128]{2,1,0:T(8,128)(2,1)S(1)} custom-call(f32[8,8,128]{2,1,0:T(8,128)S(1)} %get-tuple-element.89.rates_ref, bf16[8,512,128]{2,1,0:T(8,128)(2,1)S(1)} %get-tuple-element.119.v_ref.a_ref.v, bf16[8,512,128]{2,1,0:T(8,128)(2,1)S(1)} %get-tuple-element.151.c_ref.b_ref.g_ref, ...), custom_call_target="tpu_custom_call" | custom-call | flops 2000000000 | bytes 5242880 | tf_op jit(solution)/shard_map/gk_local/pallas_call | solution.py:67
  64.1 0.7 collective-permute-done.16.from2
  64.8 0.7 collective-permute-done.15.from1
  65.6 1.0 %collective-permute-start.18 = (f32[128,128]{1,0:T(8,128)S(1)}, f32[128,128]{1,0:T(8,128)S(1)}, u32[]{:S(2)}, u32[]{:S(2)}) collective-permute-start(f32[128,128]{1,0:T(8,128)S(1)} %get-tuple-element.156), channel_id=1, source_target_pairs={{0,16},{8,24},{16,32},{24,40},{32,48},{40,56},{48,0},{56,8},{64,80... | collective-permute-start | bytes 196616 | tf_op jit(solution)/shard_map/ppermute | solution.py:582
  66.6 2.6 %collective-permute-start.19 = (f32[128,128]{1,0:T(8,128)S(1)}, f32[128,128]{1,0:T(8,128)S(1)}, u32[]{:S(2)}, u32[]{:S(2)}) collective-permute-start(f32[128,128]{1,0:T(8,128)S(1)} %get-tuple-element.157), channel_id=1, source_target_pairs={{0,32},{8,40},{16,48},{24,56},{32,0},{40,8},{48,16},{56,24},{64,96... | collective-permute-start | bytes 196616 | tf_op jit(solution)/shard_map/ppermute | solution.py:582
  69.2 3.3 %grad_query.1 = bf16[512,8,128]{2,1,0:T(8,128)(2,1)} custom-call(f32[8,8,128]{2,1,0:T(8,128)S(1)} %get-tuple-element.89.rates_ref, bf16[8,512,128]{2,1,0:T(8,128)(2,1)S(1)} %get-tuple-element.151.c_ref.b_ref.g_ref, bf16[8,512,128]{2,1,0:T(8,128)(2,1)S(1)} %get-tuple-element.118.k_ref.a_ref.k, bf16[8,512,128]{2,1,0:T(8,128)(2,1)S(1)} %get-tuple-element.119.v_ref.a_ref.v, ...), custom_call_target="tpu_custom_call" | custom-call | flops 3000000000 | bytes 5242880 | tf_op jit(solution)/shard_map/grad_query/pallas_call | solution.py:67
  72.7 4.7 %collective-permute-start.21 = (f32[4,128,128]{2,1,0:T(8,128)S(1)}, f32[4,128,128]{2,1,0:T(8,128)S(1)}, u32[]{:S(2)}, u32[]{:S(2)}) collective-permute-start(f32[4,128,128]{2,1,0:T(8,128)S(1)} %get-tuple-element.166), channel_id=1, source_target_pairs={{0,8},{8,0},{16,24},{24,16},{32,40},{40,32},{48,56},{56,48},{64,72... | collective-permute-start | bytes 786440 | tf_op jit(solution)/shard_map/ppermute | solution.py:582
  77.4 0.7 own_finish.1
  78.5 2.0 %other_finish.1 = (bf16[512,8,128]{2,1,0:T(8,128)(2,1)}, bf16[512,8,128]{2,1,0:T(8,128)(2,1)}, f32[4096,128]{1,0:T(8,128)S(1)}, f32[4096,128]{1,0:T(8,128)S(1)}) custom-call(f32[8,8,128]{2,1,0:T(8,128)S(1)} %get-tuple-element.89.rates_ref, bf16[8,512,128]{2,1,0:T(8,128)(2,1)S(1)} %get-tuple-element.118.k_ref.a_ref.k, ...), custom_call_target="tpu_custom_call", output_to_operand_aliasing={{2}: (6, {}), {3}: (7, {})} | custom-call | tf_op jit(solution)/shard_map/other_finish/pallas_call | solution.py:67
  (37 shorter events, 7.9 us)
Async XLA Ops:
  2.7 4.5 %collective-permute-start = (f32[4,128,128]{2,1,0:T(8,128)S(1)}, f32[4,128,128]{2,1,0:T(8,128)S(1)}, u32[]{:S(2)}, u32[]{:S(2)}) collective-permute-start(f32[4,128,128]{2,1,0:T(8,128)S(1)} %get-tuple-element.90), channel_id=1, source_target_pairs={{0,8},{8,0},{16,24},{24,16},{32,40},{40,32},{48,56},{56,48},{64,72... | collective-permute-start | bytes 786440 | tf_op jit(solution)/shard_map/ppermute | solution.py:582
  7.3 5.2 %collective-permute-start.1 = (f32[128,128]{1,0:T(8,128)S(1)}, f32[128,128]{1,0:T(8,128)S(1)}, u32[]{:S(2)}, u32[]{:S(2)}) collective-permute-start(f32[128,128]{1,0:T(8,128)S(1)} %get-tuple-element.95), channel_id=1, source_target_pairs={{0,16},{8,24},{16,32},{24,40},{32,48},{40,56},{48,0},{56,8},{64,80... | collective-permute-start | bytes 196616 | tf_op jit(solution)/shard_map/ppermute | solution.py:582
  7.4 5.7 %collective-permute-start.2 = (f32[128,128]{1,0:T(8,128)S(1)}, f32[128,128]{1,0:T(8,128)S(1)}, u32[]{:S(2)}, u32[]{:S(2)}) collective-permute-start(f32[128,128]{1,0:T(8,128)S(1)} %get-tuple-element.96), channel_id=1, source_target_pairs={{0,32},{8,40},{16,48},{24,56},{32,0},{40,8},{48,16},{56,24},{64,96... | collective-permute-start | bytes 196616 | tf_op jit(solution)/shard_map/ppermute | solution.py:582
  9.3 4.2 %collective-permute-start.3 = (f32[128,128]{1,0:T(8,128)S(1)}, f32[128,128]{1,0:T(8,128)S(1)}, u32[]{:S(2)}, u32[]{:S(2)}) collective-permute-start(f32[128,128]{1,0:T(8,128)S(1)} %get-tuple-element.97), channel_id=1, source_target_pairs={{0,48},{8,56},{16,0},{24,8},{32,16},{40,24},{48,32},{56,40},{64,11... | collective-permute-start | bytes 196616 | tf_op jit(solution)/shard_map/ppermute | solution.py:582
  13.6 4.9 %collective-permute-start.6 = (f32[128,128]{1,0:T(8,128)S(1)}, f32[128,128]{1,0:T(8,128)S(1)}, u32[]{:S(2)}, u32[]{:S(2)}) collective-permute-start(f32[128,128]{1,0:T(8,128)S(1)} %get-tuple-element.105.own_ref), channel_id=1, source_target_pairs={{0,192},{8,200},{16,208},{24,216},{32,224},{40,232},{48,240},{56,2... | collective-permute-start | bytes 196616 | tf_op jit(solution)/shard_map/ppermute | solution.py:582
  15.6 4.7 %collective-permute-start.5 = (f32[128,128]{1,0:T(8,128)S(1)}, f32[128,128]{1,0:T(8,128)S(1)}, u32[]{:S(2)}, u32[]{:S(2)}) collective-permute-start(f32[128,128]{1,0:T(8,128)S(1)} %get-tuple-element.105.own_ref), channel_id=1, source_target_pairs={{0,128},{8,136},{16,144},{24,152},{32,160},{40,168},{48,176},{56,1... | collective-permute-start | bytes 196616 | tf_op jit(solution)/shard_map/ppermute | solution.py:582
  16.0 5.0 %collective-permute-start.4 = (f32[128,128]{1,0:T(8,128)S(1)}, f32[128,128]{1,0:T(8,128)S(1)}, u32[]{:S(2)}, u32[]{:S(2)}) collective-permute-start(f32[128,128]{1,0:T(8,128)S(1)} %get-tuple-element.105.own_ref), channel_id=1, source_target_pairs={{0,64},{8,72},{16,80},{24,88},{32,96},{40,104},{48,112},{56,120},{... | collective-permute-start | bytes 196616 | tf_op jit(solution)/shard_map/ppermute | solution.py:582
  21.1 6.0 %collective-permute-start.7 = (f32[128,128]{1,0:T(8,128)S(1)}, f32[128,128]{1,0:T(8,128)S(1)}, u32[]{:S(2)}, u32[]{:S(2)}) collective-permute-start(f32[128,128]{1,0:T(8,128)S(1)} %get-tuple-element.115), channel_id=1, source_target_pairs={{0,16},{8,24},{16,32},{24,40},{32,48},{40,56},{48,0},{56,8},{64,80... | collective-permute-start | bytes 196616 | tf_op jit(solution)/shard_map/ppermute | solution.py:582
  21.1 6.0 %collective-permute-start.8 = (f32[128,128]{1,0:T(8,128)S(1)}, f32[128,128]{1,0:T(8,128)S(1)}, u32[]{:S(2)}, u32[]{:S(2)}) collective-permute-start(f32[128,128]{1,0:T(8,128)S(1)} %get-tuple-element.116), channel_id=1, source_target_pairs={{0,32},{8,40},{16,48},{24,56},{32,0},{40,8},{48,16},{56,24},{64,96... | collective-permute-start | bytes 196616 | tf_op jit(solution)/shard_map/ppermute | solution.py:582
  24.4 8.6 %copy-start = (f32[8,128]{1,0:T(8,128)S(1)}, f32[8,128]{1,0:T(8,128)}, u32[]{:S(2)}) copy-start(f32[8,128]{1,0:T(8,128)} %gain_ref.7) | copy-start | bytes 12292
  24.4 3.1 %collective-permute-start.9 = (f32[128,128]{1,0:T(8,128)S(1)}, f32[128,128]{1,0:T(8,128)S(1)}, u32[]{:S(2)}, u32[]{:S(2)}) collective-permute-start(f32[128,128]{1,0:T(8,128)S(1)} %get-tuple-element.117), channel_id=1, source_target_pairs={{0,48},{8,56},{16,0},{24,8},{32,16},{40,24},{48,32},{56,40},{64,11... | collective-permute-start | bytes 196616 | tf_op jit(solution)/shard_map/ppermute | solution.py:582
  27.6 6.5 %collective-permute-start.10 = (f32[4,128,128]{2,1,0:T(8,128)S(1)}, f32[4,128,128]{2,1,0:T(8,128)S(1)}, u32[]{:S(2)}, u32[]{:S(2)}) collective-permute-start(f32[4,128,128]{2,1,0:T(8,128)S(1)} %get-tuple-element.123), channel_id=1, source_target_pairs={{0,8},{8,0},{16,24},{24,16},{32,40},{40,32},{48,56},{56,48},{64,72... | collective-permute-start | bytes 786440 | tf_op jit(solution)/shard_map/ppermute | solution.py:582
  50.2 3.0 %collective-permute-start.11 = (f32[4,128,128]{2,1,0:T(8,128)S(1)}, f32[4,128,128]{2,1,0:T(8,128)S(1)}, u32[]{:S(2)}, u32[]{:S(2)}) collective-permute-start(f32[4,128,128]{2,1,0:T(8,128)S(1)} %get-tuple-element.135), channel_id=1, source_target_pairs={{0,8},{8,0},{16,24},{24,16},{32,40},{40,32},{48,56},{56,48},{64,72... | collective-permute-start | bytes 786440 | tf_op jit(solution)/shard_map/ppermute | solution.py:582
  53.3 5.7 %collective-permute-start.12 = (f32[128,128]{1,0:T(8,128)S(1)}, f32[128,128]{1,0:T(8,128)S(1)}, u32[]{:S(2)}, u32[]{:S(2)}) collective-permute-start(f32[128,128]{1,0:T(8,128)S(1)} %get-tuple-element.143), channel_id=1, source_target_pairs={{0,16},{8,24},{16,32},{24,40},{32,48},{40,56},{48,0},{56,8},{64,80... | collective-permute-start | bytes 196616 | tf_op jit(solution)/shard_map/ppermute | solution.py:582
  53.4 5.6 %collective-permute-start.13 = (f32[128,128]{1,0:T(8,128)S(1)}, f32[128,128]{1,0:T(8,128)S(1)}, u32[]{:S(2)}, u32[]{:S(2)}) collective-permute-start(f32[128,128]{1,0:T(8,128)S(1)} %get-tuple-element.144), channel_id=1, source_target_pairs={{0,32},{8,40},{16,48},{24,56},{32,0},{40,8},{48,16},{56,24},{64,96... | collective-permute-start | bytes 196616 | tf_op jit(solution)/shard_map/ppermute | solution.py:582
  55.9 3.8 %collective-permute-start.14 = (f32[128,128]{1,0:T(8,128)S(1)}, f32[128,128]{1,0:T(8,128)S(1)}, u32[]{:S(2)}, u32[]{:S(2)}) collective-permute-start(f32[128,128]{1,0:T(8,128)S(1)} %get-tuple-element.145), channel_id=1, source_target_pairs={{0,48},{8,56},{16,0},{24,8},{32,16},{40,24},{48,32},{56,40},{64,11... | collective-permute-start | bytes 196616 | tf_op jit(solution)/shard_map/ppermute | solution.py:582
  59.8 4.3 %collective-permute-start.17 = (f32[128,128]{1,0:T(8,128)S(1)}, f32[128,128]{1,0:T(8,128)S(1)}, u32[]{:S(2)}, u32[]{:S(2)}) collective-permute-start(f32[128,128]{1,0:T(8,128)S(1)} %get-tuple-element.150.own_ref), channel_id=1, source_target_pairs={{0,192},{8,200},{16,208},{24,216},{32,224},{40,232},{48,240},{56,2... | collective-permute-start | bytes 196616 | tf_op jit(solution)/shard_map/ppermute | solution.py:582
  60.1 4.6 %collective-permute-start.16 = (f32[128,128]{1,0:T(8,128)S(1)}, f32[128,128]{1,0:T(8,128)S(1)}, u32[]{:S(2)}, u32[]{:S(2)}) collective-permute-start(f32[128,128]{1,0:T(8,128)S(1)} %get-tuple-element.150.own_ref), channel_id=1, source_target_pairs={{0,128},{8,136},{16,144},{24,152},{32,160},{40,168},{48,176},{56,1... | collective-permute-start | bytes 196616 | tf_op jit(solution)/shard_map/ppermute | solution.py:582
  61.0 4.5 %collective-permute-start.15 = (f32[128,128]{1,0:T(8,128)S(1)}, f32[128,128]{1,0:T(8,128)S(1)}, u32[]{:S(2)}, u32[]{:S(2)}) collective-permute-start(f32[128,128]{1,0:T(8,128)S(1)} %get-tuple-element.150.own_ref), channel_id=1, source_target_pairs={{0,64},{8,72},{16,80},{24,88},{32,96},{40,104},{48,112},{56,120},{... | collective-permute-start | bytes 196616 | tf_op jit(solution)/shard_map/ppermute | solution.py:582
  65.6 6.9 %collective-permute-start.18 = (f32[128,128]{1,0:T(8,128)S(1)}, f32[128,128]{1,0:T(8,128)S(1)}, u32[]{:S(2)}, u32[]{:S(2)}) collective-permute-start(f32[128,128]{1,0:T(8,128)S(1)} %get-tuple-element.156), channel_id=1, source_target_pairs={{0,16},{8,24},{16,32},{24,40},{32,48},{40,56},{48,0},{56,8},{64,80... | collective-permute-start | bytes 196616 | tf_op jit(solution)/shard_map/ppermute | solution.py:582
  66.6 5.9 %collective-permute-start.19 = (f32[128,128]{1,0:T(8,128)S(1)}, f32[128,128]{1,0:T(8,128)S(1)}, u32[]{:S(2)}, u32[]{:S(2)}) collective-permute-start(f32[128,128]{1,0:T(8,128)S(1)} %get-tuple-element.157), channel_id=1, source_target_pairs={{0,32},{8,40},{16,48},{24,56},{32,0},{40,8},{48,16},{56,24},{64,96... | collective-permute-start | bytes 196616 | tf_op jit(solution)/shard_map/ppermute | solution.py:582
  69.2 3.3 %collective-permute-start.20 = (f32[128,128]{1,0:T(8,128)S(1)}, f32[128,128]{1,0:T(8,128)S(1)}, u32[]{:S(2)}, u32[]{:S(2)}) collective-permute-start(f32[128,128]{1,0:T(8,128)S(1)} %get-tuple-element.158), channel_id=1, source_target_pairs={{0,48},{8,56},{16,0},{24,8},{32,16},{40,24},{48,32},{56,40},{64,11... | collective-permute-start | bytes 196616 | tf_op jit(solution)/shard_map/ppermute | solution.py:582
  72.7 5.9 %collective-permute-start.21 = (f32[4,128,128]{2,1,0:T(8,128)S(1)}, f32[4,128,128]{2,1,0:T(8,128)S(1)}, u32[]{:S(2)}, u32[]{:S(2)}) collective-permute-start(f32[4,128,128]{2,1,0:T(8,128)S(1)} %get-tuple-element.166), channel_id=1, source_target_pairs={{0,8},{8,0},{16,24},{24,16},{32,40},{40,32},{48,56},{56,48},{64,72... | collective-permute-start | bytes 786440 | tf_op jit(solution)/shard_map/ppermute | solution.py:582
